TPU v7x, 32 devices: a whole 2x2x4 slice. The times are simulated.
32 devices in a mesh: oct: 2 (over core), sub: 16 (over z, y, x).
Axes of the slice: x: 2, y: 2, z: 4, core: 2. Of those that a mesh axis runs over, the one named last changes fastest.
Arguments:
- coefficients: float32 [512, 4096], P(('oct', 'sub')), may hold values from -6 to 6
- potential: float32 [512, 4096], P(('oct', 'sub')), may hold values from 0.2 to 2
- to_values: float32 [16, 16], replicated, may hold values from -1.5 to 1.5
- x_kernels: bfloat16 [20, 48, 16], replicated, may hold values from -0.5 to 0.5
- yz_kernels: bfloat16 [256, 46080], replicated, may hold values from -0.046875 to 0.046875
- two_scale: float32 [2, 16, 16], replicated, may hold values from -1 to 1
- disp_ids: int32 [512, 16], P(('oct', 'sub')), may hold values from -1 to 26, as said below
- dest_box: int32 [512, 16], P(('oct', 'sub')), may hold values from -1 to 511, as said below
- parent_of: int32 [512], P(('oct', 'sub')), may hold values from 0 to 63, as said below
- child_octant: int32 [512], P(('oct', 'sub')), may hold values from 0 to 7
Outputs:
- next_field: float32 [512, 4096], P(('oct', 'sub'))
- parents: float32 [64, 4096], P(('oct', 'sub'))
Inputs may be any that keep to these rules, and one draw needn't show every extreme that they name: `disp_ids`: -1 marks an empty slot, exactly where dest_box is -1; in every row the live slots come first, 4 or more of them. `dest_box`: among the live slots of one aligned block of 16 rows, at most 8 name boxes of any one aligned block of 16 boxes; some box block receives exactly 8 from every row block. Every parent is named by exactly 8 boxes, whose child_octant values are 0 to 7; parent_of[b] // 32 == b // 256. Within one aligned block of 16 boxes, at most 1 box has its parent in any one aligned block of 2 parents, and some parent block is named by exactly 1 of them.
All inputs are finite; a program needn't handle non-finite values.
Results may differ from a plain program's by a relative error of at most 0.018.
Values may be sent and summed in bfloat16 or wider, within the bound.
No kernel may reach another device: no remote copies, remote signals or barrier semaphores. Data moves between devices by JAX's collectives and lax.ppermute only.
A program may use at most 192 MiB of HBM per device.

v0:
```python
import functools

import jax
import jax.numpy as jnp
from jax import lax
from jax.experimental import pallas as pl
from jax.experimental.pallas import tpu as pltpu
from jax.sharding import Mesh
from jax.sharding import PartitionSpec as P

ITERS = 2
BLOCK = 32
GROUP = 4
MIB = 1024 * 1024


def mm(left, right):
    return jnp.dot(left, right, precision=lax.Precision.HIGHEST, preferred_element_type=jnp.float32)


def rows_high(matrix):
    order_k, width = matrix.shape
    return jnp.broadcast_to(matrix[:, None, :], (order_k, order_k, width)).reshape(order_k * order_k, width)


def rows_low(matrix):
    order_k, width = matrix.shape
    return jnp.broadcast_to(matrix[None, :, :], (order_k, order_k, width)).reshape(order_k * order_k, width)


def spread_columns(matrix):
    order_k = matrix.shape[0]
    shape = (order_k, order_k * order_k)
    slot = lax.broadcasted_iota(jnp.int32, shape, 0)
    lane = lax.broadcasted_iota(jnp.int32, shape, 1)
    high = (lane // order_k == slot).astype(jnp.float32)
    low = (lane % order_k == slot).astype(jnp.float32)
    return mm(matrix, high), mm(matrix, low)


def masks(order_k):
    shape = (order_k * order_k, order_k * order_k)
    row = lax.broadcasted_iota(jnp.int32, shape, 0)
    lane = lax.broadcasted_iota(jnp.int32, shape, 1)
    return row // order_k, row % order_k, lane // order_k, lane % order_k


def first_kernel(coef_ref, pot_ref, to_ref, back_ref, out_ref):
    order_k = to_ref.shape[0]
    plane = order_k * order_k
    to_high, to_low = spread_columns(to_ref[...])
    back_high, back_low = spread_columns(back_ref[...])
    row_high, row_low, lane_high, lane_low = masks(order_k)
    value_pair = rows_high(back_high) * rows_low(back_low)
    back_pair = rows_high(to_high) * rows_low(to_low)
    value_x = jnp.where(row_low == lane_low, rows_high(to_high), 0.0)
    source_x = jnp.where(row_high == lane_low, rows_low(back_high), 0.0)

    def by_x(ref):
        return jnp.concatenate([ref[:, x * plane : (x + 1) * plane] for x in range(order_k)], axis=0)

    values = mm(value_x, mm(by_x(coef_ref), value_pair))
    product = values * (by_x(pot_ref) + 0.25 * values * values)
    source = mm(source_x, mm(product, back_pair))
    out_ref[...] = source.astype(jnp.bfloat16).reshape(out_ref.shape)


def tree_kernel(last, part_count, *refs):
    parts = refs[:part_count]
    two_ref, flip_ref = refs[part_count : part_count + 2]
    rest = refs[part_count + 2 :]
    order_k = two_ref.shape[1]
    plane = order_k * order_k
    gathered = parts[0][...].astype(jnp.float32)
    for part in parts[1:]:
        gathered = gathered + part[...].astype(jnp.float32)
    boxes = gathered.shape[0]
    parent_count = boxes // 8

    def stacked(quad):
        return jnp.concatenate(
            [gathered[8 * p + 4 * c + quad] for p in range(parent_count) for c in range(2)], axis=0
        )

    two = [spread_columns(two_ref[c]) for c in range(2)]
    flip = [spread_columns(flip_ref[c]) for c in range(2)]
    summed = None
    for quad in range(4):
        lift = rows_high(flip[quad // 2][0]) * rows_low(flip[quad % 2][1])
        inner = mm(stacked(quad), lift)
        summed = inner if summed is None else summed + inner
    own = []
    dropped_x = []
    for p in range(parent_count):
        total = None
        for c in range(2):
            start = (2 * p + c) * order_k
            part = mm(two_ref[c], summed[start : start + order_k])
            total = part if total is None else total + part
        own.append(total)
        dropped_x += [mm(flip_ref[c], total) for c in range(2)]
    dropped_x = jnp.concatenate(dropped_x, axis=0)
    dropped = []
    for quad in range(4):
        drop = rows_high(two[quad // 2][0]) * rows_low(two[quad % 2][1])
        dropped.append(mm(dropped_x, drop))
    fields = []
    for b in range(boxes):
        p, c, quad = b // 8, (b // 4) % 2, b % 4
        start = (2 * p + c) * order_k
        fields.append(gathered[b] - dropped[quad][start : start + order_k])
    if last:
        pick_ref, field_ref, parent_ref, held = rest
        for b in range(boxes):
            held[b] = fields[b]
        for s in range(field_ref.shape[0]):
            field_ref[s] = held[pick_ref[s]]
        for p in range(parent_count):
            for i in range(order_k):
                parent_ref[p : p + 1, i * plane : (i + 1) * plane] = own[p][i : i + 1]
    else:
        pot_ref, to_ref, back_ref, out_ref = rest
        to_high, to_low = spread_columns(to_ref[...])
        back_high, back_low = spread_columns(back_ref[...])
        row_high, row_low, lane_high, lane_low = masks(order_k)
        value_pair = rows_high(back_high) * rows_low(back_low)
        back_pair = rows_high(to_high) * rows_low(to_low)
        value_x = jnp.where(row_high == lane_high, rows_low(to_low), 0.0)
        source_x = jnp.where(row_high == lane_high, rows_low(back_low), 0.0)
        current = jnp.concatenate(fields, axis=0)
        values = mm(value_x, mm(current, value_pair))
        product = values * (pot_ref[...].reshape(values.shape) + 0.25 * values * values)
        source = mm(source_x, mm(product, back_pair))
        out_ref[...] = source.astype(jnp.bfloat16).reshape(out_ref.shape)


def conv_kernel(dims, packed, offs, *refs):
    term_count, order_k, disp_count, source_count, dest_count = dims
    source_refs = refs[:source_count]
    xl_ref, w_hbm = refs[source_count : source_count + 2]
    out_refs = refs[source_count + 2 : source_count + 2 + dest_count]
    wbuf, pbuf, total, held, sems, held_sems = refs[source_count + 2 + dest_count :]
    plane = order_k * order_k
    half = term_count // 2
    depth = term_count * order_k
    block_boxes = out_refs[0].shape[0]
    dest_rows = dest_count * block_boxes
    loads = [
        pltpu.make_async_copy(ref, held.at[pl.ds(n * block_boxes, block_boxes)], held_sems.at[n])
        for n, ref in enumerate(source_refs)
    ]
    for load in loads:
        load.start()
    for ll in range(disp_count):
        for m in range(term_count):
            pltpu.make_async_copy(
                w_hbm.at[:, pl.ds((m * disp_count + ll) * plane, plane)], wbuf.at[ll, m], sems.at[ll]
            ).start()
    total[...] = jnp.zeros_like(total)
    for load in loads:
        load.wait()

    def push_w(ll, j, reg):
        pltpu.matmul_push_rhs(wbuf[ll, j], reg, 0)
        pltpu.matmul_push_rhs(wbuf[ll, half + j], reg, 1)

    def block_body(ll, base, live, slots):
        pl.run_scoped(
            functools.partial(with_accs, ll, base, live, slots),
            *[
                [[pltpu.ACC(unit)((order_k, plane), jnp.float32) for _ in range(slots)] for _ in range(2)]
                for unit in range(2)
            ],
        )

    def with_accs(ll, base, live, slots, *accs):
        codes = [packed[base + t] for t in range(slots)]
        ids = [code // (4 * dest_rows) for code in codes]
        shifts = [(code // dest_rows) % 4 for code in codes]

        def acc(par):
            for t in range(slots):
                lhs = held[ids[t]]
                for unit in range(2):
                    pltpu.matmul_acc_lhs(accs[unit][par][t], lhs, par if t == 0 else None)

        def pop(par, j):
            for t in range(slots):
                for unit in range(2):
                    row = pl.multiple_of((unit * half + j) * order_k + t * depth, order_k)
                    pbuf[pl.ds(row, order_k), :] = pltpu.matmul_pop(accs[unit][par][t]).astype(jnp.bfloat16)

        push_w(ll, 0, 0)
        acc(0)
        push_w(ll, 1, 1)

        def pair(g, carry):
            j = 2 * g
            acc(1)
            push_w(ll, j + 2, 0)
            pop(0, j)
            acc(0)
            push_w(ll, j + 3, 1)
            pop(1, j + 1)
            return carry

        lax.fori_loop(0, half // 2 - 1, pair, 0)
        acc(1)
        pop(0, half - 2)
        pop(1, half - 1)

        tiles = GROUP * depth // plane
        for g in range(slots // GROUP):
            unit = g % 2
            for q in range(tiles):
                reg = q % 2
                pltpu.matmul_push_rhs(pbuf[pl.ds(g * GROUP * depth + q * plane, plane), :], reg, unit)
                first = True
                for s in range(GROUP):
                    if s * depth < (q + 1) * plane and (s + 1) * depth > q * plane:
                        t = g * GROUP + s
                        pltpu.matmul_acc_lhs(
                            accs[unit][0][t], xl_ref[shifts[t], q + s], reg if first else None
                        )
                        first = False
            for s in range(GROUP):
                t = g * GROUP + s
                tile = pltpu.matmul_pop(accs[unit][0][t])
                dest = jnp.where(t < live, codes[t] % dest_rows, dest_rows)
                total[dest] = total[dest] + tile

    def per_disp(ll, carry):
        pltpu.make_async_copy(wbuf.at[ll], wbuf.at[ll], sems.at[ll]).wait()
        start, stop = offs[ll], offs[ll + 1]

        def per_block(blk, inner):
            base = start + blk * BLOCK
            live = jnp.minimum(stop - base, BLOCK)
            lax.switch(
                (live + GROUP - 1) // GROUP - 1,
                [functools.partial(block_body, ll, base, live, GROUP * (c + 1)) for c in range(BLOCK // GROUP)],
            )
            return inner

        lax.fori_loop(0, (stop - start + BLOCK - 1) // BLOCK, per_block, 0)
        return carry

    lax.fori_loop(0, disp_count, per_disp, 0)
    for r, out_ref in enumerate(out_refs):
        out_ref[...] = total[pl.ds(r * block_boxes, block_boxes)].astype(jnp.bfloat16)


SMEM = pl.BlockSpec(memory_space=pltpu.SMEM)
VMEM = pl.BlockSpec(memory_space=pltpu.VMEM)
ANY = pl.BlockSpec(memory_space=pl.ANY)


def convolve(sources, shifted, yz_kernels, packed, offs, dest_count, term_count, order_k):
    plane = order_k * order_k
    block_boxes = sources[0].shape[0]
    disp_count = yz_kernels.shape[1] // (term_count * plane)
    dims = (term_count, order_k, disp_count, len(sources), dest_count)
    tile = jax.ShapeDtypeStruct((block_boxes, order_k, plane), jnp.bfloat16)
    return pl.pallas_call(
        functools.partial(conv_kernel, dims),
        out_shape=[tile] * dest_count,
        in_specs=[SMEM, SMEM] + [ANY] * len(sources) + [VMEM, ANY],
        out_specs=[VMEM] * dest_count,
        scratch_shapes=[
            pltpu.VMEM((disp_count, term_count, plane, plane), jnp.bfloat16),
            pltpu.VMEM((BLOCK * term_count * order_k, plane), jnp.bfloat16),
            pltpu.VMEM((dest_count * block_boxes + 1, order_k, plane), jnp.float32),
            pltpu.VMEM((len(sources) * block_boxes, order_k, plane), jnp.bfloat16),
            pltpu.SemaphoreType.DMA((disp_count,)),
            pltpu.SemaphoreType.DMA((len(sources),)),
        ],
        compiler_params=pltpu.CompilerParams(vmem_limit_bytes=52 * MIB),
        name="convolve",
    )(packed, offs, *sources, shifted, yz_kernels)


def shifted_factors(x_kernels):
    term_count, stacked, order_k = x_kernels.shape
    plane = order_k * order_k
    depth = term_count * order_k
    flat = x_kernels.reshape(term_count, 3, order_k, order_k).transpose(1, 2, 0, 3).reshape(3, order_k, depth)
    padded = jnp.pad(flat, ((0, 0), (0, 0), (plane, plane)))
    parts = {}
    for q in range(GROUP * depth // plane):
        for s in range(GROUP):
            if s * depth < (q + 1) * plane and (s + 1) * depth > q * plane:
                low = plane + q * plane - s * depth
                parts[q + s] = padded[:, :, low : low + plane]
    return jnp.stack([parts[p] for p in range(len(parts))], axis=1)


def route(tables, places, box_ids, here, sizes, disp_rows):
    oct_here, hi_here, lo_here = here
    hi_count, lo_count, block_boxes = sizes
    entries = jnp.take(tables, box_ids, axis=0).reshape(-1)
    slot_count = entries.shape[0]
    live = entries >= 0
    dest = jnp.maximum(entries, 0) // 32
    disp = jnp.maximum(entries, 0) % 32
    box_range = jnp.arange(places.shape[0], dtype=jnp.int32)
    place = jnp.sum(jnp.where(dest[:, None] == box_range[None, :], places[None, :], 0), axis=1)
    owner = place // block_boxes
    keep = live & (owner // (hi_count * lo_count) == oct_here) & (owner % lo_count == lo_here)
    away = ((owner // lo_count) % hi_count) ^ hi_here
    row = disp % disp_rows
    key = jnp.where(keep, row, disp_rows)
    index = jnp.arange(slot_count, dtype=jnp.int32)
    full_key = key * slot_count + index
    position = jnp.sum((full_key[None, :] < full_key[:, None]).astype(jnp.int32), axis=1)
    source = index // (slot_count // box_ids.shape[0])
    code = (source * 4 + disp // disp_rows) * (hi_count * block_boxes) + away * block_boxes + place % block_boxes
    listed = jnp.arange(slot_count + BLOCK, dtype=jnp.int32)
    packed = jnp.sum(jnp.where(position[None, :] == listed[:, None], code[None, :], 0), axis=1)
    bounds = jnp.arange(16, dtype=jnp.int32)
    offs = jnp.sum((key[None, :] < bounds[:, None]).astype(jnp.int32), axis=1)
    return packed, offs


def flips(count, step):
    return [(i, i ^ step) for i in range(count)]


def gather_sources(source, lo_count):
    near = [source] + [lax.ppermute(source, "lo", flips(lo_count, r)) for r in range(1, lo_count)]
    return near + [lax.ppermute(block, "oct", flips(2, 1)) for block in near]


def shards(
    coefficients,
    potential,
    to_values,
    x_kernels,
    yz_kernels,
    two_scale,
    disp_ids,
    dest_box,
    parent_of,
    child_octant,
):
    box_count, slot_count = disp_ids.shape
    order_k = to_values.shape[0]
    plane = order_k * order_k
    term_count = x_kernels.shape[0]
    disp_rows = yz_kernels.shape[1] // (term_count * plane)
    oct_count, hi_count, lo_count = (lax.axis_size(name) for name in ("oct", "hi", "lo"))
    here = tuple(lax.axis_index(name) for name in ("oct", "hi", "lo"))
    oct_here, hi_here, lo_here = here
    sub_count = hi_count * lo_count
    devices_all = oct_count * sub_count
    sub_here = hi_here * lo_count + lo_here
    sizes = (hi_count, lo_count, box_count)
    flipped = jnp.swapaxes(two_scale, 1, 2)
    back_values = to_values.T

    own_place = parent_of * 8 + child_octant
    own_owner = own_place // box_count - oct_here * sub_count
    own_table = jnp.where(dest_box >= 0, dest_box * 32 + disp_ids, -1)
    words = jnp.concatenate([own_table.reshape(-1), own_place])
    words = jnp.pad(words, (0, -words.shape[0] % 1024)).reshape(-1, 128)
    words = lax.all_to_all(
        jnp.broadcast_to(words[None], (devices_all,) + words.shape), ("oct", "hi", "lo"), 0, 0, tiled=True
    ).reshape(devices_all, -1)
    tables = words[:, : box_count * slot_count].reshape(devices_all * box_count, slot_count)
    places = words[:, box_count * slot_count : box_count * (slot_count + 1)].reshape(-1)

    source = pl.pallas_call(
        first_kernel,
        out_shape=jax.ShapeDtypeStruct((box_count, order_k, plane), jnp.bfloat16),
        in_specs=[VMEM] * 4,
        out_specs=VMEM,
        name="first_source",
    )(coefficients, potential, to_values, back_values)

    group_devices = jnp.stack(
        [
            (oct_here ^ (r // lo_count)) * sub_count + hi_here * lo_count + (lo_here ^ (r % lo_count))
            for r in range(2 * lo_count)
        ]
    )
    group_rows = (group_devices[:, None] * box_count + jnp.arange(box_count)[None, :]).reshape(-1)
    all_rows = jnp.arange(devices_all * box_count, dtype=jnp.int32)
    moved_rows = jnp.sum(
        jnp.where(places[None, :] == group_rows[:, None], all_rows[None, :], 0), axis=1
    )
    shifted = shifted_factors(x_kernels)

    peers = jnp.arange(sub_count, dtype=jnp.int32)
    send_hit = own_owner[None, :] == peers[:, None]
    send_row = jnp.sum(jnp.where(send_hit, jnp.arange(box_count)[None, :], 0), axis=1)
    moved_own = lax.dynamic_slice_in_dim(moved_rows, 0, box_count)
    came_from = moved_own // box_count - oct_here * sub_count
    pick_hit = came_from[None, :] == peers[:, None]
    pick = jnp.sum(jnp.where(pick_hit, jnp.arange(box_count)[None, :], 0), axis=1)

    moved_potential = lax.all_to_all(
        jnp.take(potential.reshape(box_count, order_k, plane), send_row, axis=0),
        ("hi", "lo"),
        0,
        0,
        tiled=True,
    )
    moved_potential = jnp.take(moved_potential, came_from, axis=0)

    tile = (box_count, order_k, plane)
    for iteration in range(ITERS):
        last = iteration == ITERS - 1
        sources = gather_sources(source, lo_count)
        rows = group_rows if iteration == 0 else moved_rows
        packed, offs = route(tables, places, rows, here, sizes, disp_rows)
        outs = convolve(sources, shifted, yz_kernels, packed, offs, hi_count, term_count, order_k)
        parts = [outs[0]] + [lax.ppermute(outs[r], "hi", flips(hi_count, r)) for r in range(1, hi_count)]
        kernel = functools.partial(tree_kernel, last, hi_count)
        if last:
            fields, parents = pl.pallas_call(
                kernel,
                out_shape=[
                    jax.ShapeDtypeStruct((sub_count, order_k, plane), jnp.float32),
                    jax.ShapeDtypeStruct((box_count // 8, order_k * plane), jnp.float32),
                ],
                in_specs=[VMEM] * (hi_count + 2) + [SMEM],
                out_specs=[VMEM] * 2,
                scratch_shapes=[pltpu.VMEM(tile, jnp.float32)],
                name="last_tree",
            )(*parts, two_scale, flipped, pick)
        else:
            source = pl.pallas_call(
                kernel,
                out_shape=jax.ShapeDtypeStruct(tile, jnp.bfloat16),
                in_specs=[VMEM] * (hi_count + 5),
                out_specs=VMEM,
                name="tree_source",
            )(*parts, two_scale, flipped, moved_potential, to_values, back_values)
    returned = lax.all_to_all(fields, ("hi", "lo"), 0, 0, tiled=True)
    next_field = jnp.take(returned, own_owner, axis=0).reshape(box_count, order_k * plane)
    return next_field, parents


def solution(mesh):
    oct_count, sub_count = mesh.devices.shape
    lo_count = 4
    split = Mesh(mesh.devices.reshape(oct_count, sub_count // lo_count, lo_count), ("oct", "hi", "lo"))
    rows = ("oct", "hi", "lo")
    placed = (
        P(rows, None),
        P(rows, None),
        P(),
        P(),
        P(),
        P(),
        P(rows, None),
        P(rows, None),
        P(rows),
        P(rows),
    )
    return jax.shard_map(
        shards,
        mesh=split,
        in_specs=placed,
        out_specs=(P(rows, None), P(rows, None)),
        check_vma=False,
    )
```

profile of v0, /device:TPU:0, one launch (start us, length us, event | category | flops | bytes accessed | tf_op | source)
XLA Modules:
  0.0 158.1 jit_solution(9297669426646446691)
XLA Ops:
  0.6 1.4 copy.31
  2.0 4.0 %first_source.1.refs_0_ = bf16[16,16,256]{2,1,0:T(8,128)(2,1)} custom-call(f32[16,4096]{1,0:T(8,128)} %coef_ref.1, f32[16,4096]{1,0:T(8,128)} %pot_ref.1, f32[16,16]{1,0:T(8,128)} %refs_7_.1, f32[16,16]{1,0:T(8,128)} %bitcast.75), custom_call_target="tpu_custom_call" | custom-call | tf_op jit(solution)/shard_map/first_source/pallas_call | solution.py:371
  6.0 2.9 %collective-permute-start = (bf16[16,16,256]{2,1,0:T(8,128)(2,1)}, bf16[16,16,256]{2,1,0:T(8,128)(2,1)S(1)}, u32[]{:S(2)}, u32[]{:S(2)}) collective-permute-start(bf16[16,16,256]{2,1,0:T(8,128)(2,1)} %first_source.1.refs_0_), channel_id=1, source_target_pairs={{0,1},{1,0},{2,3},{3,2},{4,5},{5,4},{6,7},{7,6},{8,9},{9,8},{10,11... | collective-permute-start | bytes 393224 | tf_op jit(solution)/shard_map/ppermute | solution.py:329
  8.9 1.5 collective-permute-start.1
  10.4 0.7 add_select_fusion.21
  11.2 0.7 compare_and_fusion
  12.0 0.7 broadcast_in_dim.123
  12.6 6.4 %all-to-all-start = ((s32[32,8,128]{2,1,0:T(8,128)}), s32[32,8,128]{2,1,0:T(8,128)S(1)}, u32[]{:S(2)}, u32[]{:S(2)}) async-start(s32[32,8,128]{2,1,0:T(8,128)} %broadcast_in_dim.123), calls=%async_computation | async-start | bytes 262144 | tf_op jit(solution)/shard_map/all_to_all | solution.py:365
  19.5 1.1 copy.40
  21.1 1.0 copy.42
  22.2 0.6 gather_fusion.2
  22.8 0.8 broadcast_select_fusion.2
  23.6 1.4 copy.39
  25.8 1.2 all-to-all-done
  27.0 5.6 %all-to-all-start.1 = ((f32[16,16,256]{2,1,0:T(8,128)}), f32[16,16,256]{2,1,0:T(8,128)S(1)}, u32[]{:S(2)}, u32[]{:S(2)}) async-start(f32[16,16,256]{2,1,0:T(8,128)} %broadcast_select_fusion.2), calls=%async_computation.1 | async-start | bytes 524288 | tf_op jit(solution)/shard_map/all_to_all | solution.py:400
  32.7 0.6 gather_fusion.1
  33.9 0.6 gather_fusion
  35.5 1.6 %select_reduce_fusion.2 = (s32[2048]{0:T(1024)S(1)}, s32[2048]{0:T(1024)S(1)}) fusion(s32[2048]{0:T(1024)S(1)} %add_select_fusion.9, s32[512]{0:T(512)S(1)} %eq.168, s32[2048]{0:T(1024)S(1)} %add_select_fusion.20), kind=kLoop, calls=%fused_computation.11 | loop fusion | flops 6287360 | bytes 34816 | tf_op jit(solution)/shard_map/reduce_sum | solution.py:306
  37.2 1.8 %convert_reduce_fusion = s32[2048]{0:T(1024)S(1)} fusion(s32[2048]{0:T(1024)S(1)} %get-tuple-element.31), kind=kLoop, calls=%fused_computation.9 | loop fusion | flops 12580864 | bytes 16384 | tf_op jit(solution)/shard_map/reduce_sum | solution.py:314
  39.0 1.8 %select_reduce_fusion.packed = s32[2080]{0:T(1024)S(1)} fusion(s32[2048]{0:T(1024)S(1)} %get-tuple-element.43, s32[2048]{0:T(1024)S(1)} %convert_reduce_fusion), kind=kLoop, calls=%fused_computation.5 | loop fusion | flops 12777440 | bytes 24704 | tf_op jit(solution)/shard_map/reduce_sum | solution.py:318
  41.0 0.9 copy-done
  41.9 21.2 %convolve.2 = (bf16[16,16,256]{2,1,0:T(8,128)(2,1)S(1)}, bf16[16,16,256]{2,1,0:T(8,128)(2,1)S(1)}, bf16[16,16,256]{2,1,0:T(8,128)(2,1)S(1)}, bf16[16,16,256]{2,1,0:T(8,128)(2,1)S(1)}) custom-call(s32[2080]{0:T(1024)S(1)} %select_reduce_fusion.packed, s32[16]{0:T(128)S(1)} %convert_reduce_fusion.2.offs, bf16[16,16,256]{2,1,0:T(8,128)(2,1)S(1)} %copy-done, ...), custom_call_target="tpu_custom_call" | custom-call | tf_op jit(solution)/shard_map/convolve/pallas_call | solution.py:264
  63.2 0.6 copy-done.3
  63.8 2.1 %collective-permute-start.7 = (bf16[16,16,256]{2,1,0:T(8,128)(2,1)S(1)}, bf16[16,16,256]{2,1,0:T(8,128)(2,1)S(1)}, u32[]{:S(2)}, u32[]{:S(2)}) collective-permute-start(bf16[16,16,256]{2,1,0:T(8,128)(2,1)S(1)} %get-tuple-element.15), channel_id=1, source_target_pairs={{0,4},{4,0},{8,12},{12,8},{1,5},{5,1},{9,13},{13,9},{2,6},{6,2},{1... | collective-permute-start | bytes 393224 | tf_op jit(solution)/shard_map/ppermute | solution.py:416
  65.9 2.3 %collective-permute-start.8 = (bf16[16,16,256]{2,1,0:T(8,128)(2,1)S(1)}, bf16[16,16,256]{2,1,0:T(8,128)(2,1)S(1)}, u32[]{:S(2)}, u32[]{:S(2)}) collective-permute-start(bf16[16,16,256]{2,1,0:T(8,128)(2,1)S(1)} %get-tuple-element.16), channel_id=1, source_target_pairs={{0,8},{4,12},{8,0},{12,4},{1,9},{5,13},{9,1},{13,5},{2,10},{6,14},... | collective-permute-start | bytes 393224 | tf_op jit(solution)/shard_map/ppermute | solution.py:416
  68.8 0.8 broadcast_select_fusion.1.refs_6_
  69.8 8.9 %collective-permute-done.8.refs_2_ = bf16[16,16,256]{2,1,0:T(8,128)(2,1)S(1)} collective-permute-done((bf16[16,16,256]{2,1,0:T(8,128)(2,1)S(1)}, bf16[16,16,256]{2,1,0:T(8,128)(2,1)S(1)}, u32[]{:S(2)}, u32[]{:S(2)}) %collective-permute-start.8) | collective-permute-done | bytes 131104 | tf_op jit(solution)/shard_map/ppermute | solution.py:416
  78.8 0.6 copy-done.8
  79.5 7.0 %tree_source.1.refs_0_ = bf16[16,16,256]{2,1,0:T(8,128)(2,1)} custom-call(bf16[16,16,256]{2,1,0:T(8,128)(2,1)} %copy-done.3, bf16[16,16,256]{2,1,0:T(8,128)(2,1)} %copy-done.7, bf16[16,16,256]{2,1,0:T(8,128)(2,1)} %copy-done.8, bf16[16,16,256]{2,1,0:T(8,128)(2,1)} %copy-done.9, f32[2,16,16]{2,1,0:T(8,128)} %refs_4_.3, f32[2,16,16]{2,1,0:T(8,128)} %bitcast.73, ...), custom_call_target="tpu_custom_call" | custom-call | tf_op jit(solution)/shard_map/tree_source/pallas_call | solution.py:431
  87.0 1.6 %collective-permute-start.11 = (bf16[16,16,256]{2,1,0:T(8,128)(2,1)}, bf16[16,16,256]{2,1,0:T(8,128)(2,1)S(1)}, u32[]{:S(2)}, u32[]{:S(2)}) collective-permute-start(bf16[16,16,256]{2,1,0:T(8,128)(2,1)} %tree_source.1.refs_0_), channel_id=1, source_target_pairs={{0,2},{1,3},{2,0},{3,1},{4,6},{5,7},{6,4},{7,5},{8,10},{9,11},{10,... | collective-permute-start | bytes 393224 | tf_op jit(solution)/shard_map/ppermute | solution.py:329
  88.6 1.4 collective-permute-start.12
  90.0 1.8 %convert_reduce_fusion.1 = s32[2048]{0:T(1024)S(1)} fusion(s32[2048]{0:T(1024)S(1)} %get-tuple-element.46), kind=kLoop, calls=%fused_computation.10 | loop fusion | flops 12580864 | bytes 16384 | tf_op jit(solution)/shard_map/reduce_sum | solution.py:314
  91.9 1.2 collective-permute-done.10.refs_1_
  93.6 1.6 %collective-permute-done.12.refs_3_ = bf16[16,16,256]{2,1,0:T(8,128)(2,1)S(1)} collective-permute-done((bf16[16,16,256]{2,1,0:T(8,128)(2,1)}, bf16[16,16,256]{2,1,0:T(8,128)(2,1)S(1)}, u32[]{:S(2)}, u32[]{:S(2)}) %collective-permute-start.12) | collective-permute-done | bytes 131104 | tf_op jit(solution)/shard_map/ppermute | solution.py:329
  95.2 1.8 %select_reduce_fusion.1.packed = s32[2080]{0:T(1024)S(1)} fusion(s32[2048]{0:T(1024)S(1)} %get-tuple-element.45, s32[2048]{0:T(1024)S(1)} %convert_reduce_fusion.1), kind=kLoop, calls=%fused_computation.7 | loop fusion | flops 12777440 | bytes 24704 | tf_op jit(solution)/shard_map/reduce_sum | solution.py:318
  97.2 0.9 copy-done.1
  98.1 19.8 %convolve.3 = (bf16[16,16,256]{2,1,0:T(8,128)(2,1)S(1)}, bf16[16,16,256]{2,1,0:T(8,128)(2,1)S(1)}, bf16[16,16,256]{2,1,0:T(8,128)(2,1)S(1)}, bf16[16,16,256]{2,1,0:T(8,128)(2,1)S(1)}) custom-call(s32[2080]{0:T(1024)S(1)} %select_reduce_fusion.1.packed, s32[16]{0:T(128)S(1)} %convert_reduce_fusion.3.offs, bf16[16,16,256]{2,1,0:T(8,128)(2,1)S(1)} %copy-done.1, ...), custom_call_target="tpu_custom_call" | custom-call | tf_op jit(solution)/shard_map/convolve/pallas_call | solution.py:264
  117.9 0.6 copy-done.2
  118.5 4.4 %collective-permute-start.17 = (bf16[16,16,256]{2,1,0:T(8,128)(2,1)S(1)}, bf16[16,16,256]{2,1,0:T(8,128)(2,1)S(1)}, u32[]{:S(2)}, u32[]{:S(2)}) collective-permute-start(bf16[16,16,256]{2,1,0:T(8,128)(2,1)S(1)} %get-tuple-element.19), channel_id=1, source_target_pairs={{0,4},{4,0},{8,12},{12,8},{1,5},{5,1},{9,13},{13,9},{2,6},{6,2},{1... | collective-permute-start | bytes 393224 | tf_op jit(solution)/shard_map/ppermute | solution.py:416
  122.9 1.4 collective-permute-start.18
  124.3 1.5 collective-permute-start.19
  125.8 0.6 select_reduce_fusion.5.refs_6_
  126.9 8.9 %collective-permute-done.18.refs_2_ = bf16[16,16,256]{2,1,0:T(8,128)(2,1)S(1)} collective-permute-done((bf16[16,16,256]{2,1,0:T(8,128)(2,1)S(1)}, bf16[16,16,256]{2,1,0:T(8,128)(2,1)S(1)}, u32[]{:S(2)}, u32[]{:S(2)}) %collective-permute-start.18) | collective-permute-done | bytes 131104 | tf_op jit(solution)/shard_map/ppermute | solution.py:416
  135.8 0.6 copy-done.5
  136.5 4.6 %last_tree.1 = (f32[16,16,256]{2,1,0:T(8,128)}, f32[2,4096]{1,0:T(2,128)}) custom-call(bf16[16,16,256]{2,1,0:T(8,128)(2,1)} %copy-done.2, bf16[16,16,256]{2,1,0:T(8,128)(2,1)} %copy-done.4, bf16[16,16,256]{2,1,0:T(8,128)(2,1)} %copy-done.5, bf16[16,16,256]{2,1,0:T(8,128)(2,1)} %copy-done.6, f32[2,16,16]{2,1,0:T(8,128)} %refs_4_.3, f32[2,16,16]{2,1,0:T(8,128)} %bitcast.74, ...), custom_call_target="tpu_custom_call" | custom-call | tf_op jit(solution)/shard_map/last_tree/pallas_call | solution.py:419
  141.1 5.7 %all-to-all-start.2 = ((f32[16,16,256]{2,1,0:T(8,128)}), f32[16,16,256]{2,1,0:T(8,128)S(1)}, u32[]{:S(2)}, u32[]{:S(2)}) async-start(f32[16,16,256]{2,1,0:T(8,128)} %get-tuple-element.22), calls=%async_computation.2 | async-start | bytes 524288 | tf_op jit(solution)/shard_map/all_to_all | solution.py:438
  146.8 9.8 %all-to-all-done.2 = f32[16,16,256]{2,1,0:T(8,128)S(1)} async-done(((f32[16,16,256]{2,1,0:T(8,128)}), f32[16,16,256]{2,1,0:T(8,128)S(1)}, u32[]{:S(2)}, u32[]{:S(2)}) %all-to-all-start.2) | async-done | bytes 262176 | tf_op jit(solution)/shard_map/all_to_all | solution.py:438
  157.3 0.9 copy.43
  (99 shorter events, 7.0 us)
Async XLA Ops:
  6.0 19.0 %collective-permute-start = (bf16[16,16,256]{2,1,0:T(8,128)(2,1)}, bf16[16,16,256]{2,1,0:T(8,128)(2,1)S(1)}, u32[]{:S(2)}, u32[]{:S(2)}) collective-permute-start(bf16[16,16,256]{2,1,0:T(8,128)(2,1)} %first_source.1.refs_0_), channel_id=1, source_target_pairs={{0,1},{1,0},{2,3},{3,2},{4,5},{5,4},{6,7},{7,6},{8,9},{9,8},{10,11... | collective-permute-start | bytes 393224 | tf_op jit(solution)/shard_map/ppermute | solution.py:329
  8.9 16.4 %collective-permute-start.1 = (bf16[16,16,256]{2,1,0:T(8,128)(2,1)}, bf16[16,16,256]{2,1,0:T(8,128)(2,1)S(1)}, u32[]{:S(2)}, u32[]{:S(2)}) collective-permute-start(bf16[16,16,256]{2,1,0:T(8,128)(2,1)} %first_source.1.refs_0_), channel_id=1, source_target_pairs={{0,2},{1,3},{2,0},{3,1},{4,6},{5,7},{6,4},{7,5},{8,10},{9,11},{10,... | collective-permute-start | bytes 393224 | tf_op jit(solution)/shard_map/ppermute | solution.py:329
  10.4 15.1 %collective-permute-start.2 = (bf16[16,16,256]{2,1,0:T(8,128)(2,1)}, bf16[16,16,256]{2,1,0:T(8,128)(2,1)S(1)}, u32[]{:S(2)}, u32[]{:S(2)}) collective-permute-start(bf16[16,16,256]{2,1,0:T(8,128)(2,1)} %first_source.1.refs_0_), channel_id=1, source_target_pairs={{0,3},{1,2},{2,1},{3,0},{4,7},{5,6},{6,5},{7,4},{8,11},{9,10},{10,... | collective-permute-start | bytes 393224 | tf_op jit(solution)/shard_map/ppermute | solution.py:329
  10.4 30.6 %collective-permute-start.3 = (bf16[16,16,256]{2,1,0:T(8,128)(2,1)}, bf16[16,16,256]{2,1,0:T(8,128)(2,1)S(1)}, u32[]{:S(2)}, u32[]{:S(2)}) collective-permute-start(bf16[16,16,256]{2,1,0:T(8,128)(2,1)} %first_source.1.refs_0_), channel_id=1, source_target_pairs={{0,16},{16,0},{1,17},{17,1},{2,18},{18,2},{3,19},{19,3},{4,20},{20... | collective-permute-start | bytes 393224 | tf_op jit(solution)/shard_map/ppermute | solution.py:330
  12.6 14.4 %all-to-all-start = ((s32[32,8,128]{2,1,0:T(8,128)}), s32[32,8,128]{2,1,0:T(8,128)S(1)}, u32[]{:S(2)}, u32[]{:S(2)}) async-start(s32[32,8,128]{2,1,0:T(8,128)} %broadcast_in_dim.123), calls=%async_computation | async-start | bytes 262144 | tf_op jit(solution)/shard_map/all_to_all | solution.py:365
  25.0 16.0 %collective-permute-start.4 = (bf16[16,16,256]{2,1,0:T(8,128)(2,1)S(1)}, bf16[16,16,256]{2,1,0:T(8,128)(2,1)S(1)}, u32[]{:S(2)}, u32[]{:S(2)}) collective-permute-start(bf16[16,16,256]{2,1,0:T(8,128)(2,1)S(1)} %collective-permute-done.refs_1_), channel_id=1, source_target_pairs={{0,16},{16,0},{1,17},{17,1},{2,18},{18,2},{3,19},{19,3},{4,20},{20... | collective-permute-start | bytes 393224 | tf_op jit(solution)/shard_map/ppermute | solution.py:330
  25.3 15.7 %collective-permute-start.5 = (bf16[16,16,256]{2,1,0:T(8,128)(2,1)S(1)}, bf16[16,16,256]{2,1,0:T(8,128)(2,1)S(1)}, u32[]{:S(2)}, u32[]{:S(2)}) collective-permute-start(bf16[16,16,256]{2,1,0:T(8,128)(2,1)S(1)} %collective-permute-done.1.refs_2_), channel_id=1, source_target_pairs={{0,16},{16,0},{1,17},{17,1},{2,18},{18,2},{3,19},{19,3},{4,20},{20... | collective-permute-start | bytes 393224 | tf_op jit(solution)/shard_map/ppermute | solution.py:330
  25.5 15.5 %collective-permute-start.6 = (bf16[16,16,256]{2,1,0:T(8,128)(2,1)S(1)}, bf16[16,16,256]{2,1,0:T(8,128)(2,1)S(1)}, u32[]{:S(2)}, u32[]{:S(2)}) collective-permute-start(bf16[16,16,256]{2,1,0:T(8,128)(2,1)S(1)} %collective-permute-done.2.refs_3_), channel_id=1, source_target_pairs={{0,16},{16,0},{1,17},{17,1},{2,18},{18,2},{3,19},{19,3},{4,20},{20... | collective-permute-start | bytes 393224 | tf_op jit(solution)/shard_map/ppermute | solution.py:330
  27.0 41.3 %all-to-all-start.1 = ((f32[16,16,256]{2,1,0:T(8,128)}), f32[16,16,256]{2,1,0:T(8,128)S(1)}, u32[]{:S(2)}, u32[]{:S(2)}) async-start(f32[16,16,256]{2,1,0:T(8,128)} %broadcast_select_fusion.2), calls=%async_computation.1 | async-start | bytes 524288 | tf_op jit(solution)/shard_map/all_to_all | solution.py:400
  41.0 0.9 copy-start
  63.2 0.7 copy-start.3
  63.8 6.0 %collective-permute-start.7 = (bf16[16,16,256]{2,1,0:T(8,128)(2,1)S(1)}, bf16[16,16,256]{2,1,0:T(8,128)(2,1)S(1)}, u32[]{:S(2)}, u32[]{:S(2)}) collective-permute-start(bf16[16,16,256]{2,1,0:T(8,128)(2,1)S(1)} %get-tuple-element.15), channel_id=1, source_target_pairs={{0,4},{4,0},{8,12},{12,8},{1,5},{5,1},{9,13},{13,9},{2,6},{6,2},{1... | collective-permute-start | bytes 393224 | tf_op jit(solution)/shard_map/ppermute | solution.py:416
  65.9 12.9 %collective-permute-start.8 = (bf16[16,16,256]{2,1,0:T(8,128)(2,1)S(1)}, bf16[16,16,256]{2,1,0:T(8,128)(2,1)S(1)}, u32[]{:S(2)}, u32[]{:S(2)}) collective-permute-start(bf16[16,16,256]{2,1,0:T(8,128)(2,1)S(1)} %get-tuple-element.16), channel_id=1, source_target_pairs={{0,8},{4,12},{8,0},{12,4},{1,9},{5,13},{9,1},{13,5},{2,10},{6,14},... | collective-permute-start | bytes 393224 | tf_op jit(solution)/shard_map/ppermute | solution.py:416
  68.2 10.6 %collective-permute-start.9 = (bf16[16,16,256]{2,1,0:T(8,128)(2,1)S(1)}, bf16[16,16,256]{2,1,0:T(8,128)(2,1)S(1)}, u32[]{:S(2)}, u32[]{:S(2)}) collective-permute-start(bf16[16,16,256]{2,1,0:T(8,128)(2,1)S(1)} %get-tuple-element.17), channel_id=1, source_target_pairs={{0,12},{4,8},{8,4},{12,0},{1,13},{5,9},{9,5},{13,1},{2,14},{6,10},... | collective-permute-start | bytes 393224 | tf_op jit(solution)/shard_map/ppermute | solution.py:416
  69.8 9.0 %copy-start.7 = (bf16[16,16,256]{2,1,0:T(8,128)(2,1)}, bf16[16,16,256]{2,1,0:T(8,128)(2,1)S(1)}, u32[]{:S(2)}) copy-start(bf16[16,16,256]{2,1,0:T(8,128)(2,1)S(1)} %collective-permute-done.7.refs_1_) | copy-start | bytes 393220
  78.8 0.7 copy-start.8
  78.8 0.7 copy-start.9
  86.5 6.6 %collective-permute-start.10 = (bf16[16,16,256]{2,1,0:T(8,128)(2,1)}, bf16[16,16,256]{2,1,0:T(8,128)(2,1)S(1)}, u32[]{:S(2)}, u32[]{:S(2)}) collective-permute-start(bf16[16,16,256]{2,1,0:T(8,128)(2,1)} %tree_source.1.refs_0_), channel_id=1, source_target_pairs={{0,1},{1,0},{2,3},{3,2},{4,5},{5,4},{6,7},{7,6},{8,9},{9,8},{10,11... | collective-permute-start | bytes 393224 | tf_op jit(solution)/shard_map/ppermute | solution.py:329
  87.0 6.6 %collective-permute-start.11 = (bf16[16,16,256]{2,1,0:T(8,128)(2,1)}, bf16[16,16,256]{2,1,0:T(8,128)(2,1)S(1)}, u32[]{:S(2)}, u32[]{:S(2)}) collective-permute-start(bf16[16,16,256]{2,1,0:T(8,128)(2,1)} %tree_source.1.refs_0_), channel_id=1, source_target_pairs={{0,2},{1,3},{2,0},{3,1},{4,6},{5,7},{6,4},{7,5},{8,10},{9,11},{10,... | collective-permute-start | bytes 393224 | tf_op jit(solution)/shard_map/ppermute | solution.py:329
  88.6 6.6 %collective-permute-start.12 = (bf16[16,16,256]{2,1,0:T(8,128)(2,1)}, bf16[16,16,256]{2,1,0:T(8,128)(2,1)S(1)}, u32[]{:S(2)}, u32[]{:S(2)}) collective-permute-start(bf16[16,16,256]{2,1,0:T(8,128)(2,1)} %tree_source.1.refs_0_), channel_id=1, source_target_pairs={{0,3},{1,2},{2,1},{3,0},{4,7},{5,6},{6,5},{7,4},{8,11},{9,10},{10,... | collective-permute-start | bytes 393224 | tf_op jit(solution)/shard_map/ppermute | solution.py:329
  91.8 5.3 %collective-permute-start.13 = (bf16[16,16,256]{2,1,0:T(8,128)(2,1)}, bf16[16,16,256]{2,1,0:T(8,128)(2,1)S(1)}, u32[]{:S(2)}, u32[]{:S(2)}) collective-permute-start(bf16[16,16,256]{2,1,0:T(8,128)(2,1)} %tree_source.1.refs_0_), channel_id=1, source_target_pairs={{0,16},{16,0},{1,17},{17,1},{2,18},{18,2},{3,19},{19,3},{4,20},{20... | collective-permute-start | bytes 393224 | tf_op jit(solution)/shard_map/ppermute | solution.py:330
  93.1 4.1 %collective-permute-start.14 = (bf16[16,16,256]{2,1,0:T(8,128)(2,1)S(1)}, bf16[16,16,256]{2,1,0:T(8,128)(2,1)S(1)}, u32[]{:S(2)}, u32[]{:S(2)}) collective-permute-start(bf16[16,16,256]{2,1,0:T(8,128)(2,1)S(1)} %collective-permute-done.10.refs_1_), channel_id=1, source_target_pairs={{0,16},{16,0},{1,17},{17,1},{2,18},{18,2},{3,19},{19,3},{4,20},{20... | collective-permute-start | bytes 393224 | tf_op jit(solution)/shard_map/ppermute | solution.py:330
  93.6 3.6 %collective-permute-start.15 = (bf16[16,16,256]{2,1,0:T(8,128)(2,1)S(1)}, bf16[16,16,256]{2,1,0:T(8,128)(2,1)S(1)}, u32[]{:S(2)}, u32[]{:S(2)}) collective-permute-start(bf16[16,16,256]{2,1,0:T(8,128)(2,1)S(1)} %collective-permute-done.11.refs_2_), channel_id=1, source_target_pairs={{0,16},{16,0},{1,17},{17,1},{2,18},{18,2},{3,19},{19,3},{4,20},{20... | collective-permute-start | bytes 393224 | tf_op jit(solution)/shard_map/ppermute | solution.py:330
  95.2 1.9 %collective-permute-start.16 = (bf16[16,16,256]{2,1,0:T(8,128)(2,1)S(1)}, bf16[16,16,256]{2,1,0:T(8,128)(2,1)S(1)}, u32[]{:S(2)}, u32[]{:S(2)}) collective-permute-start(bf16[16,16,256]{2,1,0:T(8,128)(2,1)S(1)} %collective-permute-done.12.refs_3_), channel_id=1, source_target_pairs={{0,16},{16,0},{1,17},{17,1},{2,18},{18,2},{3,19},{19,3},{4,20},{20... | collective-permute-start | bytes 393224 | tf_op jit(solution)/shard_map/ppermute | solution.py:330
  97.2 0.9 copy-start.1
  117.9 0.7 copy-start.2
  118.5 8.3 %collective-permute-start.17 = (bf16[16,16,256]{2,1,0:T(8,128)(2,1)S(1)}, bf16[16,16,256]{2,1,0:T(8,128)(2,1)S(1)}, u32[]{:S(2)}, u32[]{:S(2)}) collective-permute-start(bf16[16,16,256]{2,1,0:T(8,128)(2,1)S(1)} %get-tuple-element.19), channel_id=1, source_target_pairs={{0,4},{4,0},{8,12},{12,8},{1,5},{5,1},{9,13},{13,9},{2,6},{6,2},{1... | collective-permute-start | bytes 393224 | tf_op jit(solution)/shard_map/ppermute | solution.py:416
  122.9 12.9 %collective-permute-start.18 = (bf16[16,16,256]{2,1,0:T(8,128)(2,1)S(1)}, bf16[16,16,256]{2,1,0:T(8,128)(2,1)S(1)}, u32[]{:S(2)}, u32[]{:S(2)}) collective-permute-start(bf16[16,16,256]{2,1,0:T(8,128)(2,1)S(1)} %get-tuple-element.20), channel_id=1, source_target_pairs={{0,8},{4,12},{8,0},{12,4},{1,9},{5,13},{9,1},{13,5},{2,10},{6,14},... | collective-permute-start | bytes 393224 | tf_op jit(solution)/shard_map/ppermute | solution.py:416
  124.3 11.5 %collective-permute-start.19 = (bf16[16,16,256]{2,1,0:T(8,128)(2,1)S(1)}, bf16[16,16,256]{2,1,0:T(8,128)(2,1)S(1)}, u32[]{:S(2)}, u32[]{:S(2)}) collective-permute-start(bf16[16,16,256]{2,1,0:T(8,128)(2,1)S(1)} %get-tuple-element.21), channel_id=1, source_target_pairs={{0,12},{4,8},{8,4},{12,0},{1,13},{5,9},{9,5},{13,1},{2,14},{6,10},... | collective-permute-start | bytes 393224 | tf_op jit(solution)/shard_map/ppermute | solution.py:416
  126.9 8.9 %copy-start.4 = (bf16[16,16,256]{2,1,0:T(8,128)(2,1)}, bf16[16,16,256]{2,1,0:T(8,128)(2,1)S(1)}, u32[]{:S(2)}) copy-start(bf16[16,16,256]{2,1,0:T(8,128)(2,1)S(1)} %collective-permute-done.17.refs_1_) | copy-start | bytes 393220
  135.8 0.7 copy-start.5
  135.8 0.7 copy-start.6
  141.1 15.5 %all-to-all-start.2 = ((f32[16,16,256]{2,1,0:T(8,128)}), f32[16,16,256]{2,1,0:T(8,128)S(1)}, u32[]{:S(2)}, u32[]{:S(2)}) async-start(f32[16,16,256]{2,1,0:T(8,128)} %get-tuple-element.22), calls=%async_computation.2 | async-start | bytes 524288 | tf_op jit(solution)/shard_map/all_to_all | solution.py:438
where the time goes:
time: 158 us
  Pallas kernels  56.6 us (36%)
  starting transfers between devices  38.3 us (24%)
  waiting for transfers between devices  32.9 us (21%)
  local copies, waits for them, and re-layouts  15.6 us (10%)
  other arithmetic  13.7 us (9%)
    pallas_call x2, Pallas kernels, convolve(): pl.pallas_call(functools.partial(conv_kernel, dims), out_shape=[tile] * d...  41 us
    ppermute x6, waiting for transfers between devices, shards(): lax.ppermute(outs[r], 'hi', flips(hi_count, r))  18.5 us
    ppermute x6, starting transfers between devices, shards(): lax.ppermute(outs[r], 'hi', flips(hi_count, r))  11.7 us
    all_to_all x1, waiting for transfers between devices, shards(): returned = lax.all_to_all(fields, ('hi', 'lo'), 0, 0, tiled=True)  9.76 us
    unnamed x32, local copies, waits for them, and re-layouts  9.41 us
    ppermute x6, starting transfers between devices, gather_sources(): lax.ppermute(source, 'lo', flips(lo_count, r))  7.94 us
    pallas_call x1, Pallas kernels, shards(): pl.pallas_call(kernel, out_shape=jax.ShapeDtypeStruct(tile, jnp.bfloat16)...  7 us
    all_to_all x1, starting transfers between devices, shards(): lax.all_to_all(jnp.broadcast_to(words[None], (devices_all,) + words.shape...  6.44 us
  transfers between devices with their start and end apart: 23, of which 9 were waited for; matrix products, arithmetic and copies ran while one was open for 14% of the time, Pallas kernels for 13%

commit v1 on v0

v1 whole, which is shorter than its diff:
```python
import functools

import jax
import jax.numpy as jnp
from jax import lax
from jax.experimental import pallas as pl
from jax.experimental.pallas import tpu as pltpu
from jax.sharding import Mesh
from jax.sharding import PartitionSpec as P

ITERS = 2
BLOCK = 32
GROUP = 4
LANES = 128
MIB = 1024 * 1024
SMEM = pl.BlockSpec(memory_space=pltpu.SMEM)
VMEM = pl.BlockSpec(memory_space=pltpu.VMEM)
ANY = pl.BlockSpec(memory_space=pl.ANY)


def iota(shape, dim):
    return lax.broadcasted_iota(jnp.int32, shape, dim)


def mm(left, right):
    return jnp.dot(left, right, precision=lax.Precision.HIGHEST, preferred_element_type=jnp.float32)


def dot16(left, right):
    return jnp.dot(left, right, preferred_element_type=jnp.float32)


def halves(matrix):
    high = matrix.astype(jnp.bfloat16)
    return high, (matrix - high.astype(jnp.float32)).astype(jnp.bfloat16)


def mm_halves(left, right):
    rows = left[0].shape[0]
    both = dot16(jnp.concatenate(left, axis=0), right[0])
    return both[:rows] + both[rows:] + dot16(left[0], right[1])


def rows_high(matrix):
    order_k, width = matrix.shape
    return jnp.broadcast_to(matrix[:, None, :], (order_k, order_k, width)).reshape(order_k * order_k, width)


def rows_low(matrix):
    order_k, width = matrix.shape
    return jnp.broadcast_to(matrix[None, :, :], (order_k, order_k, width)).reshape(order_k * order_k, width)


def spread_columns(matrix):
    order_k = matrix.shape[0]
    shape = (order_k, order_k * order_k)
    slot, lane = iota(shape, 0), iota(shape, 1)
    high = (lane // order_k == slot).astype(jnp.float32)
    low = (lane % order_k == slot).astype(jnp.float32)
    return mm(matrix, high), mm(matrix, low)


def masks(order_k):
    shape = (order_k * order_k, order_k * order_k)
    row, lane = iota(shape, 0), iota(shape, 1)
    return row // order_k, row % order_k, lane // order_k, lane % order_k


def pack_kernel(info, disp_ref, dest_ref, place_ref, out_ref):
    boxes, slots = disp_ref.shape
    half = boxes // 2
    dest = dest_ref[...]
    entry = jnp.where(dest >= 0, dest * 32 + disp_ref[...] + 1, 0).astype(jnp.float32)
    lane = iota((slots, LANES), 1)
    slot = iota((slots, LANES), 0)
    lane_out = iota((half, LANES), 1)
    row_out = iota((half, LANES), 0)
    words = jnp.zeros((half, LANES), jnp.float32)
    for h in range(2):
        start = h * (LANES // 2)
        words += mm(entry[h * half : (h + 1) * half], (lane == slot + start).astype(jnp.float32))
    words = words.astype(jnp.int32)
    for h in range(2):
        start = h * (LANES // 2)
        place = place_ref[h * half : (h + 1) * half, :]
        words = jnp.where(lane_out == start + slots, place, words)
        words = jnp.where(lane_out == start + slots + 1, info[3] * boxes + h * half + row_out, words)
    for d in range(out_ref.shape[0]):
        out_ref[d] = words


def first_kernel(coef_ref, pot_ref, to_ref, back_ref, out_ref):
    order_k = to_ref.shape[0]
    plane = order_k * order_k
    to_high, to_low = spread_columns(to_ref[...])
    back_high, back_low = spread_columns(back_ref[...])
    row_high, row_low, lane_high, lane_low = masks(order_k)
    value_pair = halves(rows_high(back_high) * rows_low(back_low))
    back_pair = halves(rows_high(to_high) * rows_low(to_low))
    value_x = halves(jnp.where(row_low == lane_low, rows_high(to_high), 0.0))
    source_x = halves(jnp.where(row_high == lane_low, rows_low(back_high), 0.0))

    def by_x(ref):
        return jnp.concatenate([ref[:, x * plane : (x + 1) * plane] for x in range(order_k)], axis=0)

    values = mm_halves(value_x, halves(mm_halves(halves(by_x(coef_ref)), value_pair)))
    product = values * (by_x(pot_ref) + 0.25 * values * values)
    source = mm_halves(source_x, halves(mm_halves(halves(product), back_pair)))
    out_ref[...] = source.astype(jnp.bfloat16).reshape(out_ref.shape)


def route_kernel(dims, info, words_ref, w_hbm, *refs):
    oct_count, hi_count, lo_count, boxes, slots, disp_rows = dims
    list_refs, moved_ref, held_ref, sem = refs[:ITERS], refs[ITERS], refs[ITERS + 1], refs[ITERS + 2]
    load = pltpu.make_async_copy(w_hbm, held_ref, sem)
    load.start()
    oct_here, hi_here, lo_here = info[0], info[1], info[2]
    width = LANES // 2
    words = words_ref[...].reshape(-1, LANES)
    table = jnp.concatenate([words[:, :width], words[:, width:]], axis=0)
    total = table.shape[0]
    place_col, id_col = table[:, slots : slots + 1], table[:, slots + 1 : slots + 2]
    flat = table.astype(jnp.float32).T.astype(jnp.int32)
    low = (flat % 256).astype(jnp.float32).astype(jnp.bfloat16)
    high = (flat // 256).astype(jnp.float32).astype(jnp.bfloat16)

    def look(hit):
        chosen = hit.astype(jnp.float32).astype(jnp.bfloat16)
        return (dot16(low, chosen) + 256.0 * dot16(high, chosen)).astype(jnp.int32)

    lanes = oct_count * lo_count * boxes
    lane = iota((1, lanes), 1)
    member = lane // boxes
    device = ((member // lo_count) ^ oct_here) * (hi_count * lo_count) + hi_here * lo_count
    device = device + ((member % lo_count) ^ lo_here)
    target = device * boxes + lane % boxes
    dest_rows = hi_count * boxes
    source = iota((slots, lanes), 1)
    list_rows = list_refs[0].shape[0]
    upper = (iota((lanes, lanes), 0) < iota((lanes, lanes), 1)).astype(jnp.float32).astype(jnp.bfloat16)
    ones = jnp.ones((lanes, lanes), jnp.bfloat16)
    ranks = disp_rows * slots
    lower = (iota((ranks, ranks), 1) < iota((ranks, ranks), 0)).astype(jnp.float32).astype(jnp.bfloat16)
    for it in range(ITERS):
        found = look((id_col if it == 0 else place_col) == target)
        if it == 1:
            moved_ref[...] = found[slots : slots + 8]
        entry = found[:slots] - 1
        dest = jnp.where(entry >= 0, entry // 32, -1)
        disp = jnp.maximum(entry, 0) % 32
        place = jnp.concatenate(
            [look(id_col == dest[s : s + 1])[slots : slots + 1] for s in range(slots)], axis=0
        )
        owner = place // boxes
        keep = (entry >= 0) & (owner // (hi_count * lo_count) == oct_here) & (owner % lo_count == lo_here)
        away = ((owner // lo_count) % hi_count) ^ hi_here
        shift = jnp.zeros_like(disp)
        for c in range(1, 3):
            shift += (disp >= c * disp_rows).astype(jnp.int32)
        row = disp - shift * disp_rows
        member_of = [keep & (row == g) for g in range(disp_rows)]
        marks = jnp.concatenate(member_of, axis=0).astype(jnp.float32).astype(jnp.bfloat16)
        sums = dot16(marks, ones)
        starts = dot16(lower, sums.astype(jnp.bfloat16))
        ordinal = (starts + dot16(marks, upper)).astype(jnp.int32)
        position = jnp.full((slots, lanes), -1, jnp.int32)
        for g in range(disp_rows):
            position = jnp.where(member_of[g], ordinal[g * slots : (g + 1) * slots], position)
        code = (source * 4 + shift) * dest_rows + away * boxes + place % boxes
        pieces = [((code // 256**n) % 256).astype(jnp.float32) for n in range(3)]
        listed = jnp.zeros((3 * list_rows, LANES), jnp.float32)
        for s in range(slots):
            spot = position[s : s + 1]
            in_row = (spot // LANES == iota((list_rows, lanes), 0)) & (spot >= 0)
            left = jnp.concatenate([jnp.where(in_row, piece[s : s + 1], 0.0) for piece in pieces], axis=0)
            in_lane = (spot % LANES == iota((LANES, lanes), 0)).astype(jnp.float32).astype(jnp.bfloat16)
            listed += lax.dot_general(
                left.astype(jnp.bfloat16), in_lane, (((1,), (1,)), ((), ())), preferred_element_type=jnp.float32
            )
        packed = sum(
            listed[n * list_rows : (n + 1) * list_rows].astype(jnp.int32) * 256**n for n in range(3)
        )
        bound = (starts[ranks - 1 : ranks] + sums[ranks - 1 : ranks]).astype(jnp.int32)
        for g in range(disp_rows):
            bound = jnp.where(lane == g, starts[g * slots : g * slots + 1].astype(jnp.int32), bound)
        list_refs[it][...] = jnp.where(iota(packed.shape, 0) == list_rows - 7, bound, packed)
    load.wait()


def constants_kernel(owner, pot_ref, to_ref, back_ref, two_ref, flip_ref, mats_ref, lift_ref, drop_ref, pot_out, rows_ref):
    order_k = to_ref.shape[0]
    plane = order_k * order_k
    to_high, to_low = spread_columns(to_ref[...])
    back_high, back_low = spread_columns(back_ref[...])
    two = [spread_columns(two_ref[c]) for c in range(2)]
    flip = [spread_columns(flip_ref[c]) for c in range(2)]
    row_high, row_low, lane_high, lane_low = masks(order_k)
    made = []
    for quad in range(4):
        made.append(rows_high(flip[quad // 2][0]) * rows_low(flip[quad % 2][1]))
    for quad in range(4):
        made.append(rows_high(two[quad // 2][0]) * rows_low(two[quad % 2][1]))
    made.append(rows_high(back_high) * rows_low(back_low))
    made.append(rows_high(to_high) * rows_low(to_low))
    made.append(jnp.where(row_high == lane_high, rows_low(to_low), 0.0))
    made.append(jnp.where(row_high == lane_high, rows_low(back_low), 0.0))
    for n, matrix in enumerate(made):
        mats_ref[n, 0], mats_ref[n, 1] = halves(matrix)
    parents, wide = lift_ref.shape
    shape = (order_k, wide)
    lifted = jnp.zeros(shape, jnp.float32)
    for c in range(2):
        hot = (iota(shape, 1) % order_k == iota(shape, 0)) & ((iota(shape, 1) // order_k) % 2 == c)
        lifted += mm(two_ref[c], hot.astype(jnp.float32))
    lifted = jnp.concatenate([lifted] * (parents // order_k), axis=0)
    lift_ref[...] = jnp.where(
        iota(lift_ref.shape, 0) // order_k == iota(lift_ref.shape, 1) // (2 * order_k), lifted, 0.0
    )
    hot = (iota((order_k, parents), 1) % order_k == iota((order_k, parents), 0)).astype(jnp.float32)
    dropped = jnp.concatenate([mm(flip_ref[c], hot) for c in range(2)] * (parents // order_k), axis=0)
    drop_ref[...] = jnp.where(
        iota(drop_ref.shape, 0) // (2 * order_k) == iota(drop_ref.shape, 1) // order_k, dropped, 0.0
    )
    if rows_ref.shape[0] > pot_ref.shape[0]:
        rows_ref[...] = jnp.zeros_like(rows_ref)
    for b in range(pot_ref.shape[0]):
        peer = owner[b]
        for x in range(order_k):
            rows_ref[peer, x : x + 1, :] = pot_ref[b : b + 1, x * plane : (x + 1) * plane]
    pot_out[...] = rows_ref[...].astype(jnp.bfloat16)


def tree_kernel(last, part_count, came_from, *refs):
    parts = refs[:part_count]
    mats_ref, lift_ref, drop_ref = refs[part_count : part_count + 3]
    rest = refs[part_count + 3 :]
    gathered = parts[0][...].astype(jnp.float32)
    for part in parts[1:]:
        gathered = gathered + part[...].astype(jnp.float32)
    boxes, order_k, plane = gathered.shape
    parent_count = boxes // 8

    def matrix(n):
        return mats_ref[n, 0], mats_ref[n, 1]

    summed = None
    for quad in range(4):
        stacked = jnp.concatenate(
            [gathered[8 * p + 4 * c + quad] for p in range(parent_count) for c in range(2)], axis=0
        )
        inner = mm_halves(halves(stacked), matrix(quad))
        summed = inner if summed is None else summed + inner
    own = mm_halves(halves(lift_ref[...]), halves(summed))
    dropped_x = halves(mm_halves(halves(drop_ref[...]), halves(own)))
    dropped = [mm_halves(dropped_x, matrix(4 + quad)) for quad in range(4)]
    fields = []
    for b in range(boxes):
        start = (b // 4) * order_k
        fields.append(gathered[b] - dropped[b % 4][start : start + order_k])
    if last:
        field_ref, parent_ref = rest
        if field_ref.shape[0] > boxes:
            field_ref[...] = jnp.zeros_like(field_ref)
        for b in range(boxes):
            field_ref[came_from[b]] = fields[b].astype(field_ref.dtype)
        for p in range(parent_count):
            for i in range(order_k):
                parent_ref[p : p + 1, i * plane : (i + 1) * plane] = own[p * order_k + i : p * order_k + i + 1]
    else:
        pot_ref, out_ref = rest
        potential = jnp.concatenate([pot_ref[came_from[b]] for b in range(boxes)], axis=0).astype(jnp.float32)
        current = halves(jnp.concatenate(fields, axis=0))
        values = mm_halves(matrix(10), halves(mm_halves(current, matrix(8))))
        product = values * (potential + 0.25 * values * values)
        source = mm_halves(matrix(11), halves(mm_halves(halves(product), matrix(9))))
        out_ref[...] = source.astype(jnp.bfloat16).reshape(out_ref.shape)


def unpack_kernel(owner, field_ref, out_ref):
    order_k, plane = field_ref.shape[1:]
    for b in range(out_ref.shape[0]):
        box = field_ref[owner[b]].astype(jnp.float32)
        for x in range(order_k):
            out_ref[b : b + 1, x * plane : (x + 1) * plane] = box[x : x + 1]


def conv_kernel(dims, packed, *refs):
    term_count, order_k, disp_count, source_count, dest_count = dims
    source_refs = refs[:source_count]
    xl_ref, w_ref = refs[source_count : source_count + 2]
    out_refs = refs[source_count + 2 : source_count + 2 + dest_count]
    pbuf, total, held, held_sems = refs[source_count + 2 + dest_count :]
    plane = order_k * order_k
    list_rows = packed.shape[0] - 7
    half = term_count // 2
    depth = term_count * order_k
    block_boxes = out_refs[0].shape[0]
    dest_rows = dest_count * block_boxes
    loads = [
        pltpu.make_async_copy(ref, held.at[pl.ds(n * block_boxes, block_boxes)], held_sems.at[n])
        for n, ref in enumerate(source_refs)
    ]
    for load in loads:
        load.start()
    total[...] = jnp.zeros_like(total)
    for load in loads:
        load.wait()

    def push_w(ll, j, reg):
        for unit in range(2):
            column = pl.multiple_of(((unit * half + j) * disp_count + ll) * plane, plane)
            pltpu.matmul_push_rhs(w_ref[:, pl.ds(column, plane)], reg, unit)

    def block_body(ll, base, live, slots):
        pl.run_scoped(
            functools.partial(with_accs, ll, base, live, slots),
            *[
                [
                    [pltpu.ACC(unit)((order_k, plane), jnp.float32) for _ in range(slots)]
                    for _ in range(max(2, min(half, 2 * BLOCK // slots)))
                ]
                for unit in range(2)
            ],
        )

    def with_accs(ll, base, live, slots, *accs):
        codes = [packed[(base + t) // LANES, (base + t) % LANES] for t in range(slots)]
        ids = [code // (4 * dest_rows) for code in codes]
        shifts = [(code // dest_rows) % 4 for code in codes]

        stages = len(accs[0])

        def take(j, t):
            for unit in range(2):
                row = (unit * half + j) * order_k + t * depth
                tile = pltpu.matmul_pop(accs[unit][j % stages][t])
                pbuf[row : row + order_k, :] = tile.astype(jnp.bfloat16)

        push_w(ll, 0, 0)
        for j in range(half):
            if j + 1 < half:
                push_w(ll, j + 1, (j + 1) % 2)
            for t in range(slots):
                lhs = held[ids[t]]
                for unit in range(2):
                    pltpu.matmul_acc_lhs(accs[unit][j % stages][t], lhs, j % 2 if t == 0 else None)
                if j + 1 >= stages:
                    take(j + 1 - stages, t)
        for j in range(half - stages + 1, half):
            for t in range(slots):
                take(j, t)

        tiles = GROUP * depth // plane
        groups = slots // GROUP

        def place(g):
            for s in range(GROUP):
                t = g * GROUP + s
                tile = pltpu.matmul_pop(accs[g % 2][0][t])
                dest = jnp.where(t < live, codes[t] % dest_rows, dest_rows)
                total[dest] = total[dest] + tile

        for g in range(groups):
            unit = g % 2
            for q in range(tiles):
                reg = q % 2
                pltpu.matmul_push_rhs(pbuf[pl.ds(g * GROUP * depth + q * plane, plane), :], reg, unit)
                first = True
                for s in range(GROUP):
                    if s * depth < (q + 1) * plane and (s + 1) * depth > q * plane:
                        t = g * GROUP + s
                        pltpu.matmul_acc_lhs(
                            accs[unit][0][t], xl_ref[shifts[t], q + s], reg if first else None
                        )
                        first = False
            if g >= 3:
                place(g - 3)
        for g in range(max(groups - 3, 0), groups):
            place(g)

    def per_disp(ll, carry):
        start, stop = packed[list_rows, ll], packed[list_rows, ll + 1]

        def per_block(blk, inner):
            base = start + blk * BLOCK
            live = jnp.minimum(stop - base, BLOCK)
            lax.switch(
                (live + GROUP - 1) // GROUP - 1,
                [functools.partial(block_body, ll, base, live, GROUP * (c + 1)) for c in range(BLOCK // GROUP)],
            )
            return inner

        lax.fori_loop(0, (stop - start + BLOCK - 1) // BLOCK, per_block, 0)
        return carry

    lax.fori_loop(0, disp_count, per_disp, 0)
    for r, out_ref in enumerate(out_refs):
        out_ref[...] = total[pl.ds(r * block_boxes, block_boxes)].astype(jnp.bfloat16)


def shifted_factors(x_kernels):
    term_count, stacked, order_k = x_kernels.shape
    plane = order_k * order_k
    depth = term_count * order_k
    flat = x_kernels.reshape(term_count, 3, order_k, order_k).transpose(1, 2, 0, 3).reshape(3, order_k, depth)
    padded = jnp.pad(flat, ((0, 0), (0, 0), (plane, plane)))
    parts = {}
    for q in range(GROUP * depth // plane):
        for s in range(GROUP):
            if s * depth < (q + 1) * plane and (s + 1) * depth > q * plane:
                low = plane + q * plane - s * depth
                parts[q + s] = padded[:, :, low : low + plane]
    return jnp.stack([parts[p] for p in range(len(parts))], axis=1)


def convolve(sources, shifted, held_kernels, packed, dest_count, term_count, order_k):
    plane = order_k * order_k
    block_boxes = sources[0].shape[0]
    disp_count = held_kernels.shape[1] // (term_count * plane)
    dims = (term_count, order_k, disp_count, len(sources), dest_count)
    tile = jax.ShapeDtypeStruct((block_boxes, order_k, plane), jnp.bfloat16)
    return pl.pallas_call(
        functools.partial(conv_kernel, dims),
        out_shape=[tile] * dest_count,
        in_specs=[SMEM] + [ANY] * len(sources) + [VMEM, VMEM],
        out_specs=[VMEM] * dest_count,
        scratch_shapes=[
            pltpu.VMEM((BLOCK * term_count * order_k, plane), jnp.bfloat16),
            pltpu.VMEM((dest_count * block_boxes + 1, order_k, plane), jnp.float32),
            pltpu.VMEM((len(sources) * block_boxes, order_k, plane), jnp.bfloat16),
            pltpu.SemaphoreType.DMA((len(sources),)),
        ],
        compiler_params=pltpu.CompilerParams(vmem_limit_bytes=20 * MIB),
        name="convolve",
    )(packed, *sources, shifted, held_kernels)


def flips(count, step):
    return [(i, i ^ step) for i in range(count)]


def gather_sources(source, lo_count):
    near = [source] + [lax.ppermute(source, "lo", flips(lo_count, r)) for r in range(1, lo_count)]
    return near + [lax.ppermute(block, "oct", flips(2, 1)) for block in near]


def shards(
    coefficients,
    potential,
    to_values,
    x_kernels,
    yz_kernels,
    two_scale,
    disp_ids,
    dest_box,
    parent_of,
    child_octant,
):
    box_count, slot_count = disp_ids.shape
    order_k = to_values.shape[0]
    plane = order_k * order_k
    term_count = x_kernels.shape[0]
    disp_rows = yz_kernels.shape[1] // (term_count * plane)
    oct_count, hi_count, lo_count = (lax.axis_size(name) for name in ("oct", "hi", "lo"))
    oct_here, hi_here, lo_here = (lax.axis_index(name) for name in ("oct", "hi", "lo"))
    sub_count = hi_count * lo_count
    devices_all = oct_count * sub_count
    device_here = oct_here * sub_count + hi_here * lo_count + lo_here
    info = jnp.stack([oct_here, hi_here, lo_here, device_here]).astype(jnp.int32)
    flipped = jnp.swapaxes(two_scale, 1, 2)
    back_values = to_values.T
    tile = (box_count, order_k, plane)

    own_place = parent_of * 8 + child_octant
    own_owner = own_place // box_count % sub_count
    words = pl.pallas_call(
        pack_kernel,
        out_shape=jax.ShapeDtypeStruct((devices_all, box_count // 2, LANES), jnp.int32),
        in_specs=[SMEM] + [VMEM] * 3,
        out_specs=VMEM,
        name="pack_tables",
    )(info, disp_ids, dest_box, own_place.reshape(box_count, 1))
    words = lax.all_to_all(words, ("oct", "hi", "lo"), 0, 0, tiled=True)

    source = pl.pallas_call(
        first_kernel,
        out_shape=jax.ShapeDtypeStruct(tile, jnp.bfloat16),
        in_specs=[VMEM] * 4,
        out_specs=VMEM,
        name="first_source",
    )(coefficients, potential, to_values, back_values)

    list_rows = -(-(oct_count * lo_count * box_count * slot_count // LANES + 8) // 8) * 8
    *lists, moved, held_kernels = pl.pallas_call(
        functools.partial(route_kernel, (oct_count, hi_count, lo_count, box_count, slot_count, disp_rows)),
        out_shape=[jax.ShapeDtypeStruct((list_rows, LANES), jnp.int32)] * ITERS
        + [
            jax.ShapeDtypeStruct((8, LANES), jnp.int32),
            pltpu.VMEM(yz_kernels.shape, yz_kernels.dtype),
        ],
        in_specs=[SMEM, VMEM, ANY],
        out_specs=[VMEM] * (ITERS + 2),
        scratch_shapes=[pltpu.SemaphoreType.DMA],
        compiler_params=pltpu.CompilerParams(vmem_limit_bytes=20 * MIB),
        name="route_slots",
    )(info, words, yz_kernels)
    came_from = moved[1, :box_count] // box_count % sub_count
    shifted = shifted_factors(x_kernels)

    for iteration in range(ITERS):
        last = iteration == ITERS - 1
        sources = gather_sources(source, lo_count)
        outs = convolve(sources, shifted, held_kernels, lists[iteration], hi_count, term_count, order_k)
        if not last:
            late, outs = lax.optimization_barrier(((potential, own_owner), outs))
            parents = box_count // 8 * order_k
            *fixed, send_potential = pl.pallas_call(
                constants_kernel,
                out_shape=[
                    jax.ShapeDtypeStruct((12, 2, plane, plane), jnp.bfloat16),
                    jax.ShapeDtypeStruct((parents, 2 * parents), jnp.float32),
                    jax.ShapeDtypeStruct((2 * parents, parents), jnp.float32),
                    jax.ShapeDtypeStruct((sub_count, order_k, plane), jnp.bfloat16),
                ],
                in_specs=[SMEM] + [VMEM] * 5,
                out_specs=[VMEM] * 4,
                scratch_shapes=[pltpu.VMEM((sub_count, order_k, plane), jnp.float32)],
                compiler_params=pltpu.CompilerParams(vmem_limit_bytes=16 * MIB),
                name="make_constants",
            )(late[1], late[0], to_values, back_values, two_scale, flipped)
        parts = [outs[0]] + [lax.ppermute(outs[r], "hi", flips(hi_count, r)) for r in range(1, hi_count)]
        kernel = functools.partial(tree_kernel, last, hi_count)
        if last:
            fields, parents = pl.pallas_call(
                kernel,
                out_shape=[
                    jax.ShapeDtypeStruct((sub_count, order_k, plane), jnp.bfloat16),
                    jax.ShapeDtypeStruct((box_count // 8, order_k * plane), jnp.float32),
                ],
                in_specs=[SMEM] + [VMEM] * (hi_count + 3),
                out_specs=[VMEM] * 2,
                name="last_tree",
            )(came_from, *parts, *fixed)
        else:
            moved_potential = lax.all_to_all(send_potential, ("hi", "lo"), 0, 0, tiled=True)
            source = pl.pallas_call(
                kernel,
                out_shape=jax.ShapeDtypeStruct(tile, jnp.bfloat16),
                in_specs=[SMEM] + [VMEM] * (hi_count + 4),
                out_specs=VMEM,
                name="tree_source",
            )(came_from, *parts, *fixed, moved_potential)
    returned = lax.all_to_all(fields, ("hi", "lo"), 0, 0, tiled=True)
    next_field = pl.pallas_call(
        unpack_kernel,
        out_shape=jax.ShapeDtypeStruct((box_count, order_k * plane), jnp.float32),
        in_specs=[SMEM, VMEM],
        out_specs=VMEM,
        name="unpack_fields",
    )(own_owner, returned)
    return next_field, parents


def solution(mesh):
    oct_count, sub_count = mesh.devices.shape
    lo_count = 4
    split = Mesh(mesh.devices.reshape(oct_count, sub_count // lo_count, lo_count), ("oct", "hi", "lo"))
    rows = ("oct", "hi", "lo")
    placed = (
        P(rows, None),
        P(rows, None),
        P(),
        P(),
        P(),
        P(),
        P(rows, None),
        P(rows, None),
        P(rows),
        P(rows),
    )
    return jax.shard_map(
        shards,
        mesh=split,
        in_specs=placed,
        out_specs=(P(rows, None), P(rows, None)),
        check_vma=False,
    )
```

time: 158 us -> 173 us (1.095)
  local copies, waits for them, and re-layouts: 15.6 us -> 34.2 us
  blocking collectives: 0 us -> 14.9 us
  other arithmetic: 13.7 us -> 1.89 us
  starting transfers between devices: 38.3 us -> 29.2 us
  Pallas kernels: 56.6 us -> 63.1 us
  waiting for transfers between devices: 32.9 us -> 30.3 us
    unnamed x32 -> x55, local copies, waits for them, and re-layouts: 9.41 us -> 32.2 us
    all_to_all x0 -> x1, blocking collectives: none -> 14.9 us  [shards(): returned = lax.all_to_all(fields, ('hi', 'lo'), 0, 0, tiled=True)]
    pallas_call x1 -> x5, Pallas kernels: 3.99 us -> 17 us  [the longest x1 8.34 us: shards(): pl.pallas_call(functools.partial(route_kernel, (oct_count, hi_count, lo_c...]
    reduce_sum x10 -> x0, other arithmetic: 9.93 us -> none  [the longest x2 3.6 us: route(): jnp.sum((full_key[None, :] < full_key[:, None]).astype(jnp.int32), axis=1)]
    all_to_all x3 -> x2, starting transfers between devices: 17.8 us -> 11.1 us  [the longest x1 6.25 us: shards(): words = lax.all_to_all(words, ('oct', 'hi', 'lo'), 0, 0, tiled=True)]
    all_to_all x3 -> x2, waiting for transfers between devices: 10.9 us -> 4.68 us  [the longest x1 4.68 us: shards(): words = lax.all_to_all(words, ('oct', 'hi', 'lo'), 0, 0, tiled=True)]
    pallas_call x2, Pallas kernels: 41 us -> 37.1 us  [convolve(): pl.pallas_call(functools.partial(conv_kernel, dims), out_shape=[tile] * d...]
    gather x5 -> x0, local copies, waits for them, and re-layouts: 2.99 us -> none  [the longest x2 1.29 us: route(): entries = jnp.take(tables, box_ids, axis=0).reshape(-1)]
  transfers between devices with their start and end apart: 23 -> 22, of which waited for: 9 -> 10; matrix products, arithmetic and copies ran while one was open for 14% -> 3% of each run, Pallas kernels for 13% -> 6%
where the time goes in v1:
time: 173 us; the launch traced here: 175 us
  Pallas kernels  63.1 us (36%)
  local copies, waits for them, and re-layouts  34.2 us (20%)
  waiting for transfers between devices  30.3 us (18%)
  starting transfers between devices  29.2 us (17%)
  blocking collectives  14.9 us (9%)
  other arithmetic  1.89 us (1%)
    pallas_call x2, Pallas kernels, convolve(): pl.pallas_call(functools.partial(conv_kernel, dims), out_shape=[tile] * d...  37.1 us
    unnamed x55, local copies, waits for them, and re-layouts  32.2 us
    ppermute x6, waiting for transfers between devices, shards(): lax.ppermute(outs[r], 'hi', flips(hi_count, r))  19.4 us
    all_to_all x1, blocking collectives, shards(): returned = lax.all_to_all(fields, ('hi', 'lo'), 0, 0, tiled=True)  14.9 us
    ppermute x6, starting transfers between devices, shards(): lax.ppermute(outs[r], 'hi', flips(hi_count, r))  8.85 us
    pallas_call x1, Pallas kernels, shards(): pl.pallas_call(functools.partial(route_kernel, (oct_count, hi_count, lo_c...  8.34 us
    ppermute x6, starting transfers between devices, gather_sources(): lax.ppermute(source, 'lo', flips(lo_count, r))  7.57 us
    all_to_all x1, starting transfers between devices, shards(): words = lax.all_to_all(words, ('oct', 'hi', 'lo'), 0, 0, tiled=True)  6.25 us
  transfers between devices with their start and end apart: 22, of which 10 were waited for; matrix products, arithmetic and copies ran while one was open for 3% of the time, Pallas kernels for 6%

profile of v1, /device:TPU:0, one launch (start us, length us, event | category | flops | bytes accessed | tf_op | source)
XLA Modules:
  0.0 174.6 jit_solution(4370015652098009720)
XLA Ops:
  0.6 1.4 copy.24
  2.0 3.1 %first_source.1.refs_0_ = bf16[16,16,256]{2,1,0:T(8,128)(2,1)} custom-call(f32[16,4096]{1,0:T(8,128)} %coef_ref.1, f32[16,4096]{1,0:T(8,128)} %pot_ref.2, f32[16,16]{1,0:T(8,128)} %to_ref.3, f32[16,16]{1,0:T(8,128)} %bitcast.63), custom_call_target="tpu_custom_call" | custom-call | tf_op jit(solution)/shard_map/first_source/pallas_call | solution.py:485
  5.1 0.5 collective-permute-start.3
  5.6 3.4 %collective-permute-start.2 = (bf16[16,16,256]{2,1,0:T(8,128)(2,1)}, bf16[16,16,256]{2,1,0:T(8,128)(2,1)S(1)}, u32[]{:S(2)}, u32[]{:S(2)}) collective-permute-start(bf16[16,16,256]{2,1,0:T(8,128)(2,1)} %first_source.1.refs_0_), channel_id=1, source_target_pairs={{0,3},{1,2},{2,1},{3,0},{4,7},{5,6},{6,5},{7,4},{8,11},{9,10},{10,... | collective-permute-start | bytes 393224 | tf_op jit(solution)/shard_map/ppermute | solution.py:443
  9.0 0.5 collective-permute-start.1
  9.7 0.7 fusion.16
  10.4 0.7 copy.23.place_ref
  11.0 0.6 pad_add_fusion.info
  11.7 1.6 pack_tables.1
  13.3 6.3 %all-to-all-start = ((s32[32,8,128]{2,1,0:T(8,128)}), s32[32,8,128]{2,1,0:T(8,128)S(1)}, u32[]{:S(2)}, u32[]{:S(2)}) async-start(s32[32,8,128]{2,1,0:T(8,128)} %pack_tables.1), calls=%async_computation | async-start | bytes 262144 | tf_op jit(solution)/shard_map/all_to_all | solution.py:483
  19.6 1.1 copy.33
  21.1 0.8 copy.32
  22.8 4.7 %all-to-all-done.words_ref = s32[32,8,128]{2,1,0:T(8,128)S(1)} async-done(((s32[32,8,128]{2,1,0:T(8,128)}), s32[32,8,128]{2,1,0:T(8,128)S(1)}, u32[]{:S(2)}, u32[]{:S(2)}) %all-to-all-start) | async-done | bytes 131104 | tf_op jit(solution)/shard_map/all_to_all | solution.py:483
  27.5 0.7 copy-done.14
  28.1 8.3 %route_slots.1 = (s32[24,128]{1,0:T(8,128)S(1)}, s32[24,128]{1,0:T(8,128)S(1)}, s32[8,128]{1,0:T(8,128)S(1)}, bf16[256,46080]{1,0:T(8,128)(2,1)S(1)}) custom-call(s32[4]{0:T(128)S(1)} %copy-done.14, s32[32,8,128]{2,1,0:T(8,128)S(1)} %all-to-all-done.words_ref, bf16[256,46080]{1,0:T(8,128)(2,1)} %w_hbm.1), custom_call_target="tpu_custom_call" | custom-call | tf_op jit(solution)/shard_map/route_slots/pallas_call | solution.py:494
  36.5 7.8 %copy-done = bf16[256,46080]{1,0:T(8,128)(2,1)} copy-done((bf16[256,46080]{1,0:T(8,128)(2,1)}, bf16[256,46080]{1,0:T(8,128)(2,1)S(1)}, u32[]{:S(2)}) %copy-start) | copy-done | bytes 23592984
  44.3 7.7 %copy-done.1 = bf16[256,46080]{1,0:T(8,128)(2,1)S(1)} copy-done((bf16[256,46080]{1,0:T(8,128)(2,1)S(1)}, bf16[256,46080]{1,0:T(8,128)(2,1)}, u32[]{:S(2)}) %copy-start.1) | copy-done | bytes 23592984
  52.0 17.7 %convolve.2 = (bf16[16,16,256]{2,1,0:T(8,128)(2,1)S(1)}, bf16[16,16,256]{2,1,0:T(8,128)(2,1)S(1)}, bf16[16,16,256]{2,1,0:T(8,128)(2,1)S(1)}, bf16[16,16,256]{2,1,0:T(8,128)(2,1)S(1)}) custom-call(s32[24,128]{1,0:T(8,128)S(1)} %get-tuple-element.28.packed, bf16[16,16,256]{2,1,0:T(8,128)(2,1)S(1)} %copy-done.6, ...), custom_call_target="tpu_custom_call" | custom-call | tf_op jit(solution)/shard_map/convolve/pallas_call | solution.py:422
  69.8 2.2 %make_constants.1 = (bf16[12,2,256,256]{3,2,1,0:T(8,128)(2,1)S(1)}, f32[32,64]{1,0:T(8,128)S(1)}, f32[64,32]{1,0:T(8,128)S(1)}, bf16[16,16,256]{2,1,0:T(8,128)(2,1)}) custom-call(s32[16]{0:T(128)S(1)} %get-tuple-element.38.owner, f32[16,4096]{1,0:T(8,128)S(1)} %copy-done.4, f32[16,16]{1,0:T(8,128)S(1)} %copy-done.10, f32[16,16]{1,0:T(8,128)S(1)} %bitcast.64, ...), custom_call_target="tpu_custom_call" | custom-call | tf_op jit(solution)/shard_map/make_constants/pallas_call | solution.py:517
  72.0 1.7 copy-done.3
  73.7 0.6 copy-done.7
  74.3 0.6 copy-done.12
  74.9 4.9 %all-to-all-start.1 = ((bf16[16,16,256]{2,1,0:T(8,128)(2,1)}), bf16[16,16,256]{2,1,0:T(8,128)(2,1)S(1)}, u32[]{:S(2)}, u32[]{:S(2)}) async-start(bf16[16,16,256]{2,1,0:T(8,128)(2,1)} %get-tuple-element.43), calls=%async_computation.1 | async-start | bytes 262144 | tf_op jit(solution)/shard_map/all_to_all | solution.py:545
  79.8 1.9 %collective-permute-start.7 = (bf16[16,16,256]{2,1,0:T(8,128)(2,1)S(1)}, bf16[16,16,256]{2,1,0:T(8,128)(2,1)S(1)}, u32[]{:S(2)}, u32[]{:S(2)}) collective-permute-start(bf16[16,16,256]{2,1,0:T(8,128)(2,1)S(1)} %get-tuple-element.35), channel_id=1, source_target_pairs={{0,4},{4,0},{8,12},{12,8},{1,5},{5,1},{9,13},{13,9},{2,6},{6,2},{1... | collective-permute-start | bytes 393224 | tf_op jit(solution)/shard_map/ppermute | solution.py:531
  81.7 2.4 %collective-permute-start.8 = (bf16[16,16,256]{2,1,0:T(8,128)(2,1)S(1)}, bf16[16,16,256]{2,1,0:T(8,128)(2,1)S(1)}, u32[]{:S(2)}, u32[]{:S(2)}) collective-permute-start(bf16[16,16,256]{2,1,0:T(8,128)(2,1)S(1)} %get-tuple-element.36), channel_id=1, source_target_pairs={{0,8},{4,12},{8,0},{12,4},{1,9},{5,13},{9,1},{13,5},{2,10},{6,14},... | collective-permute-start | bytes 393224 | tf_op jit(solution)/shard_map/ppermute | solution.py:531
  84.3 0.6 and_select_fusion.came_from
  84.8 5.7 %collective-permute-done.7.refs_1_ = bf16[16,16,256]{2,1,0:T(8,128)(2,1)S(1)} collective-permute-done((bf16[16,16,256]{2,1,0:T(8,128)(2,1)S(1)}, bf16[16,16,256]{2,1,0:T(8,128)(2,1)S(1)}, u32[]{:S(2)}, u32[]{:S(2)}) %collective-permute-start.7) | collective-permute-done | bytes 131104 | tf_op jit(solution)/shard_map/ppermute | solution.py:531
  90.5 4.9 %collective-permute-done.8.refs_2_ = bf16[16,16,256]{2,1,0:T(8,128)(2,1)S(1)} collective-permute-done((bf16[16,16,256]{2,1,0:T(8,128)(2,1)S(1)}, bf16[16,16,256]{2,1,0:T(8,128)(2,1)S(1)}, u32[]{:S(2)}, u32[]{:S(2)}) %collective-permute-start.8) | collective-permute-done | bytes 131104 | tf_op jit(solution)/shard_map/ppermute | solution.py:531
  95.4 0.6 copy-done.19
  96.1 5.1 %tree_source.1.refs_0_ = bf16[16,16,256]{2,1,0:T(8,128)(2,1)} custom-call(s32[16]{0:T(128)} %and_select_fusion.came_from, bf16[16,16,256]{2,1,0:T(8,128)(2,1)} %copy-done.8, bf16[16,16,256]{2,1,0:T(8,128)(2,1)} %copy-done.17, bf16[16,16,256]{2,1,0:T(8,128)(2,1)} %copy-done.19, bf16[16,16,256]{2,1,0:T(8,128)(2,1)} %copy-done.21, ...), custom_call_target="tpu_custom_call" | custom-call | tf_op jit(solution)/shard_map/tree_source/pallas_call | solution.py:546
  101.3 2.4 %collective-permute-start.12 = (bf16[16,16,256]{2,1,0:T(8,128)(2,1)}, bf16[16,16,256]{2,1,0:T(8,128)(2,1)S(1)}, u32[]{:S(2)}, u32[]{:S(2)}) collective-permute-start(bf16[16,16,256]{2,1,0:T(8,128)(2,1)} %tree_source.1.refs_0_), channel_id=1, source_target_pairs={{0,3},{1,2},{2,1},{3,0},{4,7},{5,6},{6,5},{7,4},{8,11},{9,10},{10,... | collective-permute-start | bytes 393224 | tf_op jit(solution)/shard_map/ppermute | solution.py:443
  103.6 0.6 collective-permute-start.11
  104.2 0.6 collective-permute-start.10
  104.8 3.3 %collective-permute-done.12.refs_3_ = bf16[16,16,256]{2,1,0:T(8,128)(2,1)S(1)} collective-permute-done((bf16[16,16,256]{2,1,0:T(8,128)(2,1)}, bf16[16,16,256]{2,1,0:T(8,128)(2,1)S(1)}, u32[]{:S(2)}, u32[]{:S(2)}) %collective-permute-start.12) | collective-permute-done | bytes 131104 | tf_op jit(solution)/shard_map/ppermute | solution.py:443
  108.1 1.9 %collective-permute-done.11.refs_2_ = bf16[16,16,256]{2,1,0:T(8,128)(2,1)S(1)} collective-permute-done((bf16[16,16,256]{2,1,0:T(8,128)(2,1)}, bf16[16,16,256]{2,1,0:T(8,128)(2,1)S(1)}, u32[]{:S(2)}, u32[]{:S(2)}) %collective-permute-start.11) | collective-permute-done | bytes 131104 | tf_op jit(solution)/shard_map/ppermute | solution.py:443
  110.0 0.5 collective-permute-start.14
  110.4 0.8 collective-permute-done.15.refs_6_
  111.5 7.7 %copy-done.2 = bf16[256,46080]{1,0:T(8,128)(2,1)S(1)} copy-done((bf16[256,46080]{1,0:T(8,128)(2,1)S(1)}, bf16[256,46080]{1,0:T(8,128)(2,1)}, u32[]{:S(2)}) %copy-start.2) | copy-done | bytes 23592984
  119.2 0.9 copy-done.5
  120.1 19.4 %convolve.3 = (bf16[16,16,256]{2,1,0:T(8,128)(2,1)S(1)}, bf16[16,16,256]{2,1,0:T(8,128)(2,1)S(1)}, bf16[16,16,256]{2,1,0:T(8,128)(2,1)S(1)}, bf16[16,16,256]{2,1,0:T(8,128)(2,1)S(1)}) custom-call(s32[24,128]{1,0:T(8,128)S(1)} %get-tuple-element.27.packed, bf16[16,16,256]{2,1,0:T(8,128)(2,1)S(1)} %copy-done.5, ...), custom_call_target="tpu_custom_call" | custom-call | tf_op jit(solution)/shard_map/convolve/pallas_call | solution.py:422
  139.5 0.6 copy-done.9
  140.6 4.0 %collective-permute-start.19 = (bf16[16,16,256]{2,1,0:T(8,128)(2,1)S(1)}, bf16[16,16,256]{2,1,0:T(8,128)(2,1)S(1)}, u32[]{:S(2)}, u32[]{:S(2)}) collective-permute-start(bf16[16,16,256]{2,1,0:T(8,128)(2,1)S(1)} %get-tuple-element.47), channel_id=1, source_target_pairs={{0,12},{4,8},{8,4},{12,0},{1,13},{5,9},{9,5},{13,1},{2,14},{6,10},... | collective-permute-start | bytes 393224 | tf_op jit(solution)/shard_map/ppermute | solution.py:531
  144.6 2.6 %collective-permute-done.17.refs_1_ = bf16[16,16,256]{2,1,0:T(8,128)(2,1)S(1)} collective-permute-done((bf16[16,16,256]{2,1,0:T(8,128)(2,1)S(1)}, bf16[16,16,256]{2,1,0:T(8,128)(2,1)S(1)}, u32[]{:S(2)}, u32[]{:S(2)}) %collective-permute-start.17) | collective-permute-done | bytes 131104 | tf_op jit(solution)/shard_map/ppermute | solution.py:531
  147.2 6.2 %collective-permute-done.18.refs_2_ = bf16[16,16,256]{2,1,0:T(8,128)(2,1)S(1)} collective-permute-done((bf16[16,16,256]{2,1,0:T(8,128)(2,1)S(1)}, bf16[16,16,256]{2,1,0:T(8,128)(2,1)S(1)}, u32[]{:S(2)}, u32[]{:S(2)}) %collective-permute-start.18) | collective-permute-done | bytes 131104 | tf_op jit(solution)/shard_map/ppermute | solution.py:531
  153.4 0.6 copy-done.20
  154.1 3.9 %last_tree.1 = (bf16[16,16,256]{2,1,0:T(8,128)(2,1)}, f32[2,4096]{1,0:T(2,128)}) custom-call(s32[16]{0:T(128)} %and_select_fusion.came_from, bf16[16,16,256]{2,1,0:T(8,128)(2,1)} %copy-done.9, bf16[16,16,256]{2,1,0:T(8,128)(2,1)} %copy-done.18, bf16[16,16,256]{2,1,0:T(8,128)(2,1)} %copy-done.20, bf16[16,16,256]{2,1,0:T(8,128)(2,1)} %copy-done.22, ...), custom_call_target="tpu_custom_call" | custom-call | tf_op jit(solution)/shard_map/last_tree/pallas_call | solution.py:534
  157.9 14.9 %all_to_all.15.field_ref = bf16[16,16,256]{2,1,0:T(8,128)(2,1)} all-to-all(bf16[16,16,256]{2,1,0:T(8,128)(2,1)} %get-tuple-element.48), channel_id=1, replica_groups=mesh['oct'=2,'hi'=4,'lo'=4] {'hi','lo'}, dimensions={0} | all-to-all | bytes 262144 | tf_op jit(solution)/shard_map/all_to_all | solution.py:553
  172.9 1.7 unpack_fields.1
  (68 shorter events, 2.5 us)
Async XLA Ops:
  5.1 39.2 %copy-start.6 = (bf16[16,16,256]{2,1,0:T(8,128)(2,1)S(1)}, bf16[16,16,256]{2,1,0:T(8,128)(2,1)}, u32[]{:S(2)}) copy-start(bf16[16,16,256]{2,1,0:T(8,128)(2,1)} %first_source.1.refs_0_) | copy-start | bytes 393220
  5.1 39.2 %collective-permute-start.3 = (bf16[16,16,256]{2,1,0:T(8,128)(2,1)}, bf16[16,16,256]{2,1,0:T(8,128)(2,1)S(1)}, u32[]{:S(2)}, u32[]{:S(2)}) collective-permute-start(bf16[16,16,256]{2,1,0:T(8,128)(2,1)} %first_source.1.refs_0_), channel_id=1, source_target_pairs={{0,16},{16,0},{1,17},{17,1},{2,18},{18,2},{3,19},{19,3},{4,20},{20... | collective-permute-start | bytes 393224 | tf_op jit(solution)/shard_map/ppermute | solution.py:444
  5.6 16.3 %collective-permute-start.2 = (bf16[16,16,256]{2,1,0:T(8,128)(2,1)}, bf16[16,16,256]{2,1,0:T(8,128)(2,1)S(1)}, u32[]{:S(2)}, u32[]{:S(2)}) collective-permute-start(bf16[16,16,256]{2,1,0:T(8,128)(2,1)} %first_source.1.refs_0_), channel_id=1, source_target_pairs={{0,3},{1,2},{2,1},{3,0},{4,7},{5,6},{6,5},{7,4},{8,11},{9,10},{10,... | collective-permute-start | bytes 393224 | tf_op jit(solution)/shard_map/ppermute | solution.py:443
  9.0 13.1 %collective-permute-start.1 = (bf16[16,16,256]{2,1,0:T(8,128)(2,1)}, bf16[16,16,256]{2,1,0:T(8,128)(2,1)S(1)}, u32[]{:S(2)}, u32[]{:S(2)}) collective-permute-start(bf16[16,16,256]{2,1,0:T(8,128)(2,1)} %first_source.1.refs_0_), channel_id=1, source_target_pairs={{0,2},{1,3},{2,0},{3,1},{4,6},{5,7},{6,4},{7,5},{8,10},{9,11},{10,... | collective-permute-start | bytes 393224 | tf_op jit(solution)/shard_map/ppermute | solution.py:443
  9.5 12.9 %collective-permute-start = (bf16[16,16,256]{2,1,0:T(8,128)(2,1)}, bf16[16,16,256]{2,1,0:T(8,128)(2,1)S(1)}, u32[]{:S(2)}, u32[]{:S(2)}) collective-permute-start(bf16[16,16,256]{2,1,0:T(8,128)(2,1)} %first_source.1.refs_0_), channel_id=1, source_target_pairs={{0,1},{1,0},{2,3},{3,2},{4,5},{5,4},{6,7},{7,6},{8,9},{9,8},{10,11... | collective-permute-start | bytes 393224 | tf_op jit(solution)/shard_map/ppermute | solution.py:443
  10.4 59.4 %copy-start.15 = (s32[16]{0:T(128)}, s32[16]{0:T(128)S(1)}, u32[]{:S(2)}) copy-start(s32[16]{0:T(128)S(1)} %get-tuple-element.38.owner) | copy-start | bytes 196
  13.3 14.2 %all-to-all-start = ((s32[32,8,128]{2,1,0:T(8,128)}), s32[32,8,128]{2,1,0:T(8,128)S(1)}, u32[]{:S(2)}, u32[]{:S(2)}) async-start(s32[32,8,128]{2,1,0:T(8,128)} %pack_tables.1), calls=%async_computation | async-start | bytes 262144 | tf_op jit(solution)/shard_map/all_to_all | solution.py:483
  21.9 22.4 %collective-permute-start.6 = (bf16[16,16,256]{2,1,0:T(8,128)(2,1)S(1)}, bf16[16,16,256]{2,1,0:T(8,128)(2,1)S(1)}, u32[]{:S(2)}, u32[]{:S(2)}) collective-permute-start(bf16[16,16,256]{2,1,0:T(8,128)(2,1)S(1)} %collective-permute-done.2.refs_3_), channel_id=1, source_target_pairs={{0,16},{16,0},{1,17},{17,1},{2,18},{18,2},{3,19},{19,3},{4,20},{20... | collective-permute-start | bytes 393224 | tf_op jit(solution)/shard_map/ppermute | solution.py:444
  22.2 22.1 %collective-permute-start.5 = (bf16[16,16,256]{2,1,0:T(8,128)(2,1)S(1)}, bf16[16,16,256]{2,1,0:T(8,128)(2,1)S(1)}, u32[]{:S(2)}, u32[]{:S(2)}) collective-permute-start(bf16[16,16,256]{2,1,0:T(8,128)(2,1)S(1)} %collective-permute-done.1.refs_2_), channel_id=1, source_target_pairs={{0,16},{16,0},{1,17},{17,1},{2,18},{18,2},{3,19},{19,3},{4,20},{20... | collective-permute-start | bytes 393224 | tf_op jit(solution)/shard_map/ppermute | solution.py:444
  22.4 21.9 %collective-permute-start.4 = (bf16[16,16,256]{2,1,0:T(8,128)(2,1)S(1)}, bf16[16,16,256]{2,1,0:T(8,128)(2,1)S(1)}, u32[]{:S(2)}, u32[]{:S(2)}) collective-permute-start(bf16[16,16,256]{2,1,0:T(8,128)(2,1)S(1)} %collective-permute-done.refs_1_), channel_id=1, source_target_pairs={{0,16},{16,0},{1,17},{17,1},{2,18},{18,2},{3,19},{19,3},{4,20},{20... | collective-permute-start | bytes 393224 | tf_op jit(solution)/shard_map/ppermute | solution.py:444
  22.8 47.0 %copy-start.4 = (f32[16,4096]{1,0:T(8,128)S(1)}, f32[16,4096]{1,0:T(8,128)}, u32[]{:S(2)}) copy-start(f32[16,4096]{1,0:T(8,128)} %pot_ref.2) | copy-start | bytes 786436
  22.8 47.0 %copy-start.10 = (f32[16,16]{1,0:T(8,128)S(1)}, f32[16,16]{1,0:T(8,128)}, u32[]{:S(2)}) copy-start(f32[16,16]{1,0:T(8,128)} %to_ref.3) | copy-start | bytes 3076
  22.8 47.0 %copy-start.11 = (f32[16,16]{0,1:T(8,128)S(1)}, f32[16,16]{0,1:T(8,128)}, u32[]{:S(2)}) copy-start(f32[16,16]{0,1:T(8,128)} %copy.24) | copy-start | bytes 3076
  22.8 47.0 %copy-start.13 = (f32[2,16,16]{2,1,0:T(8,128)S(1)}, f32[2,16,16]{2,1,0:T(8,128)}, u32[]{:S(2)}) copy-start(f32[2,16,16]{2,1,0:T(8,128)} %two_ref.1) | copy-start | bytes 6148
  27.5 0.7 copy-start.14
  36.5 7.8 %copy-start = (bf16[256,46080]{1,0:T(8,128)(2,1)}, bf16[256,46080]{1,0:T(8,128)(2,1)S(1)}, u32[]{:S(2)}) copy-start(bf16[256,46080]{1,0:T(8,128)(2,1)S(1)} %get-tuple-element.29.refs_9_) | copy-start | bytes 70778880
  44.3 7.7 %copy-start.1 = (bf16[256,46080]{1,0:T(8,128)(2,1)S(1)}, bf16[256,46080]{1,0:T(8,128)(2,1)}, u32[]{:S(2)}) copy-start(bf16[256,46080]{1,0:T(8,128)(2,1)} %copy-done) | copy-start | bytes 70778880
  69.7 2.3 %copy-start.8 = (bf16[16,16,256]{2,1,0:T(8,128)(2,1)}, bf16[16,16,256]{2,1,0:T(8,128)(2,1)S(1)}, u32[]{:S(2)}) copy-start(bf16[16,16,256]{2,1,0:T(8,128)(2,1)S(1)} %get-tuple-element.34.refs_0_) | copy-start | bytes 393220
  72.0 1.7 copy-start.3
  73.7 0.6 copy-start.7
  74.3 0.6 copy-start.12
  74.9 20.5 %all-to-all-start.1 = ((bf16[16,16,256]{2,1,0:T(8,128)(2,1)}), bf16[16,16,256]{2,1,0:T(8,128)(2,1)S(1)}, u32[]{:S(2)}, u32[]{:S(2)}) async-start(bf16[16,16,256]{2,1,0:T(8,128)(2,1)} %get-tuple-element.43), calls=%async_computation.1 | async-start | bytes 262144 | tf_op jit(solution)/shard_map/all_to_all | solution.py:545
  79.8 10.7 %collective-permute-start.7 = (bf16[16,16,256]{2,1,0:T(8,128)(2,1)S(1)}, bf16[16,16,256]{2,1,0:T(8,128)(2,1)S(1)}, u32[]{:S(2)}, u32[]{:S(2)}) collective-permute-start(bf16[16,16,256]{2,1,0:T(8,128)(2,1)S(1)} %get-tuple-element.35), channel_id=1, source_target_pairs={{0,4},{4,0},{8,12},{12,8},{1,5},{5,1},{9,13},{13,9},{2,6},{6,2},{1... | collective-permute-start | bytes 393224 | tf_op jit(solution)/shard_map/ppermute | solution.py:531
  81.7 13.7 %collective-permute-start.8 = (bf16[16,16,256]{2,1,0:T(8,128)(2,1)S(1)}, bf16[16,16,256]{2,1,0:T(8,128)(2,1)S(1)}, u32[]{:S(2)}, u32[]{:S(2)}) collective-permute-start(bf16[16,16,256]{2,1,0:T(8,128)(2,1)S(1)} %get-tuple-element.36), channel_id=1, source_target_pairs={{0,8},{4,12},{8,0},{12,4},{1,9},{5,13},{9,1},{13,5},{2,10},{6,14},... | collective-permute-start | bytes 393224 | tf_op jit(solution)/shard_map/ppermute | solution.py:531
  84.1 11.3 %collective-permute-start.9 = (bf16[16,16,256]{2,1,0:T(8,128)(2,1)S(1)}, bf16[16,16,256]{2,1,0:T(8,128)(2,1)S(1)}, u32[]{:S(2)}, u32[]{:S(2)}) collective-permute-start(bf16[16,16,256]{2,1,0:T(8,128)(2,1)S(1)} %get-tuple-element.37), channel_id=1, source_target_pairs={{0,12},{4,8},{8,4},{12,0},{1,13},{5,9},{9,5},{13,1},{2,14},{6,10},... | collective-permute-start | bytes 393224 | tf_op jit(solution)/shard_map/ppermute | solution.py:531
  90.5 4.9 %copy-start.17 = (bf16[16,16,256]{2,1,0:T(8,128)(2,1)}, bf16[16,16,256]{2,1,0:T(8,128)(2,1)S(1)}, u32[]{:S(2)}) copy-start(bf16[16,16,256]{2,1,0:T(8,128)(2,1)S(1)} %collective-permute-done.7.refs_1_) | copy-start | bytes 393220
  95.4 0.7 copy-start.19
  95.4 0.7 copy-start.21
  95.4 0.7 copy-start.16
  101.3 6.8 %collective-permute-start.12 = (bf16[16,16,256]{2,1,0:T(8,128)(2,1)}, bf16[16,16,256]{2,1,0:T(8,128)(2,1)S(1)}, u32[]{:S(2)}, u32[]{:S(2)}) collective-permute-start(bf16[16,16,256]{2,1,0:T(8,128)(2,1)} %tree_source.1.refs_0_), channel_id=1, source_target_pairs={{0,3},{1,2},{2,1},{3,0},{4,7},{5,6},{6,5},{7,4},{8,11},{9,10},{10,... | collective-permute-start | bytes 393224 | tf_op jit(solution)/shard_map/ppermute | solution.py:443
  103.6 6.3 %collective-permute-start.11 = (bf16[16,16,256]{2,1,0:T(8,128)(2,1)}, bf16[16,16,256]{2,1,0:T(8,128)(2,1)S(1)}, u32[]{:S(2)}, u32[]{:S(2)}) collective-permute-start(bf16[16,16,256]{2,1,0:T(8,128)(2,1)} %tree_source.1.refs_0_), channel_id=1, source_target_pairs={{0,2},{1,3},{2,0},{3,1},{4,6},{5,7},{6,4},{7,5},{8,10},{9,11},{10,... | collective-permute-start | bytes 393224 | tf_op jit(solution)/shard_map/ppermute | solution.py:443
  104.2 5.8 %collective-permute-start.10 = (bf16[16,16,256]{2,1,0:T(8,128)(2,1)}, bf16[16,16,256]{2,1,0:T(8,128)(2,1)S(1)}, u32[]{:S(2)}, u32[]{:S(2)}) collective-permute-start(bf16[16,16,256]{2,1,0:T(8,128)(2,1)} %tree_source.1.refs_0_), channel_id=1, source_target_pairs={{0,1},{1,0},{2,3},{3,2},{4,5},{5,4},{6,7},{7,6},{8,9},{9,8},{10,11... | collective-permute-start | bytes 393224 | tf_op jit(solution)/shard_map/ppermute | solution.py:443
  104.8 5.7 %collective-permute-start.13 = (bf16[16,16,256]{2,1,0:T(8,128)(2,1)}, bf16[16,16,256]{2,1,0:T(8,128)(2,1)S(1)}, u32[]{:S(2)}, u32[]{:S(2)}) collective-permute-start(bf16[16,16,256]{2,1,0:T(8,128)(2,1)} %tree_source.1.refs_0_), channel_id=1, source_target_pairs={{0,16},{16,0},{1,17},{17,1},{2,18},{18,2},{3,19},{19,3},{4,20},{20... | collective-permute-start | bytes 393224 | tf_op jit(solution)/shard_map/ppermute | solution.py:444
  108.1 2.4 %collective-permute-start.16 = (bf16[16,16,256]{2,1,0:T(8,128)(2,1)S(1)}, bf16[16,16,256]{2,1,0:T(8,128)(2,1)S(1)}, u32[]{:S(2)}, u32[]{:S(2)}) collective-permute-start(bf16[16,16,256]{2,1,0:T(8,128)(2,1)S(1)} %collective-permute-done.12.refs_3_), channel_id=1, source_target_pairs={{0,16},{16,0},{1,17},{17,1},{2,18},{18,2},{3,19},{19,3},{4,20},{20... | collective-permute-start | bytes 393224 | tf_op jit(solution)/shard_map/ppermute | solution.py:444
  109.9 1.3 collective-permute-start.15
  110.0 1.5 collective-permute-start.14
  111.5 7.7 %copy-start.2 = (bf16[256,46080]{1,0:T(8,128)(2,1)S(1)}, bf16[256,46080]{1,0:T(8,128)(2,1)}, u32[]{:S(2)}) copy-start(bf16[256,46080]{1,0:T(8,128)(2,1)} %copy-done) | copy-start | bytes 70778880
  119.2 0.9 copy-start.5
  139.5 0.7 copy-start.9
  140.2 7.0 %collective-permute-start.17 = (bf16[16,16,256]{2,1,0:T(8,128)(2,1)S(1)}, bf16[16,16,256]{2,1,0:T(8,128)(2,1)S(1)}, u32[]{:S(2)}, u32[]{:S(2)}) collective-permute-start(bf16[16,16,256]{2,1,0:T(8,128)(2,1)S(1)} %get-tuple-element.45), channel_id=1, source_target_pairs={{0,4},{4,0},{8,12},{12,8},{1,5},{5,1},{9,13},{13,9},{2,6},{6,2},{1... | collective-permute-start | bytes 393224 | tf_op jit(solution)/shard_map/ppermute | solution.py:531
  140.6 12.8 %collective-permute-start.18 = (bf16[16,16,256]{2,1,0:T(8,128)(2,1)S(1)}, bf16[16,16,256]{2,1,0:T(8,128)(2,1)S(1)}, u32[]{:S(2)}, u32[]{:S(2)}) collective-permute-start(bf16[16,16,256]{2,1,0:T(8,128)(2,1)S(1)} %get-tuple-element.46), channel_id=1, source_target_pairs={{0,8},{4,12},{8,0},{12,4},{1,9},{5,13},{9,1},{13,5},{2,10},{6,14},... | collective-permute-start | bytes 393224 | tf_op jit(solution)/shard_map/ppermute | solution.py:531
  140.6 12.8 %collective-permute-start.19 = (bf16[16,16,256]{2,1,0:T(8,128)(2,1)S(1)}, bf16[16,16,256]{2,1,0:T(8,128)(2,1)S(1)}, u32[]{:S(2)}, u32[]{:S(2)}) collective-permute-start(bf16[16,16,256]{2,1,0:T(8,128)(2,1)S(1)} %get-tuple-element.47), channel_id=1, source_target_pairs={{0,12},{4,8},{8,4},{12,0},{1,13},{5,9},{9,5},{13,1},{2,14},{6,10},... | collective-permute-start | bytes 393224 | tf_op jit(solution)/shard_map/ppermute | solution.py:531
  147.2 6.2 %copy-start.18 = (bf16[16,16,256]{2,1,0:T(8,128)(2,1)}, bf16[16,16,256]{2,1,0:T(8,128)(2,1)S(1)}, u32[]{:S(2)}) copy-start(bf16[16,16,256]{2,1,0:T(8,128)(2,1)S(1)} %collective-permute-done.17.refs_1_) | copy-start | bytes 393220
  153.4 0.6 copy-start.20
  153.4 0.7 copy-start.22

commit v2 on v1

--- a/solution.py
+++ b/solution.py
@@ -51,12 +51,14 @@
     return jnp.broadcast_to(matrix[None, :, :], (order_k, order_k, width)).reshape(order_k * order_k, width)
 
 
-def spread_columns(matrix):
+def spread_columns(matrix, flip=False):
     order_k = matrix.shape[0]
     shape = (order_k, order_k * order_k)
     slot, lane = iota(shape, 0), iota(shape, 1)
     high = (lane // order_k == slot).astype(jnp.float32)
     low = (lane % order_k == slot).astype(jnp.float32)
+    if flip:
+        matrix = matrix.T
     return mm(matrix, high), mm(matrix, low)
 
 
@@ -66,7 +68,7 @@
     return row // order_k, row % order_k, lane // order_k, lane % order_k
 
 
-def pack_kernel(info, disp_ref, dest_ref, place_ref, out_ref):
+def pack_kernel(parent_of, octant, disp_ref, dest_ref, out_ref):
     boxes, slots = disp_ref.shape
     half = boxes // 2
     dest = dest_ref[...]
@@ -80,20 +82,18 @@
         start = h * (LANES // 2)
         words += mm(entry[h * half : (h + 1) * half], (lane == slot + start).astype(jnp.float32))
     words = words.astype(jnp.int32)
-    for h in range(2):
-        start = h * (LANES // 2)
-        place = place_ref[h * half : (h + 1) * half, :]
-        words = jnp.where(lane_out == start + slots, place, words)
-        words = jnp.where(lane_out == start + slots + 1, info[3] * boxes + h * half + row_out, words)
+    for b in range(boxes):
+        here = (row_out == b % half) & (lane_out == b // half * (LANES // 2) + slots)
+        words = jnp.where(here, parent_of[b] * 8 + octant[b], words)
     for d in range(out_ref.shape[0]):
         out_ref[d] = words
 
 
-def first_kernel(coef_ref, pot_ref, to_ref, back_ref, out_ref):
+def first_kernel(parent_of, coef_ref, pot_ref, to_ref, out_ref, pot_out, rows_ref):
     order_k = to_ref.shape[0]
     plane = order_k * order_k
     to_high, to_low = spread_columns(to_ref[...])
-    back_high, back_low = spread_columns(back_ref[...])
+    back_high, back_low = spread_columns(to_ref[...], True)
     row_high, row_low, lane_high, lane_low = masks(order_k)
     value_pair = halves(rows_high(back_high) * rows_low(back_low))
     back_pair = halves(rows_high(to_high) * rows_low(to_low))
@@ -107,6 +107,14 @@
     product = values * (by_x(pot_ref) + 0.25 * values * values)
     source = mm_halves(source_x, halves(mm_halves(halves(product), back_pair)))
     out_ref[...] = source.astype(jnp.bfloat16).reshape(out_ref.shape)
+    peers = rows_ref.shape[0]
+    if peers > pot_ref.shape[0]:
+        rows_ref[...] = jnp.zeros_like(rows_ref)
+    for b in range(pot_ref.shape[0]):
+        peer = parent_of[b] * 8 // pot_ref.shape[0] % peers
+        for x in range(order_k):
+            rows_ref[peer, x : x + 1, :] = pot_ref[b : b + 1, x * plane : (x + 1) * plane]
+    pot_out[...] = rows_ref[...].astype(jnp.bfloat16)
 
 
 def route_kernel(dims, info, words_ref, w_hbm, *refs):
@@ -119,8 +127,14 @@
     words = words_ref[...].reshape(-1, LANES)
     table = jnp.concatenate([words[:, :width], words[:, width:]], axis=0)
     total = table.shape[0]
-    place_col, id_col = table[:, slots : slots + 1], table[:, slots + 1 : slots + 2]
+
+    def box_id(row):
+        member = row % (total // 2)
+        return member // (boxes // 2) * boxes + row // (total // 2) * (boxes // 2) + member % (boxes // 2)
+
+    place_col, id_col = table[:, slots : slots + 1], box_id(iota((total, 1), 0))
     flat = table.astype(jnp.float32).T.astype(jnp.int32)
+    flat = jnp.where(iota(flat.shape, 0) == slots + 1, box_id(iota(flat.shape, 1)), flat)
     low = (flat % 256).astype(jnp.float32).astype(jnp.bfloat16)
     high = (flat // 256).astype(jnp.float32).astype(jnp.bfloat16)
 
@@ -187,13 +201,12 @@
     load.wait()
 
 
-def constants_kernel(owner, pot_ref, to_ref, back_ref, two_ref, flip_ref, mats_ref, lift_ref, drop_ref, pot_out, rows_ref):
+def constants_kernel(to_ref, two_ref, mats_ref, lift_ref, drop_ref):
     order_k = to_ref.shape[0]
-    plane = order_k * order_k
     to_high, to_low = spread_columns(to_ref[...])
-    back_high, back_low = spread_columns(back_ref[...])
+    back_high, back_low = spread_columns(to_ref[...], True)
     two = [spread_columns(two_ref[c]) for c in range(2)]
-    flip = [spread_columns(flip_ref[c]) for c in range(2)]
+    flip = [spread_columns(two_ref[c], True) for c in range(2)]
     row_high, row_low, lane_high, lane_low = masks(order_k)
     made = []
     for quad in range(4):
@@ -217,17 +230,10 @@
         iota(lift_ref.shape, 0) // order_k == iota(lift_ref.shape, 1) // (2 * order_k), lifted, 0.0
     )
     hot = (iota((order_k, parents), 1) % order_k == iota((order_k, parents), 0)).astype(jnp.float32)
-    dropped = jnp.concatenate([mm(flip_ref[c], hot) for c in range(2)] * (parents // order_k), axis=0)
+    dropped = jnp.concatenate([mm(two_ref[c].T, hot) for c in range(2)] * (parents // order_k), axis=0)
     drop_ref[...] = jnp.where(
         iota(drop_ref.shape, 0) // (2 * order_k) == iota(drop_ref.shape, 1) // order_k, dropped, 0.0
     )
-    if rows_ref.shape[0] > pot_ref.shape[0]:
-        rows_ref[...] = jnp.zeros_like(rows_ref)
-    for b in range(pot_ref.shape[0]):
-        peer = owner[b]
-        for x in range(order_k):
-            rows_ref[peer, x : x + 1, :] = pot_ref[b : b + 1, x * plane : (x + 1) * plane]
-    pot_out[...] = rows_ref[...].astype(jnp.bfloat16)
 
 
 def tree_kernel(last, part_count, came_from, *refs):
@@ -276,10 +282,11 @@
         out_ref[...] = source.astype(jnp.bfloat16).reshape(out_ref.shape)
 
 
-def unpack_kernel(owner, field_ref, out_ref):
-    order_k, plane = field_ref.shape[1:]
-    for b in range(out_ref.shape[0]):
-        box = field_ref[owner[b]].astype(jnp.float32)
+def unpack_kernel(parent_of, field_ref, out_ref):
+    peers, order_k, plane = field_ref.shape
+    boxes = out_ref.shape[0]
+    for b in range(boxes):
+        box = field_ref[parent_of[b] * 8 // boxes % peers].astype(jnp.float32)
         for x in range(order_k):
             out_ref[b : b + 1, x * plane : (x + 1) * plane] = box[x : x + 1]
 
@@ -430,7 +437,7 @@
             pltpu.VMEM((len(sources) * block_boxes, order_k, plane), jnp.bfloat16),
             pltpu.SemaphoreType.DMA((len(sources),)),
         ],
-        compiler_params=pltpu.CompilerParams(vmem_limit_bytes=20 * MIB),
+        compiler_params=pltpu.CompilerParams(vmem_limit_bytes=11 * MIB),
         name="convolve",
     )(packed, *sources, shifted, held_kernels)
 
@@ -465,30 +472,44 @@
     oct_here, hi_here, lo_here = (lax.axis_index(name) for name in ("oct", "hi", "lo"))
     sub_count = hi_count * lo_count
     devices_all = oct_count * sub_count
-    device_here = oct_here * sub_count + hi_here * lo_count + lo_here
-    info = jnp.stack([oct_here, hi_here, lo_here, device_here]).astype(jnp.int32)
-    flipped = jnp.swapaxes(two_scale, 1, 2)
-    back_values = to_values.T
+    info = jnp.stack([oct_here, hi_here, lo_here]).astype(jnp.int32)
     tile = (box_count, order_k, plane)
-
-    own_place = parent_of * 8 + child_octant
-    own_owner = own_place // box_count % sub_count
+    peer_tiles = jax.ShapeDtypeStruct((sub_count, order_k, plane), jnp.bfloat16)
+
     words = pl.pallas_call(
         pack_kernel,
         out_shape=jax.ShapeDtypeStruct((devices_all, box_count // 2, LANES), jnp.int32),
-        in_specs=[SMEM] + [VMEM] * 3,
+        in_specs=[SMEM] * 2 + [VMEM] * 2,
         out_specs=VMEM,
         name="pack_tables",
-    )(info, disp_ids, dest_box, own_place.reshape(box_count, 1))
+    )(parent_of, child_octant, disp_ids, dest_box)
+    words, coefficients = lax.optimization_barrier((words, coefficients))
     words = lax.all_to_all(words, ("oct", "hi", "lo"), 0, 0, tiled=True)
 
-    source = pl.pallas_call(
+    source, send_potential = pl.pallas_call(
         first_kernel,
-        out_shape=jax.ShapeDtypeStruct(tile, jnp.bfloat16),
-        in_specs=[VMEM] * 4,
-        out_specs=VMEM,
+        out_shape=[jax.ShapeDtypeStruct(tile, jnp.bfloat16), peer_tiles],
+        in_specs=[SMEM] + [VMEM] * 3,
+        out_specs=[VMEM] * 2,
+        scratch_shapes=[pltpu.VMEM(peer_tiles.shape, jnp.float32)],
         name="first_source",
-    )(coefficients, potential, to_values, back_values)
+    )(parent_of, coefficients, potential, to_values)
+
+    parents = box_count // 8 * order_k
+    source, late_values = lax.optimization_barrier((source, to_values))
+    fixed = pl.pallas_call(
+        constants_kernel,
+        out_shape=[
+            pltpu.VMEM((12, 2, plane, plane), jnp.bfloat16),
+            jax.ShapeDtypeStruct((parents, 2 * parents), jnp.float32),
+            jax.ShapeDtypeStruct((2 * parents, parents), jnp.float32),
+        ],
+        in_specs=[VMEM] * 2,
+        out_specs=[VMEM] * 3,
+        compiler_params=pltpu.CompilerParams(vmem_limit_bytes=16 * MIB),
+        name="make_constants",
+    )(late_values, two_scale)
+    fixed = [pltpu.with_memory_space_constraint(fixed[0], pltpu.VMEM)] + list(fixed[1:])
 
     list_rows = -(-(oct_count * lo_count * box_count * slot_count // LANES + 8) // 8) * 8
     *lists, moved, held_kernels = pl.pallas_call(
@@ -501,9 +522,12 @@
         in_specs=[SMEM, VMEM, ANY],
         out_specs=[VMEM] * (ITERS + 2),
         scratch_shapes=[pltpu.SemaphoreType.DMA],
-        compiler_params=pltpu.CompilerParams(vmem_limit_bytes=20 * MIB),
+        compiler_params=pltpu.CompilerParams(vmem_limit_bytes=11 * MIB),
         name="route_slots",
     )(info, words, yz_kernels)
+    held_kernels = pltpu.with_memory_space_constraint(held_kernels, pltpu.VMEM)
+    lists, send_potential = lax.optimization_barrier((lists, send_potential))
+    moved_potential = lax.all_to_all(send_potential, ("hi", "lo"), 0, 0, tiled=True)
     came_from = moved[1, :box_count] // box_count % sub_count
     shifted = shifted_factors(x_kernels)
 
@@ -511,30 +535,13 @@
         last = iteration == ITERS - 1
         sources = gather_sources(source, lo_count)
         outs = convolve(sources, shifted, held_kernels, lists[iteration], hi_count, term_count, order_k)
-        if not last:
-            late, outs = lax.optimization_barrier(((potential, own_owner), outs))
-            parents = box_count // 8 * order_k
-            *fixed, send_potential = pl.pallas_call(
-                constants_kernel,
-                out_shape=[
-                    jax.ShapeDtypeStruct((12, 2, plane, plane), jnp.bfloat16),
-                    jax.ShapeDtypeStruct((parents, 2 * parents), jnp.float32),
-                    jax.ShapeDtypeStruct((2 * parents, parents), jnp.float32),
-                    jax.ShapeDtypeStruct((sub_count, order_k, plane), jnp.bfloat16),
-                ],
-                in_specs=[SMEM] + [VMEM] * 5,
-                out_specs=[VMEM] * 4,
-                scratch_shapes=[pltpu.VMEM((sub_count, order_k, plane), jnp.float32)],
-                compiler_params=pltpu.CompilerParams(vmem_limit_bytes=16 * MIB),
-                name="make_constants",
-            )(late[1], late[0], to_values, back_values, two_scale, flipped)
         parts = [outs[0]] + [lax.ppermute(outs[r], "hi", flips(hi_count, r)) for r in range(1, hi_count)]
         kernel = functools.partial(tree_kernel, last, hi_count)
         if last:
             fields, parents = pl.pallas_call(
                 kernel,
                 out_shape=[
-                    jax.ShapeDtypeStruct((sub_count, order_k, plane), jnp.bfloat16),
+                    peer_tiles,
                     jax.ShapeDtypeStruct((box_count // 8, order_k * plane), jnp.float32),
                 ],
                 in_specs=[SMEM] + [VMEM] * (hi_count + 3),
@@ -542,7 +549,6 @@
                 name="last_tree",
             )(came_from, *parts, *fixed)
         else:
-            moved_potential = lax.all_to_all(send_potential, ("hi", "lo"), 0, 0, tiled=True)
             source = pl.pallas_call(
                 kernel,
                 out_shape=jax.ShapeDtypeStruct(tile, jnp.bfloat16),
@@ -557,7 +563,7 @@
         in_specs=[SMEM, VMEM],
         out_specs=VMEM,
         name="unpack_fields",
-    )(own_owner, returned)
+    )(parent_of, returned)
     return next_field, parents
 
 

time: 173 us -> 164 us (0.948); the launches traced: 175 us -> 163 us
  local copies, waits for them, and re-layouts: 34.2 us -> 29.6 us
  Pallas kernels: 63.1 us -> 59.1 us
  blocking collectives: 14.9 us -> 12.9 us
    unnamed x55 -> x39, local copies, waits for them, and re-layouts: 32.2 us -> 28.2 us
    pallas_call x3, Pallas kernels: 9.19 us -> 6.99 us  [the longest x1 3.3 us: shards(): pl.pallas_call(first_kernel, out_shape=[jax.ShapeDtypeStruct(tile, jnp.bf...]
    all_to_all x1, blocking collectives: 14.9 us -> 12.9 us  [shards(): returned = lax.all_to_all(fields, ('hi', 'lo'), 0, 0, tiled=True)]
  transfers between devices with their start and end apart: 22 -> 22, of which waited for: 10 -> 9; matrix products, arithmetic and copies ran while one was open for 3% -> 1% of each run, Pallas kernels for 6% -> 16%
where the time goes in v2:
time: 164 us; the launch traced here: 163 us
  Pallas kernels  59.1 us (36%)
  waiting for transfers between devices  31.2 us (19%)
  local copies, waits for them, and re-layouts  29.6 us (18%)
  starting transfers between devices  29 us (18%)
  blocking collectives  12.9 us (8%)
    pallas_call x2, Pallas kernels, convolve(): pl.pallas_call(functools.partial(conv_kernel, dims), out_shape=[tile] * d...  36.3 us
    unnamed x39, local copies, waits for them, and re-layouts  28.2 us
    ppermute x6, waiting for transfers between devices, shards(): lax.ppermute(outs[r], 'hi', flips(hi_count, r))  18.1 us
    all_to_all x1, blocking collectives, shards(): returned = lax.all_to_all(fields, ('hi', 'lo'), 0, 0, tiled=True)  12.9 us
    ppermute x6, starting transfers between devices, shards(): lax.ppermute(outs[r], 'hi', flips(hi_count, r))  9.12 us
    pallas_call x1, Pallas kernels, shards(): pl.pallas_call(functools.partial(route_kernel, (oct_count, hi_count, lo_c...  8.26 us
    ppermute x6, starting transfers between devices, gather_sources(): lax.ppermute(source, 'lo', flips(lo_count, r))  8.02 us
    ppermute x6, waiting for transfers between devices, gather_sources(): lax.ppermute(source, 'lo', flips(lo_count, r))  6.54 us
  transfers between devices with their start and end apart: 22, of which 9 were waited for; matrix products, arithmetic and copies ran while one was open for 1% of the time, Pallas kernels for 16%

profile of v2, /device:TPU:0, one launch (start us, length us, event | category | flops | bytes accessed | tf_op | source)
XLA Modules:
  0.0 163.2 jit_solution(6059395521908729275)
XLA Ops:
  0.7 1.6 %pack_tables.1 = s32[32,8,128]{2,1,0:T(8,128)} custom-call(s32[16]{0:T(128)} %parent_of.5, s32[16]{0:T(128)} %octant.1, s32[16,16]{1,0:T(8,128)} %disp_ref.1, s32[16,16]{1,0:T(8,128)} %dest_ref.1), custom_call_target="tpu_custom_call" | custom-call | tf_op jit(solution)/shard_map/pack_tables/pallas_call | solution.py:479
  2.3 3.3 %first_source.1 = (bf16[16,16,256]{2,1,0:T(8,128)(2,1)}, bf16[16,16,256]{2,1,0:T(8,128)(2,1)}) custom-call(s32[16]{0:T(128)} %parent_of.5, f32[16,4096]{1,0:T(8,128)} %coef_ref, f32[16,4096]{1,0:T(8,128)} %pot_ref.1, f32[16,16]{1,0:T(8,128)} %to_ref.2), custom_call_target="tpu_custom_call" | custom-call | tf_op jit(solution)/shard_map/first_source/pallas_call | solution.py:489
  5.6 2.9 %collective-permute-start = (bf16[16,16,256]{2,1,0:T(8,128)(2,1)}, bf16[16,16,256]{2,1,0:T(8,128)(2,1)}, u32[]{:S(2)}, u32[]{:S(2)}) collective-permute-start(bf16[16,16,256]{2,1,0:T(8,128)(2,1)} %get-tuple-element.37.refs_0_), channel_id=1, source_target_pairs={{0,1},{1,0},{2,3},{3,2},{4,5},{5,4},{6,7},{7,6},{8,9},{9,8},{10,11... | collective-permute-start | bytes 393224 | tf_op jit(solution)/shard_map/ppermute | solution.py:450
  8.5 1.5 collective-permute-start.1
  10.1 6.4 %all-to-all-start = ((s32[32,8,128]{2,1,0:T(8,128)}), s32[32,8,128]{2,1,0:T(8,128)S(1)}, u32[]{:S(2)}, u32[]{:S(2)}) async-start(s32[32,8,128]{2,1,0:T(8,128)} %pack_tables.1), calls=%async_computation | async-start | bytes 262144 | tf_op jit(solution)/shard_map/all_to_all | solution.py:487
  16.5 1.1 copy.27
  17.6 0.2 reshape.11
  18.2 0.3 collective-permute-start.4
  18.4 0.3 collective-permute-start.5
  18.7 0.3 collective-permute-start.6
  18.9 5.5 %all-to-all-done.words_ref = s32[32,8,128]{2,1,0:T(8,128)S(1)} async-done(((s32[32,8,128]{2,1,0:T(8,128)}), s32[32,8,128]{2,1,0:T(8,128)S(1)}, u32[]{:S(2)}, u32[]{:S(2)}) %all-to-all-start) | async-done | bytes 131104 | tf_op jit(solution)/shard_map/all_to_all | solution.py:487
  24.4 8.3 %route_slots.1 = (s32[24,128]{1,0:T(8,128)S(1)}, s32[24,128]{1,0:T(8,128)S(1)}, s32[8,128]{1,0:T(8,128)S(1)}, bf16[256,46080]{1,0:T(8,128)(2,1)S(1)}) custom-call(s32[3]{0:T(128)S(1)} %pad_add_fusion.info, s32[32,8,128]{2,1,0:T(8,128)S(1)} %all-to-all-done.words_ref, bf16[256,46080]{1,0:T(8,128)(2,1)} %w_hbm.1), custom_call_target="tpu_custom_call" | custom-call | tf_op jit(solution)/shard_map/route_slots/pallas_call | solution.py:515
  32.7 7.8 %copy-done = bf16[256,46080]{1,0:T(8,128)(2,1)} copy-done((bf16[256,46080]{1,0:T(8,128)(2,1)}, bf16[256,46080]{1,0:T(8,128)(2,1)S(1)}, u32[]{:S(2)}) %copy-start) | copy-done | bytes 23592984
  40.5 4.2 %all-to-all-start.1 = ((bf16[16,16,256]{2,1,0:T(8,128)(2,1)}), bf16[16,16,256]{2,1,0:T(8,128)(2,1)}, u32[]{:S(2)}, u32[]{:S(2)}) async-start(bf16[16,16,256]{2,1,0:T(8,128)(2,1)} %get-tuple-element.47), calls=%async_computation.1 | async-start | bytes 262144 | tf_op jit(solution)/shard_map/all_to_all | solution.py:530
  44.7 0.9 make_constants.1
  45.7 0.6 copy-done.5
  46.3 0.6 copy-done.8
  46.9 7.7 %copy-done.1 = bf16[256,46080]{1,0:T(8,128)(2,1)S(1)} copy-done((bf16[256,46080]{1,0:T(8,128)(2,1)S(1)}, bf16[256,46080]{1,0:T(8,128)(2,1)}, u32[]{:S(2)}) %copy-start.1) | copy-done | bytes 23592984
  54.6 17.7 %convolve.2 = (bf16[16,16,256]{2,1,0:T(8,128)(2,1)S(1)}, bf16[16,16,256]{2,1,0:T(8,128)(2,1)S(1)}, bf16[16,16,256]{2,1,0:T(8,128)(2,1)S(1)}, bf16[16,16,256]{2,1,0:T(8,128)(2,1)S(1)}) custom-call(s32[24,128]{1,0:T(8,128)S(1)} %get-tuple-element.35.packed, bf16[16,16,256]{2,1,0:T(8,128)(2,1)S(1)} %copy-done.4, ...), custom_call_target="tpu_custom_call" | custom-call | tf_op jit(solution)/shard_map/convolve/pallas_call | solution.py:429
  72.3 0.6 copy-done.6
  73.0 2.4 %collective-permute-start.7 = (bf16[16,16,256]{2,1,0:T(8,128)(2,1)S(1)}, bf16[16,16,256]{2,1,0:T(8,128)(2,1)S(1)}, u32[]{:S(2)}, u32[]{:S(2)}) collective-permute-start(bf16[16,16,256]{2,1,0:T(8,128)(2,1)S(1)} %get-tuple-element.40), channel_id=1, source_target_pairs={{0,4},{4,0},{8,12},{12,8},{1,5},{5,1},{9,13},{13,9},{2,6},{6,2},{1... | collective-permute-start | bytes 393224 | tf_op jit(solution)/shard_map/ppermute | solution.py:538
  75.3 1.5 collective-permute-start.8
  76.9 0.8 collective-permute-start.9
  77.7 0.5 and_select_fusion.came_from
  78.2 1.5 collective-permute-done.7.refs_1_
  79.7 7.3 %collective-permute-done.8.refs_2_ = bf16[16,16,256]{2,1,0:T(8,128)(2,1)S(1)} collective-permute-done((bf16[16,16,256]{2,1,0:T(8,128)(2,1)S(1)}, bf16[16,16,256]{2,1,0:T(8,128)(2,1)S(1)}, u32[]{:S(2)}, u32[]{:S(2)}) %collective-permute-start.8) | collective-permute-done | bytes 131104 | tf_op jit(solution)/shard_map/ppermute | solution.py:538
  87.0 0.7 copy-done.12
  87.6 4.2 %tree_source.1.refs_0_ = bf16[16,16,256]{2,1,0:T(8,128)(2,1)} custom-call(s32[16]{0:T(128)} %and_select_fusion.came_from, bf16[16,16,256]{2,1,0:T(8,128)(2,1)} %copy-done.6, bf16[16,16,256]{2,1,0:T(8,128)(2,1)} %copy-done.11, bf16[16,16,256]{2,1,0:T(8,128)(2,1)} %copy-done.12, bf16[16,16,256]{2,1,0:T(8,128)(2,1)} %collective-permute-done.9.refs_3_, ...), custom_call_target="tpu_custom_call" | custom-call | tf_op jit(solution)/shard_map/tree_source/pallas_call | solution.py:552
  91.8 1.6 collective-permute-start.10
  93.4 0.5 collective-permute-start.11
  93.9 1.5 collective-permute-start.12
  95.3 1.8 %collective-permute-done.10.refs_1_ = bf16[16,16,256]{2,1,0:T(8,128)(2,1)S(1)} collective-permute-done((bf16[16,16,256]{2,1,0:T(8,128)(2,1)}, bf16[16,16,256]{2,1,0:T(8,128)(2,1)S(1)}, u32[]{:S(2)}, u32[]{:S(2)}) %collective-permute-start.10) | collective-permute-done | bytes 131104 | tf_op jit(solution)/shard_map/ppermute | solution.py:450
  97.1 4.7 %collective-permute-done.11.refs_2_ = bf16[16,16,256]{2,1,0:T(8,128)(2,1)S(1)} collective-permute-done((bf16[16,16,256]{2,1,0:T(8,128)(2,1)}, bf16[16,16,256]{2,1,0:T(8,128)(2,1)S(1)}, u32[]{:S(2)}, u32[]{:S(2)}) %collective-permute-start.11) | collective-permute-done | bytes 131104 | tf_op jit(solution)/shard_map/ppermute | solution.py:450
  101.9 0.5 collective-permute-start.16
  102.4 0.8 collective-permute-done.15.refs_6_
  103.2 0.2 collective-permute-done.16.refs_7_
  103.4 7.7 %copy-done.2 = bf16[256,46080]{1,0:T(8,128)(2,1)S(1)} copy-done((bf16[256,46080]{1,0:T(8,128)(2,1)S(1)}, bf16[256,46080]{1,0:T(8,128)(2,1)}, u32[]{:S(2)}) %copy-start.2) | copy-done | bytes 23592984
  111.1 0.9 copy-done.3
  112.0 18.6 %convolve.3 = (bf16[16,16,256]{2,1,0:T(8,128)(2,1)S(1)}, bf16[16,16,256]{2,1,0:T(8,128)(2,1)S(1)}, bf16[16,16,256]{2,1,0:T(8,128)(2,1)S(1)}, bf16[16,16,256]{2,1,0:T(8,128)(2,1)S(1)}) custom-call(s32[24,128]{1,0:T(8,128)S(1)} %get-tuple-element.34.packed, bf16[16,16,256]{2,1,0:T(8,128)(2,1)S(1)} %copy-done.3, ...), custom_call_target="tpu_custom_call" | custom-call | tf_op jit(solution)/shard_map/convolve/pallas_call | solution.py:429
  130.6 0.6 copy-done.7
  131.3 1.6 collective-permute-start.17
  132.9 2.8 %collective-permute-start.19 = (bf16[16,16,256]{2,1,0:T(8,128)(2,1)S(1)}, bf16[16,16,256]{2,1,0:T(8,128)(2,1)S(1)}, u32[]{:S(2)}, u32[]{:S(2)}) collective-permute-start(bf16[16,16,256]{2,1,0:T(8,128)(2,1)S(1)} %get-tuple-element.51), channel_id=1, source_target_pairs={{0,12},{4,8},{8,4},{12,0},{1,13},{5,9},{9,5},{13,1},{2,14},{6,10},... | collective-permute-start | bytes 393224 | tf_op jit(solution)/shard_map/ppermute | solution.py:538
  135.7 1.4 collective-permute-done.17.refs_1_
  137.0 8.0 %collective-permute-done.18.refs_2_ = bf16[16,16,256]{2,1,0:T(8,128)(2,1)S(1)} collective-permute-done((bf16[16,16,256]{2,1,0:T(8,128)(2,1)S(1)}, bf16[16,16,256]{2,1,0:T(8,128)(2,1)S(1)}, u32[]{:S(2)}, u32[]{:S(2)}) %collective-permute-start.18) | collective-permute-done | bytes 131104 | tf_op jit(solution)/shard_map/ppermute | solution.py:538
  145.0 0.7 copy-done.15
  145.7 2.8 %last_tree.1 = (bf16[16,16,256]{2,1,0:T(8,128)(2,1)}, f32[2,4096]{1,0:T(2,128)}) custom-call(s32[16]{0:T(128)} %and_select_fusion.came_from, bf16[16,16,256]{2,1,0:T(8,128)(2,1)} %copy-done.7, bf16[16,16,256]{2,1,0:T(8,128)(2,1)} %copy-done.13, bf16[16,16,256]{2,1,0:T(8,128)(2,1)} %copy-done.14, bf16[16,16,256]{2,1,0:T(8,128)(2,1)} %copy-done.15, ...), custom_call_target="tpu_custom_call" | custom-call | tf_op jit(solution)/shard_map/last_tree/pallas_call | solution.py:541
  148.5 12.9 %all_to_all.15.field_ref = bf16[16,16,256]{2,1,0:T(8,128)(2,1)} all-to-all(bf16[16,16,256]{2,1,0:T(8,128)(2,1)} %get-tuple-element.52), channel_id=1, replica_groups=mesh['oct'=2,'hi'=4,'lo'=4] {'hi','lo'}, dimensions={0} | all-to-all | bytes 262144 | tf_op jit(solution)/shard_map/all_to_all | solution.py:559
  161.4 1.8 %unpack_fields.1 = f32[16,4096]{1,0:T(8,128)} custom-call(s32[16]{0:T(128)} %parent_of.5, bf16[16,16,256]{2,1,0:T(8,128)(2,1)} %all_to_all.15.field_ref), custom_call_target="tpu_custom_call" | custom-call | tf_op jit(solution)/shard_map/unpack_fields/pallas_call | solution.py:560
  (50 shorter events, 0.5 us)
Async XLA Ops:
  0.6 44.1 %copy-start.9 = (f32[16,16]{1,0:T(8,128)S(1)}, f32[16,16]{1,0:T(8,128)}, u32[]{:S(2)}) copy-start(f32[16,16]{1,0:T(8,128)} %to_ref.2) | copy-start | bytes 3076
  0.6 44.1 %copy-start.10 = (f32[2,16,16]{2,1,0:T(8,128)S(1)}, f32[2,16,16]{2,1,0:T(8,128)}, u32[]{:S(2)}) copy-start(f32[2,16,16]{2,1,0:T(8,128)} %two_ref.1) | copy-start | bytes 6148
  5.6 41.3 %copy-start.4 = (bf16[16,16,256]{2,1,0:T(8,128)(2,1)S(1)}, bf16[16,16,256]{2,1,0:T(8,128)(2,1)}, u32[]{:S(2)}) copy-start(bf16[16,16,256]{2,1,0:T(8,128)(2,1)} %get-tuple-element.37.refs_0_) | copy-start | bytes 393220
  5.6 12.6 %collective-permute-start = (bf16[16,16,256]{2,1,0:T(8,128)(2,1)}, bf16[16,16,256]{2,1,0:T(8,128)(2,1)}, u32[]{:S(2)}, u32[]{:S(2)}) collective-permute-start(bf16[16,16,256]{2,1,0:T(8,128)(2,1)} %get-tuple-element.37.refs_0_), channel_id=1, source_target_pairs={{0,1},{1,0},{2,3},{3,2},{4,5},{5,4},{6,7},{7,6},{8,9},{9,8},{10,11... | collective-permute-start | bytes 393224 | tf_op jit(solution)/shard_map/ppermute | solution.py:450
  8.5 9.9 %collective-permute-start.1 = (bf16[16,16,256]{2,1,0:T(8,128)(2,1)}, bf16[16,16,256]{2,1,0:T(8,128)(2,1)}, u32[]{:S(2)}, u32[]{:S(2)}) collective-permute-start(bf16[16,16,256]{2,1,0:T(8,128)(2,1)} %get-tuple-element.37.refs_0_), channel_id=1, source_target_pairs={{0,2},{1,3},{2,0},{3,1},{4,6},{5,7},{6,4},{7,5},{8,10},{9,11},{10,... | collective-permute-start | bytes 393224 | tf_op jit(solution)/shard_map/ppermute | solution.py:450
  10.1 8.6 %collective-permute-start.2 = (bf16[16,16,256]{2,1,0:T(8,128)(2,1)}, bf16[16,16,256]{2,1,0:T(8,128)(2,1)}, u32[]{:S(2)}, u32[]{:S(2)}) collective-permute-start(bf16[16,16,256]{2,1,0:T(8,128)(2,1)} %get-tuple-element.37.refs_0_), channel_id=1, source_target_pairs={{0,3},{1,2},{2,1},{3,0},{4,7},{5,6},{6,5},{7,4},{8,11},{9,10},{10,... | collective-permute-start | bytes 393224 | tf_op jit(solution)/shard_map/ppermute | solution.py:450
  10.1 36.8 %collective-permute-start.3 = (bf16[16,16,256]{2,1,0:T(8,128)(2,1)}, bf16[16,16,256]{2,1,0:T(8,128)(2,1)}, u32[]{:S(2)}, u32[]{:S(2)}) collective-permute-start(bf16[16,16,256]{2,1,0:T(8,128)(2,1)} %get-tuple-element.37.refs_0_), channel_id=1, source_target_pairs={{0,16},{16,0},{1,17},{17,1},{2,18},{18,2},{3,19},{19,3},{4,20},{20... | collective-permute-start | bytes 393224 | tf_op jit(solution)/shard_map/ppermute | solution.py:451
  10.1 14.4 %all-to-all-start = ((s32[32,8,128]{2,1,0:T(8,128)}), s32[32,8,128]{2,1,0:T(8,128)S(1)}, u32[]{:S(2)}, u32[]{:S(2)}) async-start(s32[32,8,128]{2,1,0:T(8,128)} %pack_tables.1), calls=%async_computation | async-start | bytes 262144 | tf_op jit(solution)/shard_map/all_to_all | solution.py:487
  18.2 28.7 %collective-permute-start.4 = (bf16[16,16,256]{2,1,0:T(8,128)(2,1)}, bf16[16,16,256]{2,1,0:T(8,128)(2,1)}, u32[]{:S(2)}, u32[]{:S(2)}) collective-permute-start(bf16[16,16,256]{2,1,0:T(8,128)(2,1)} %collective-permute-done.refs_1_), channel_id=1, source_target_pairs={{0,16},{16,0},{1,17},{17,1},{2,18},{18,2},{3,19},{19,3},{4,20},{20... | collective-permute-start | bytes 393224 | tf_op jit(solution)/shard_map/ppermute | solution.py:451
  18.4 28.4 %collective-permute-start.5 = (bf16[16,16,256]{2,1,0:T(8,128)(2,1)}, bf16[16,16,256]{2,1,0:T(8,128)(2,1)}, u32[]{:S(2)}, u32[]{:S(2)}) collective-permute-start(bf16[16,16,256]{2,1,0:T(8,128)(2,1)} %collective-permute-done.1.refs_2_), channel_id=1, source_target_pairs={{0,16},{16,0},{1,17},{17,1},{2,18},{18,2},{3,19},{19,3},{4,20},{20... | collective-permute-start | bytes 393224 | tf_op jit(solution)/shard_map/ppermute | solution.py:451
  18.7 28.2 %collective-permute-start.6 = (bf16[16,16,256]{2,1,0:T(8,128)(2,1)}, bf16[16,16,256]{2,1,0:T(8,128)(2,1)}, u32[]{:S(2)}, u32[]{:S(2)}) collective-permute-start(bf16[16,16,256]{2,1,0:T(8,128)(2,1)} %collective-permute-done.2.refs_3_), channel_id=1, source_target_pairs={{0,16},{16,0},{1,17},{17,1},{2,18},{18,2},{3,19},{19,3},{4,20},{20... | collective-permute-start | bytes 393224 | tf_op jit(solution)/shard_map/ppermute | solution.py:451
  32.7 7.8 %copy-start = (bf16[256,46080]{1,0:T(8,128)(2,1)}, bf16[256,46080]{1,0:T(8,128)(2,1)S(1)}, u32[]{:S(2)}) copy-start(bf16[256,46080]{1,0:T(8,128)(2,1)S(1)} %get-tuple-element.38.refs_9_) | copy-start | bytes 70778880
  40.5 47.1 %all-to-all-start.1 = ((bf16[16,16,256]{2,1,0:T(8,128)(2,1)}), bf16[16,16,256]{2,1,0:T(8,128)(2,1)}, u32[]{:S(2)}, u32[]{:S(2)}) async-start(bf16[16,16,256]{2,1,0:T(8,128)(2,1)} %get-tuple-element.47), calls=%async_computation.1 | async-start | bytes 262144 | tf_op jit(solution)/shard_map/all_to_all | solution.py:530
  45.7 0.6 copy-start.5
  46.3 0.6 copy-start.8
  46.9 7.7 %copy-start.1 = (bf16[256,46080]{1,0:T(8,128)(2,1)S(1)}, bf16[256,46080]{1,0:T(8,128)(2,1)}, u32[]{:S(2)}) copy-start(bf16[256,46080]{1,0:T(8,128)(2,1)} %copy-done) | copy-start | bytes 70778880
  72.3 0.7 copy-start.6
  73.0 6.7 %collective-permute-start.7 = (bf16[16,16,256]{2,1,0:T(8,128)(2,1)S(1)}, bf16[16,16,256]{2,1,0:T(8,128)(2,1)S(1)}, u32[]{:S(2)}, u32[]{:S(2)}) collective-permute-start(bf16[16,16,256]{2,1,0:T(8,128)(2,1)S(1)} %get-tuple-element.40), channel_id=1, source_target_pairs={{0,4},{4,0},{8,12},{12,8},{1,5},{5,1},{9,13},{13,9},{2,6},{6,2},{1... | collective-permute-start | bytes 393224 | tf_op jit(solution)/shard_map/ppermute | solution.py:538
  75.3 11.6 %collective-permute-start.8 = (bf16[16,16,256]{2,1,0:T(8,128)(2,1)S(1)}, bf16[16,16,256]{2,1,0:T(8,128)(2,1)S(1)}, u32[]{:S(2)}, u32[]{:S(2)}) collective-permute-start(bf16[16,16,256]{2,1,0:T(8,128)(2,1)S(1)} %get-tuple-element.41), channel_id=1, source_target_pairs={{0,8},{4,12},{8,0},{12,4},{1,9},{5,13},{9,1},{13,5},{2,10},{6,14},... | collective-permute-start | bytes 393224 | tf_op jit(solution)/shard_map/ppermute | solution.py:538
  76.9 10.8 %collective-permute-start.9 = (bf16[16,16,256]{2,1,0:T(8,128)(2,1)S(1)}, bf16[16,16,256]{2,1,0:T(8,128)(2,1)}, u32[]{:S(2)}, u32[]{:S(2)}) collective-permute-start(bf16[16,16,256]{2,1,0:T(8,128)(2,1)S(1)} %get-tuple-element.42), channel_id=1, source_target_pairs={{0,12},{4,8},{8,4},{12,0},{1,13},{5,9},{9,5},{13,1},{2,14},{6,10},... | collective-permute-start | bytes 393224 | tf_op jit(solution)/shard_map/ppermute | solution.py:538
  79.7 7.9 %copy-start.11 = (bf16[16,16,256]{2,1,0:T(8,128)(2,1)}, bf16[16,16,256]{2,1,0:T(8,128)(2,1)S(1)}, u32[]{:S(2)}) copy-start(bf16[16,16,256]{2,1,0:T(8,128)(2,1)S(1)} %collective-permute-done.7.refs_1_) | copy-start | bytes 393220
  87.0 0.7 copy-start.12
  91.8 5.4 %collective-permute-start.10 = (bf16[16,16,256]{2,1,0:T(8,128)(2,1)}, bf16[16,16,256]{2,1,0:T(8,128)(2,1)S(1)}, u32[]{:S(2)}, u32[]{:S(2)}) collective-permute-start(bf16[16,16,256]{2,1,0:T(8,128)(2,1)} %tree_source.1.refs_0_), channel_id=1, source_target_pairs={{0,1},{1,0},{2,3},{3,2},{4,5},{5,4},{6,7},{7,6},{8,9},{9,8},{10,11... | collective-permute-start | bytes 393224 | tf_op jit(solution)/shard_map/ppermute | solution.py:450
  93.4 8.5 %collective-permute-start.11 = (bf16[16,16,256]{2,1,0:T(8,128)(2,1)}, bf16[16,16,256]{2,1,0:T(8,128)(2,1)S(1)}, u32[]{:S(2)}, u32[]{:S(2)}) collective-permute-start(bf16[16,16,256]{2,1,0:T(8,128)(2,1)} %tree_source.1.refs_0_), channel_id=1, source_target_pairs={{0,2},{1,3},{2,0},{3,1},{4,6},{5,7},{6,4},{7,5},{8,10},{9,11},{10,... | collective-permute-start | bytes 393224 | tf_op jit(solution)/shard_map/ppermute | solution.py:450
  93.9 8.0 %collective-permute-start.12 = (bf16[16,16,256]{2,1,0:T(8,128)(2,1)}, bf16[16,16,256]{2,1,0:T(8,128)(2,1)S(1)}, u32[]{:S(2)}, u32[]{:S(2)}) collective-permute-start(bf16[16,16,256]{2,1,0:T(8,128)(2,1)} %tree_source.1.refs_0_), channel_id=1, source_target_pairs={{0,3},{1,2},{2,1},{3,0},{4,7},{5,6},{6,5},{7,4},{8,11},{9,10},{10,... | collective-permute-start | bytes 393224 | tf_op jit(solution)/shard_map/ppermute | solution.py:450
  95.3 7.1 %collective-permute-start.13 = (bf16[16,16,256]{2,1,0:T(8,128)(2,1)}, bf16[16,16,256]{2,1,0:T(8,128)(2,1)S(1)}, u32[]{:S(2)}, u32[]{:S(2)}) collective-permute-start(bf16[16,16,256]{2,1,0:T(8,128)(2,1)} %tree_source.1.refs_0_), channel_id=1, source_target_pairs={{0,16},{16,0},{1,17},{17,1},{2,18},{18,2},{3,19},{19,3},{4,20},{20... | collective-permute-start | bytes 393224 | tf_op jit(solution)/shard_map/ppermute | solution.py:451
  97.1 5.2 %collective-permute-start.14 = (bf16[16,16,256]{2,1,0:T(8,128)(2,1)S(1)}, bf16[16,16,256]{2,1,0:T(8,128)(2,1)S(1)}, u32[]{:S(2)}, u32[]{:S(2)}) collective-permute-start(bf16[16,16,256]{2,1,0:T(8,128)(2,1)S(1)} %collective-permute-done.10.refs_1_), channel_id=1, source_target_pairs={{0,16},{16,0},{1,17},{17,1},{2,18},{18,2},{3,19},{19,3},{4,20},{20... | collective-permute-start | bytes 393224 | tf_op jit(solution)/shard_map/ppermute | solution.py:451
  101.9 1.3 collective-permute-start.15
  101.9 1.5 collective-permute-start.16
  103.4 7.7 %copy-start.2 = (bf16[256,46080]{1,0:T(8,128)(2,1)S(1)}, bf16[256,46080]{1,0:T(8,128)(2,1)}, u32[]{:S(2)}) copy-start(bf16[256,46080]{1,0:T(8,128)(2,1)} %copy-done) | copy-start | bytes 70778880
  111.1 0.9 copy-start.3
  130.6 0.7 copy-start.7
  131.3 5.8 %collective-permute-start.17 = (bf16[16,16,256]{2,1,0:T(8,128)(2,1)S(1)}, bf16[16,16,256]{2,1,0:T(8,128)(2,1)S(1)}, u32[]{:S(2)}, u32[]{:S(2)}) collective-permute-start(bf16[16,16,256]{2,1,0:T(8,128)(2,1)S(1)} %get-tuple-element.49), channel_id=1, source_target_pairs={{0,4},{4,0},{8,12},{12,8},{1,5},{5,1},{9,13},{13,9},{2,6},{6,2},{1... | collective-permute-start | bytes 393224 | tf_op jit(solution)/shard_map/ppermute | solution.py:538
  132.9 12.1 %collective-permute-start.18 = (bf16[16,16,256]{2,1,0:T(8,128)(2,1)S(1)}, bf16[16,16,256]{2,1,0:T(8,128)(2,1)S(1)}, u32[]{:S(2)}, u32[]{:S(2)}) collective-permute-start(bf16[16,16,256]{2,1,0:T(8,128)(2,1)S(1)} %get-tuple-element.50), channel_id=1, source_target_pairs={{0,8},{4,12},{8,0},{12,4},{1,9},{5,13},{9,1},{13,5},{2,10},{6,14},... | collective-permute-start | bytes 393224 | tf_op jit(solution)/shard_map/ppermute | solution.py:538
  132.9 12.1 %collective-permute-start.19 = (bf16[16,16,256]{2,1,0:T(8,128)(2,1)S(1)}, bf16[16,16,256]{2,1,0:T(8,128)(2,1)S(1)}, u32[]{:S(2)}, u32[]{:S(2)}) collective-permute-start(bf16[16,16,256]{2,1,0:T(8,128)(2,1)S(1)} %get-tuple-element.51), channel_id=1, source_target_pairs={{0,12},{4,8},{8,4},{12,0},{1,13},{5,9},{9,5},{13,1},{2,14},{6,10},... | collective-permute-start | bytes 393224 | tf_op jit(solution)/shard_map/ppermute | solution.py:538
  137.0 8.7 %copy-start.13 = (bf16[16,16,256]{2,1,0:T(8,128)(2,1)}, bf16[16,16,256]{2,1,0:T(8,128)(2,1)S(1)}, u32[]{:S(2)}) copy-start(bf16[16,16,256]{2,1,0:T(8,128)(2,1)S(1)} %collective-permute-done.17.refs_1_) | copy-start | bytes 393220
  145.0 0.7 copy-start.14
  145.0 0.7 copy-start.15

commit v3 on v2

--- a/solution.py
+++ b/solution.py
@@ -10,6 +10,7 @@
 
 ITERS = 2
 BLOCK = 32
+AHEAD = 3
 GROUP = 4
 LANES = 128
 MIB = 1024 * 1024
@@ -117,11 +118,9 @@
     pot_out[...] = rows_ref[...].astype(jnp.bfloat16)
 
 
-def route_kernel(dims, info, words_ref, w_hbm, *refs):
+def route_kernel(dims, info, words_ref, *refs):
     oct_count, hi_count, lo_count, boxes, slots, disp_rows = dims
-    list_refs, moved_ref, held_ref, sem = refs[:ITERS], refs[ITERS], refs[ITERS + 1], refs[ITERS + 2]
-    load = pltpu.make_async_copy(w_hbm, held_ref, sem)
-    load.start()
+    list_refs, moved_ref = refs[:ITERS], refs[ITERS]
     oct_here, hi_here, lo_here = info[0], info[1], info[2]
     width = LANES // 2
     words = words_ref[...].reshape(-1, LANES)
@@ -198,7 +197,6 @@
         for g in range(disp_rows):
             bound = jnp.where(lane == g, starts[g * slots : g * slots + 1].astype(jnp.int32), bound)
         list_refs[it][...] = jnp.where(iota(packed.shape, 0) == list_rows - 7, bound, packed)
-    load.wait()
 
 
 def constants_kernel(to_ref, two_ref, mats_ref, lift_ref, drop_ref):
@@ -294,9 +292,9 @@
 def conv_kernel(dims, packed, *refs):
     term_count, order_k, disp_count, source_count, dest_count = dims
     source_refs = refs[:source_count]
-    xl_ref, w_ref = refs[source_count : source_count + 2]
+    xl_ref, w_hbm = refs[source_count : source_count + 2]
     out_refs = refs[source_count + 2 : source_count + 2 + dest_count]
-    pbuf, total, held, held_sems = refs[source_count + 2 + dest_count :]
+    wbuf, pbuf, total, held, sems, held_sems = refs[source_count + 2 + dest_count :]
     plane = order_k * order_k
     list_rows = packed.shape[0] - 7
     half = term_count // 2
@@ -309,14 +307,21 @@
     ]
     for load in loads:
         load.start()
+
+    def load_row(ll):
+        for m in range(term_count):
+            column = pl.multiple_of((m * disp_count + ll) * plane, plane)
+            pltpu.make_async_copy(w_hbm.at[:, pl.ds(column, plane)], wbuf.at[ll, m], sems.at[ll]).start()
+
+    for ll in range(AHEAD):
+        load_row(ll)
     total[...] = jnp.zeros_like(total)
     for load in loads:
         load.wait()
 
     def push_w(ll, j, reg):
         for unit in range(2):
-            column = pl.multiple_of(((unit * half + j) * disp_count + ll) * plane, plane)
-            pltpu.matmul_push_rhs(w_ref[:, pl.ds(column, plane)], reg, unit)
+            pltpu.matmul_push_rhs(wbuf[ll, unit * half + j], reg, unit)
 
     def block_body(ll, base, live, slots):
         pl.run_scoped(
@@ -386,6 +391,11 @@
             place(g)
 
     def per_disp(ll, carry):
+        @pl.when(ll + AHEAD < disp_count)
+        def _():
+            load_row(ll + AHEAD)
+
+        pltpu.make_async_copy(wbuf.at[ll], wbuf.at[ll], sems.at[ll]).wait()
         start, stop = packed[list_rows, ll], packed[list_rows, ll + 1]
 
         def per_block(blk, inner):
@@ -420,26 +430,28 @@
     return jnp.stack([parts[p] for p in range(len(parts))], axis=1)
 
 
-def convolve(sources, shifted, held_kernels, packed, dest_count, term_count, order_k):
+def convolve(sources, shifted, yz_kernels, packed, dest_count, term_count, order_k):
     plane = order_k * order_k
     block_boxes = sources[0].shape[0]
-    disp_count = held_kernels.shape[1] // (term_count * plane)
+    disp_count = yz_kernels.shape[1] // (term_count * plane)
     dims = (term_count, order_k, disp_count, len(sources), dest_count)
     tile = jax.ShapeDtypeStruct((block_boxes, order_k, plane), jnp.bfloat16)
     return pl.pallas_call(
         functools.partial(conv_kernel, dims),
         out_shape=[tile] * dest_count,
-        in_specs=[SMEM] + [ANY] * len(sources) + [VMEM, VMEM],
+        in_specs=[SMEM] + [ANY] * len(sources) + [VMEM, ANY],
         out_specs=[VMEM] * dest_count,
         scratch_shapes=[
+            pltpu.VMEM((disp_count, term_count, plane, plane), jnp.bfloat16),
             pltpu.VMEM((BLOCK * term_count * order_k, plane), jnp.bfloat16),
             pltpu.VMEM((dest_count * block_boxes + 1, order_k, plane), jnp.float32),
             pltpu.VMEM((len(sources) * block_boxes, order_k, plane), jnp.bfloat16),
+            pltpu.SemaphoreType.DMA((disp_count,)),
             pltpu.SemaphoreType.DMA((len(sources),)),
         ],
-        compiler_params=pltpu.CompilerParams(vmem_limit_bytes=11 * MIB),
+        compiler_params=pltpu.CompilerParams(vmem_limit_bytes=40 * MIB),
         name="convolve",
-    )(packed, *sources, shifted, held_kernels)
+    )(packed, *sources, shifted, yz_kernels)
 
 
 def flips(count, step):
@@ -512,29 +524,24 @@
     fixed = [pltpu.with_memory_space_constraint(fixed[0], pltpu.VMEM)] + list(fixed[1:])
 
     list_rows = -(-(oct_count * lo_count * box_count * slot_count // LANES + 8) // 8) * 8
-    *lists, moved, held_kernels = pl.pallas_call(
+    *lists, moved = pl.pallas_call(
         functools.partial(route_kernel, (oct_count, hi_count, lo_count, box_count, slot_count, disp_rows)),
         out_shape=[jax.ShapeDtypeStruct((list_rows, LANES), jnp.int32)] * ITERS
         + [
             jax.ShapeDtypeStruct((8, LANES), jnp.int32),
-            pltpu.VMEM(yz_kernels.shape, yz_kernels.dtype),
         ],
-        in_specs=[SMEM, VMEM, ANY],
-        out_specs=[VMEM] * (ITERS + 2),
-        scratch_shapes=[pltpu.SemaphoreType.DMA],
+        in_specs=[SMEM, VMEM],
+        out_specs=[VMEM] * (ITERS + 1),
         compiler_params=pltpu.CompilerParams(vmem_limit_bytes=11 * MIB),
         name="route_slots",
-    )(info, words, yz_kernels)
-    held_kernels = pltpu.with_memory_space_constraint(held_kernels, pltpu.VMEM)
-    lists, send_potential = lax.optimization_barrier((lists, send_potential))
-    moved_potential = lax.all_to_all(send_potential, ("hi", "lo"), 0, 0, tiled=True)
+    )(info, words)
     came_from = moved[1, :box_count] // box_count % sub_count
     shifted = shifted_factors(x_kernels)
 
     for iteration in range(ITERS):
         last = iteration == ITERS - 1
         sources = gather_sources(source, lo_count)
-        outs = convolve(sources, shifted, held_kernels, lists[iteration], hi_count, term_count, order_k)
+        outs = convolve(sources, shifted, yz_kernels, lists[iteration], hi_count, term_count, order_k)
         parts = [outs[0]] + [lax.ppermute(outs[r], "hi", flips(hi_count, r)) for r in range(1, hi_count)]
         kernel = functools.partial(tree_kernel, last, hi_count)
         if last:
@@ -549,6 +556,9 @@
                 name="last_tree",
             )(came_from, *parts, *fixed)
         else:
+            near, send_potential = lax.optimization_barrier((parts[1], send_potential))
+            parts[1] = near
+            moved_potential = lax.all_to_all(send_potential, ("hi", "lo"), 0, 0, tiled=True)
             source = pl.pallas_call(
                 kernel,
                 out_shape=jax.ShapeDtypeStruct(tile, jnp.bfloat16),

time: 164 us -> 147 us (0.90)
  local copies, waits for them, and re-layouts: 29.6 us -> 7.89 us
  waiting for transfers between devices: 31.2 us -> 34.5 us
  starting transfers between devices: 29 us -> 32.1 us
    unnamed x39 -> x33, local copies, waits for them, and re-layouts: 28.2 us -> 6.55 us
    ppermute x6, waiting for transfers between devices: 18.1 us -> 22.8 us  [shards(): lax.ppermute(outs[r], 'hi', flips(hi_count, r))]
    pallas_call x1, Pallas kernels: 8.26 us -> 4 us  [shards(): pl.pallas_call(functools.partial(route_kernel, (oct_count, hi_count, lo_c...]
    ppermute x6, starting transfers between devices: 9.12 us -> 12.4 us  [shards(): lax.ppermute(outs[r], 'hi', flips(hi_count, r))]
    pallas_call x2, Pallas kernels: 36.3 us -> 39 us  [convolve(): pl.pallas_call(functools.partial(conv_kernel, dims), out_shape=[tile] * d...]
  transfers between devices with their start and end apart: 22 -> 22, of which waited for: 9 -> 10; matrix products, arithmetic and copies ran while one was open for 1% -> 1% of each run, Pallas kernels for 16% -> 3%
where the time goes in v3:
time: 147 us
  Pallas kernels  57.5 us (39%)
  waiting for transfers between devices  34.5 us (23%)
  starting transfers between devices  32.1 us (22%)
  blocking collectives  13.8 us (9%)
  local copies, waits for them, and re-layouts  7.89 us (5%)
    pallas_call x2, Pallas kernels, convolve(): pl.pallas_call(functools.partial(conv_kernel, dims), out_shape=[tile] * d...  39 us
    ppermute x6, waiting for transfers between devices, shards(): lax.ppermute(outs[r], 'hi', flips(hi_count, r))  22.8 us
    all_to_all x1, blocking collectives, shards(): returned = lax.all_to_all(fields, ('hi', 'lo'), 0, 0, tiled=True)  13.8 us
    ppermute x6, starting transfers between devices, shards(): lax.ppermute(outs[r], 'hi', flips(hi_count, r))  12.4 us
    ppermute x6, starting transfers between devices, gather_sources(): lax.ppermute(source, 'lo', flips(lo_count, r))  7.56 us
    unnamed x33, local copies, waits for them, and re-layouts  6.55 us
    all_to_all x1, starting transfers between devices, shards(): words = lax.all_to_all(words, ('oct', 'hi', 'lo'), 0, 0, tiled=True)  6.26 us
    all_to_all x1, waiting for transfers between devices, shards(): words = lax.all_to_all(words, ('oct', 'hi', 'lo'), 0, 0, tiled=True)  5.4 us
  transfers between devices with their start and end apart: 22, of which 10 were waited for; matrix products, arithmetic and copies ran while one was open for 1% of the time, Pallas kernels for 3%

profile of v3, /device:TPU:0, one launch (start us, length us, event | category | flops | bytes accessed | tf_op | source)
XLA Modules:
  0.0 147.2 jit_solution(4594477414803862829)
XLA Ops:
  0.7 1.6 %pack_tables.1 = s32[32,8,128]{2,1,0:T(8,128)} custom-call(s32[16]{0:T(128)} %parent_of.5, s32[16]{0:T(128)} %octant.1, s32[16,16]{1,0:T(8,128)} %disp_ref.1, s32[16,16]{1,0:T(8,128)} %dest_ref.1), custom_call_target="tpu_custom_call" | custom-call | tf_op jit(solution)/shard_map/pack_tables/pallas_call | solution.py:491
  2.3 3.3 %first_source.1 = (bf16[16,16,256]{2,1,0:T(8,128)(2,1)}, bf16[16,16,256]{2,1,0:T(8,128)(2,1)}) custom-call(s32[16]{0:T(128)} %parent_of.5, f32[16,4096]{1,0:T(8,128)} %coef_ref, f32[16,4096]{1,0:T(8,128)} %pot_ref.1, f32[16,16]{1,0:T(8,128)} %to_ref.2), custom_call_target="tpu_custom_call" | custom-call | tf_op jit(solution)/shard_map/first_source/pallas_call | solution.py:501
  5.6 0.5 collective-permute-start.3
  6.0 3.4 %collective-permute-start.2 = (bf16[16,16,256]{2,1,0:T(8,128)(2,1)}, bf16[16,16,256]{2,1,0:T(8,128)(2,1)S(1)}, u32[]{:S(2)}, u32[]{:S(2)}) collective-permute-start(bf16[16,16,256]{2,1,0:T(8,128)(2,1)} %get-tuple-element.32.refs_0_), channel_id=1, source_target_pairs={{0,3},{1,2},{2,1},{3,0},{4,7},{5,6},{6,5},{7,4},{8,11},{9,10},{10,... | collective-permute-start | bytes 393224 | tf_op jit(solution)/shard_map/ppermute | solution.py:462
  9.5 0.5 collective-permute-start.1
  10.1 6.3 %all-to-all-start = ((s32[32,8,128]{2,1,0:T(8,128)}), s32[32,8,128]{2,1,0:T(8,128)S(1)}, u32[]{:S(2)}, u32[]{:S(2)}) async-start(s32[32,8,128]{2,1,0:T(8,128)} %pack_tables.1), calls=%async_computation | async-start | bytes 262144 | tf_op jit(solution)/shard_map/all_to_all | solution.py:499
  16.4 1.1 copy.27
  17.9 0.3 collective-permute-start.6
  18.2 0.3 collective-permute-start.5
  18.5 0.3 collective-permute-start.4
  18.9 5.4 %all-to-all-done.words_ref = s32[32,8,128]{2,1,0:T(8,128)S(1)} async-done(((s32[32,8,128]{2,1,0:T(8,128)}), s32[32,8,128]{2,1,0:T(8,128)S(1)}, u32[]{:S(2)}, u32[]{:S(2)}) %all-to-all-start) | async-done | bytes 131104 | tf_op jit(solution)/shard_map/all_to_all | solution.py:499
  24.3 4.0 %route_slots.1 = (s32[24,128]{1,0:T(8,128)S(1)}, s32[24,128]{1,0:T(8,128)S(1)}, s32[8,128]{1,0:T(8,128)S(1)}) custom-call(s32[3]{0:T(128)S(1)} %pad_add_fusion.info, s32[32,8,128]{2,1,0:T(8,128)S(1)} %all-to-all-done.words_ref), custom_call_target="tpu_custom_call" | custom-call | tf_op jit(solution)/shard_map/route_slots/pallas_call | solution.py:527
  28.3 0.9 copy-done.1
  29.2 20.2 %convolve.2 = (bf16[16,16,256]{2,1,0:T(8,128)(2,1)S(1)}, bf16[16,16,256]{2,1,0:T(8,128)(2,1)S(1)}, bf16[16,16,256]{2,1,0:T(8,128)(2,1)S(1)}, bf16[16,16,256]{2,1,0:T(8,128)(2,1)S(1)}) custom-call(s32[24,128]{1,0:T(8,128)S(1)} %get-tuple-element.29.packed, bf16[16,16,256]{2,1,0:T(8,128)(2,1)S(1)} %copy-done.1, ...), custom_call_target="tpu_custom_call" | custom-call | tf_op jit(solution)/shard_map/convolve/pallas_call | solution.py:439
  49.4 0.6 copy-done.3
  50.1 0.6 copy-done.8
  50.7 0.5 collective-permute-start.7
  51.2 4.5 %collective-permute-done.7.refs_1_ = bf16[16,16,256]{2,1,0:T(8,128)(2,1)S(1)} collective-permute-done((bf16[16,16,256]{2,1,0:T(8,128)(2,1)S(1)}, bf16[16,16,256]{2,1,0:T(8,128)(2,1)S(1)}, u32[]{:S(2)}, u32[]{:S(2)}) %collective-permute-start.7) | collective-permute-done | bytes 131104 | tf_op jit(solution)/shard_map/ppermute | solution.py:545
  55.7 0.7 copy-done.9
  56.4 4.2 %all-to-all-start.1 = ((bf16[16,16,256]{2,1,0:T(8,128)(2,1)}), bf16[16,16,256]{2,1,0:T(8,128)(2,1)}, u32[]{:S(2)}, u32[]{:S(2)}) async-start(bf16[16,16,256]{2,1,0:T(8,128)(2,1)} %get-tuple-element.43), calls=%async_computation.1 | async-start | bytes 262144 | tf_op jit(solution)/shard_map/all_to_all | solution.py:561
  60.6 0.9 make_constants.1
  61.5 0.6 copy-done.2
  62.1 0.6 copy-done.5
  62.7 2.7 %collective-permute-start.8 = (bf16[16,16,256]{2,1,0:T(8,128)(2,1)}, bf16[16,16,256]{2,1,0:T(8,128)(2,1)}, u32[]{:S(2)}, u32[]{:S(2)}) collective-permute-start(bf16[16,16,256]{2,1,0:T(8,128)(2,1)} %copy-done.8), channel_id=1, source_target_pairs={{0,8},{4,12},{8,0},{12,4},{1,9},{5,13},{9,1},{13,5},{2,10},{6,14},... | collective-permute-start | bytes 393224 | tf_op jit(solution)/shard_map/ppermute | solution.py:545
  65.4 1.4 collective-permute-start.9
  66.8 0.5 and_select_fusion.came_from
  67.4 8.4 %collective-permute-done.8.refs_2_ = bf16[16,16,256]{2,1,0:T(8,128)(2,1)} collective-permute-done((bf16[16,16,256]{2,1,0:T(8,128)(2,1)}, bf16[16,16,256]{2,1,0:T(8,128)(2,1)}, u32[]{:S(2)}, u32[]{:S(2)}) %collective-permute-start.8) | collective-permute-done | bytes 131104 | tf_op jit(solution)/shard_map/ppermute | solution.py:545
  75.8 4.1 %tree_source.1.refs_0_ = bf16[16,16,256]{2,1,0:T(8,128)(2,1)} custom-call(s32[16]{0:T(128)} %and_select_fusion.came_from, bf16[16,16,256]{2,1,0:T(8,128)(2,1)} %copy-done.3, bf16[16,16,256]{2,1,0:T(8,128)(2,1)} %copy-done.9, bf16[16,16,256]{2,1,0:T(8,128)(2,1)} %collective-permute-done.8.refs_2_, bf16[16,16,256]{2,1,0:T(8,128)(2,1)} %collective-permute-done.9.refs_3_, ...), custom_call_target="tpu_custom_call" | custom-call | tf_op jit(solution)/shard_map/tree_source/pallas_call | solution.py:562
  79.9 2.3 %collective-permute-start.12 = (bf16[16,16,256]{2,1,0:T(8,128)(2,1)}, bf16[16,16,256]{2,1,0:T(8,128)(2,1)S(1)}, u32[]{:S(2)}, u32[]{:S(2)}) collective-permute-start(bf16[16,16,256]{2,1,0:T(8,128)(2,1)} %tree_source.1.refs_0_), channel_id=1, source_target_pairs={{0,3},{1,2},{2,1},{3,0},{4,7},{5,6},{6,5},{7,4},{8,11},{9,10},{10,... | collective-permute-start | bytes 393224 | tf_op jit(solution)/shard_map/ppermute | solution.py:462
  82.2 0.6 collective-permute-start.11
  82.8 0.5 collective-permute-start.10
  83.4 3.2 %collective-permute-done.12.refs_3_ = bf16[16,16,256]{2,1,0:T(8,128)(2,1)S(1)} collective-permute-done((bf16[16,16,256]{2,1,0:T(8,128)(2,1)}, bf16[16,16,256]{2,1,0:T(8,128)(2,1)S(1)}, u32[]{:S(2)}, u32[]{:S(2)}) %collective-permute-start.12) | collective-permute-done | bytes 131104 | tf_op jit(solution)/shard_map/ppermute | solution.py:462
  86.6 2.0 %collective-permute-done.11.refs_2_ = bf16[16,16,256]{2,1,0:T(8,128)(2,1)S(1)} collective-permute-done((bf16[16,16,256]{2,1,0:T(8,128)(2,1)}, bf16[16,16,256]{2,1,0:T(8,128)(2,1)S(1)}, u32[]{:S(2)}, u32[]{:S(2)}) %collective-permute-start.11) | collective-permute-done | bytes 131104 | tf_op jit(solution)/shard_map/ppermute | solution.py:462
  88.6 0.5 collective-permute-start.14
  89.1 0.8 collective-permute-done.15.refs_6_
  89.9 0.2 collective-permute-done.14.refs_5_
  90.1 0.9 copy-done
  91.0 18.8 %convolve.3 = (bf16[16,16,256]{2,1,0:T(8,128)(2,1)S(1)}, bf16[16,16,256]{2,1,0:T(8,128)(2,1)S(1)}, bf16[16,16,256]{2,1,0:T(8,128)(2,1)S(1)}, bf16[16,16,256]{2,1,0:T(8,128)(2,1)S(1)}) custom-call(s32[24,128]{1,0:T(8,128)S(1)} %get-tuple-element.28.packed, bf16[16,16,256]{2,1,0:T(8,128)(2,1)S(1)} %copy-done, ...), custom_call_target="tpu_custom_call" | custom-call | tf_op jit(solution)/shard_map/convolve/pallas_call | solution.py:439
  109.8 0.6 copy-done.4
  110.4 4.0 %collective-permute-start.17 = (bf16[16,16,256]{2,1,0:T(8,128)(2,1)S(1)}, bf16[16,16,256]{2,1,0:T(8,128)(2,1)S(1)}, u32[]{:S(2)}, u32[]{:S(2)}) collective-permute-start(bf16[16,16,256]{2,1,0:T(8,128)(2,1)S(1)} %get-tuple-element.45), channel_id=1, source_target_pairs={{0,4},{4,0},{8,12},{12,8},{1,5},{5,1},{9,13},{13,9},{2,6},{6,2},{1... | collective-permute-start | bytes 393224 | tf_op jit(solution)/shard_map/ppermute | solution.py:545
  114.4 2.4 %collective-permute-start.18 = (bf16[16,16,256]{2,1,0:T(8,128)(2,1)S(1)}, bf16[16,16,256]{2,1,0:T(8,128)(2,1)S(1)}, u32[]{:S(2)}, u32[]{:S(2)}) collective-permute-start(bf16[16,16,256]{2,1,0:T(8,128)(2,1)S(1)} %get-tuple-element.46), channel_id=1, source_target_pairs={{0,8},{4,12},{8,0},{12,4},{1,9},{5,13},{9,1},{13,5},{2,10},{6,14},... | collective-permute-start | bytes 393224 | tf_op jit(solution)/shard_map/ppermute | solution.py:545
  116.8 1.5 collective-permute-start.19
  118.3 3.1 %collective-permute-done.17.refs_1_ = bf16[16,16,256]{2,1,0:T(8,128)(2,1)S(1)} collective-permute-done((bf16[16,16,256]{2,1,0:T(8,128)(2,1)S(1)}, bf16[16,16,256]{2,1,0:T(8,128)(2,1)S(1)}, u32[]{:S(2)}, u32[]{:S(2)}) %collective-permute-start.17) | collective-permute-done | bytes 131104 | tf_op jit(solution)/shard_map/ppermute | solution.py:545
  121.5 6.7 %collective-permute-done.19.refs_3_ = bf16[16,16,256]{2,1,0:T(8,128)(2,1)S(1)} collective-permute-done((bf16[16,16,256]{2,1,0:T(8,128)(2,1)S(1)}, bf16[16,16,256]{2,1,0:T(8,128)(2,1)S(1)}, u32[]{:S(2)}, u32[]{:S(2)}) %collective-permute-start.19) | collective-permute-done | bytes 131104 | tf_op jit(solution)/shard_map/ppermute | solution.py:545
  128.2 0.6 copy-done.12
  128.9 2.8 %last_tree.1 = (bf16[16,16,256]{2,1,0:T(8,128)(2,1)}, f32[2,4096]{1,0:T(2,128)}) custom-call(s32[16]{0:T(128)} %and_select_fusion.came_from, bf16[16,16,256]{2,1,0:T(8,128)(2,1)} %copy-done.4, bf16[16,16,256]{2,1,0:T(8,128)(2,1)} %copy-done.10, bf16[16,16,256]{2,1,0:T(8,128)(2,1)} %copy-done.11, bf16[16,16,256]{2,1,0:T(8,128)(2,1)} %copy-done.12, ...), custom_call_target="tpu_custom_call" | custom-call | tf_op jit(solution)/shard_map/last_tree/pallas_call | solution.py:548
  131.6 13.8 %all_to_all.15.field_ref = bf16[16,16,256]{2,1,0:T(8,128)(2,1)} all-to-all(bf16[16,16,256]{2,1,0:T(8,128)(2,1)} %get-tuple-element.48), channel_id=1, replica_groups=mesh['oct'=2,'hi'=4,'lo'=4] {'hi','lo'}, dimensions={0} | all-to-all | bytes 262144 | tf_op jit(solution)/shard_map/all_to_all | solution.py:569
  145.4 1.8 %unpack_fields.1 = f32[16,4096]{1,0:T(8,128)} custom-call(s32[16]{0:T(128)} %parent_of.5, bf16[16,16,256]{2,1,0:T(8,128)(2,1)} %all_to_all.15.field_ref), custom_call_target="tpu_custom_call" | custom-call | tf_op jit(solution)/shard_map/unpack_fields/pallas_call | solution.py:570
  (44 shorter events, 1.0 us)
Async XLA Ops:
  0.6 59.9 %copy-start.6 = (f32[16,16]{1,0:T(8,128)S(1)}, f32[16,16]{1,0:T(8,128)}, u32[]{:S(2)}) copy-start(f32[16,16]{1,0:T(8,128)} %to_ref.2) | copy-start | bytes 3076
  0.6 59.9 %copy-start.7 = (f32[2,16,16]{2,1,0:T(8,128)S(1)}, f32[2,16,16]{2,1,0:T(8,128)}, u32[]{:S(2)}) copy-start(f32[2,16,16]{2,1,0:T(8,128)} %two_ref.1) | copy-start | bytes 6148
  5.6 22.7 %collective-permute-start.3 = (bf16[16,16,256]{2,1,0:T(8,128)(2,1)}, bf16[16,16,256]{2,1,0:T(8,128)(2,1)S(1)}, u32[]{:S(2)}, u32[]{:S(2)}) collective-permute-start(bf16[16,16,256]{2,1,0:T(8,128)(2,1)} %get-tuple-element.32.refs_0_), channel_id=1, source_target_pairs={{0,16},{16,0},{1,17},{17,1},{2,18},{18,2},{3,19},{19,3},{4,20},{20... | collective-permute-start | bytes 393224 | tf_op jit(solution)/shard_map/ppermute | solution.py:463
  6.0 11.9 %collective-permute-start.2 = (bf16[16,16,256]{2,1,0:T(8,128)(2,1)}, bf16[16,16,256]{2,1,0:T(8,128)(2,1)S(1)}, u32[]{:S(2)}, u32[]{:S(2)}) collective-permute-start(bf16[16,16,256]{2,1,0:T(8,128)(2,1)} %get-tuple-element.32.refs_0_), channel_id=1, source_target_pairs={{0,3},{1,2},{2,1},{3,0},{4,7},{5,6},{6,5},{7,4},{8,11},{9,10},{10,... | collective-permute-start | bytes 393224 | tf_op jit(solution)/shard_map/ppermute | solution.py:462
  9.5 8.7 %collective-permute-start.1 = (bf16[16,16,256]{2,1,0:T(8,128)(2,1)}, bf16[16,16,256]{2,1,0:T(8,128)(2,1)S(1)}, u32[]{:S(2)}, u32[]{:S(2)}) collective-permute-start(bf16[16,16,256]{2,1,0:T(8,128)(2,1)} %get-tuple-element.32.refs_0_), channel_id=1, source_target_pairs={{0,2},{1,3},{2,0},{3,1},{4,6},{5,7},{6,4},{7,5},{8,10},{9,11},{10,... | collective-permute-start | bytes 393224 | tf_op jit(solution)/shard_map/ppermute | solution.py:462
  10.0 8.5 %collective-permute-start = (bf16[16,16,256]{2,1,0:T(8,128)(2,1)}, bf16[16,16,256]{2,1,0:T(8,128)(2,1)S(1)}, u32[]{:S(2)}, u32[]{:S(2)}) collective-permute-start(bf16[16,16,256]{2,1,0:T(8,128)(2,1)} %get-tuple-element.32.refs_0_), channel_id=1, source_target_pairs={{0,1},{1,0},{2,3},{3,2},{4,5},{5,4},{6,7},{7,6},{8,9},{9,8},{10,11... | collective-permute-start | bytes 393224 | tf_op jit(solution)/shard_map/ppermute | solution.py:462
  10.1 14.2 %all-to-all-start = ((s32[32,8,128]{2,1,0:T(8,128)}), s32[32,8,128]{2,1,0:T(8,128)S(1)}, u32[]{:S(2)}, u32[]{:S(2)}) async-start(s32[32,8,128]{2,1,0:T(8,128)} %pack_tables.1), calls=%async_computation | async-start | bytes 262144 | tf_op jit(solution)/shard_map/all_to_all | solution.py:499
  17.9 10.4 %collective-permute-start.6 = (bf16[16,16,256]{2,1,0:T(8,128)(2,1)S(1)}, bf16[16,16,256]{2,1,0:T(8,128)(2,1)S(1)}, u32[]{:S(2)}, u32[]{:S(2)}) collective-permute-start(bf16[16,16,256]{2,1,0:T(8,128)(2,1)S(1)} %collective-permute-done.2.refs_3_), channel_id=1, source_target_pairs={{0,16},{16,0},{1,17},{17,1},{2,18},{18,2},{3,19},{19,3},{4,20},{20... | collective-permute-start | bytes 393224 | tf_op jit(solution)/shard_map/ppermute | solution.py:463
  18.2 10.1 %collective-permute-start.5 = (bf16[16,16,256]{2,1,0:T(8,128)(2,1)S(1)}, bf16[16,16,256]{2,1,0:T(8,128)(2,1)S(1)}, u32[]{:S(2)}, u32[]{:S(2)}) collective-permute-start(bf16[16,16,256]{2,1,0:T(8,128)(2,1)S(1)} %collective-permute-done.1.refs_2_), channel_id=1, source_target_pairs={{0,16},{16,0},{1,17},{17,1},{2,18},{18,2},{3,19},{19,3},{4,20},{20... | collective-permute-start | bytes 393224 | tf_op jit(solution)/shard_map/ppermute | solution.py:463
  18.5 9.8 %collective-permute-start.4 = (bf16[16,16,256]{2,1,0:T(8,128)(2,1)S(1)}, bf16[16,16,256]{2,1,0:T(8,128)(2,1)S(1)}, u32[]{:S(2)}, u32[]{:S(2)}) collective-permute-start(bf16[16,16,256]{2,1,0:T(8,128)(2,1)S(1)} %collective-permute-done.refs_1_), channel_id=1, source_target_pairs={{0,16},{16,0},{1,17},{17,1},{2,18},{18,2},{3,19},{19,3},{4,20},{20... | collective-permute-start | bytes 393224 | tf_op jit(solution)/shard_map/ppermute | solution.py:463
  28.3 0.9 copy-start.1
  49.4 0.7 copy-start.3
  50.1 0.6 copy-start.8
  50.7 5.0 %collective-permute-start.7 = (bf16[16,16,256]{2,1,0:T(8,128)(2,1)S(1)}, bf16[16,16,256]{2,1,0:T(8,128)(2,1)S(1)}, u32[]{:S(2)}, u32[]{:S(2)}) collective-permute-start(bf16[16,16,256]{2,1,0:T(8,128)(2,1)S(1)} %get-tuple-element.34), channel_id=1, source_target_pairs={{0,4},{4,0},{8,12},{12,8},{1,5},{5,1},{9,13},{13,9},{2,6},{6,2},{1... | collective-permute-start | bytes 393224 | tf_op jit(solution)/shard_map/ppermute | solution.py:545
  55.7 0.7 copy-start.9
  56.4 19.4 %all-to-all-start.1 = ((bf16[16,16,256]{2,1,0:T(8,128)(2,1)}), bf16[16,16,256]{2,1,0:T(8,128)(2,1)}, u32[]{:S(2)}, u32[]{:S(2)}) async-start(bf16[16,16,256]{2,1,0:T(8,128)(2,1)} %get-tuple-element.43), calls=%async_computation.1 | async-start | bytes 262144 | tf_op jit(solution)/shard_map/all_to_all | solution.py:561
  61.5 0.6 copy-start.2
  62.1 0.6 copy-start.5
  62.7 13.0 %collective-permute-start.8 = (bf16[16,16,256]{2,1,0:T(8,128)(2,1)}, bf16[16,16,256]{2,1,0:T(8,128)(2,1)}, u32[]{:S(2)}, u32[]{:S(2)}) collective-permute-start(bf16[16,16,256]{2,1,0:T(8,128)(2,1)} %copy-done.8), channel_id=1, source_target_pairs={{0,8},{4,12},{8,0},{12,4},{1,9},{5,13},{9,1},{13,5},{2,10},{6,14},... | collective-permute-start | bytes 393224 | tf_op jit(solution)/shard_map/ppermute | solution.py:545
  65.4 10.3 %collective-permute-start.9 = (bf16[16,16,256]{2,1,0:T(8,128)(2,1)S(1)}, bf16[16,16,256]{2,1,0:T(8,128)(2,1)}, u32[]{:S(2)}, u32[]{:S(2)}) collective-permute-start(bf16[16,16,256]{2,1,0:T(8,128)(2,1)S(1)} %get-tuple-element.38), channel_id=1, source_target_pairs={{0,12},{4,8},{8,4},{12,0},{1,13},{5,9},{9,5},{13,1},{2,14},{6,10},... | collective-permute-start | bytes 393224 | tf_op jit(solution)/shard_map/ppermute | solution.py:545
  79.9 6.7 %collective-permute-start.12 = (bf16[16,16,256]{2,1,0:T(8,128)(2,1)}, bf16[16,16,256]{2,1,0:T(8,128)(2,1)S(1)}, u32[]{:S(2)}, u32[]{:S(2)}) collective-permute-start(bf16[16,16,256]{2,1,0:T(8,128)(2,1)} %tree_source.1.refs_0_), channel_id=1, source_target_pairs={{0,3},{1,2},{2,1},{3,0},{4,7},{5,6},{6,5},{7,4},{8,11},{9,10},{10,... | collective-permute-start | bytes 393224 | tf_op jit(solution)/shard_map/ppermute | solution.py:462
  82.2 6.4 %collective-permute-start.11 = (bf16[16,16,256]{2,1,0:T(8,128)(2,1)}, bf16[16,16,256]{2,1,0:T(8,128)(2,1)S(1)}, u32[]{:S(2)}, u32[]{:S(2)}) collective-permute-start(bf16[16,16,256]{2,1,0:T(8,128)(2,1)} %tree_source.1.refs_0_), channel_id=1, source_target_pairs={{0,2},{1,3},{2,0},{3,1},{4,6},{5,7},{6,4},{7,5},{8,10},{9,11},{10,... | collective-permute-start | bytes 393224 | tf_op jit(solution)/shard_map/ppermute | solution.py:462
  82.8 5.8 %collective-permute-start.10 = (bf16[16,16,256]{2,1,0:T(8,128)(2,1)}, bf16[16,16,256]{2,1,0:T(8,128)(2,1)S(1)}, u32[]{:S(2)}, u32[]{:S(2)}) collective-permute-start(bf16[16,16,256]{2,1,0:T(8,128)(2,1)} %tree_source.1.refs_0_), channel_id=1, source_target_pairs={{0,1},{1,0},{2,3},{3,2},{4,5},{5,4},{6,7},{7,6},{8,9},{9,8},{10,11... | collective-permute-start | bytes 393224 | tf_op jit(solution)/shard_map/ppermute | solution.py:462
  83.4 5.7 %collective-permute-start.13 = (bf16[16,16,256]{2,1,0:T(8,128)(2,1)}, bf16[16,16,256]{2,1,0:T(8,128)(2,1)S(1)}, u32[]{:S(2)}, u32[]{:S(2)}) collective-permute-start(bf16[16,16,256]{2,1,0:T(8,128)(2,1)} %tree_source.1.refs_0_), channel_id=1, source_target_pairs={{0,16},{16,0},{1,17},{17,1},{2,18},{18,2},{3,19},{19,3},{4,20},{20... | collective-permute-start | bytes 393224 | tf_op jit(solution)/shard_map/ppermute | solution.py:463
  86.6 2.5 %collective-permute-start.16 = (bf16[16,16,256]{2,1,0:T(8,128)(2,1)S(1)}, bf16[16,16,256]{2,1,0:T(8,128)(2,1)S(1)}, u32[]{:S(2)}, u32[]{:S(2)}) collective-permute-start(bf16[16,16,256]{2,1,0:T(8,128)(2,1)S(1)} %collective-permute-done.12.refs_3_), channel_id=1, source_target_pairs={{0,16},{16,0},{1,17},{17,1},{2,18},{18,2},{3,19},{19,3},{4,20},{20... | collective-permute-start | bytes 393224 | tf_op jit(solution)/shard_map/ppermute | solution.py:463
  88.6 1.3 collective-permute-start.15
  88.6 1.5 %collective-permute-start.14 = (bf16[16,16,256]{2,1,0:T(8,128)(2,1)S(1)}, bf16[16,16,256]{2,1,0:T(8,128)(2,1)S(1)}, u32[]{:S(2)}, u32[]{:S(2)}) collective-permute-start(bf16[16,16,256]{2,1,0:T(8,128)(2,1)S(1)} %collective-permute-done.10.refs_1_), channel_id=1, source_target_pairs={{0,16},{16,0},{1,17},{17,1},{2,18},{18,2},{3,19},{19,3},{4,20},{20... | collective-permute-start | bytes 393224 | tf_op jit(solution)/shard_map/ppermute | solution.py:463
  90.1 0.9 copy-start
  109.8 0.7 copy-start.4
  110.4 10.9 %collective-permute-start.17 = (bf16[16,16,256]{2,1,0:T(8,128)(2,1)S(1)}, bf16[16,16,256]{2,1,0:T(8,128)(2,1)S(1)}, u32[]{:S(2)}, u32[]{:S(2)}) collective-permute-start(bf16[16,16,256]{2,1,0:T(8,128)(2,1)S(1)} %get-tuple-element.45), channel_id=1, source_target_pairs={{0,4},{4,0},{8,12},{12,8},{1,5},{5,1},{9,13},{13,9},{2,6},{6,2},{1... | collective-permute-start | bytes 393224 | tf_op jit(solution)/shard_map/ppermute | solution.py:545
  114.4 7.1 %collective-permute-start.18 = (bf16[16,16,256]{2,1,0:T(8,128)(2,1)S(1)}, bf16[16,16,256]{2,1,0:T(8,128)(2,1)S(1)}, u32[]{:S(2)}, u32[]{:S(2)}) collective-permute-start(bf16[16,16,256]{2,1,0:T(8,128)(2,1)S(1)} %get-tuple-element.46), channel_id=1, source_target_pairs={{0,8},{4,12},{8,0},{12,4},{1,9},{5,13},{9,1},{13,5},{2,10},{6,14},... | collective-permute-start | bytes 393224 | tf_op jit(solution)/shard_map/ppermute | solution.py:545
  116.8 11.4 %collective-permute-start.19 = (bf16[16,16,256]{2,1,0:T(8,128)(2,1)S(1)}, bf16[16,16,256]{2,1,0:T(8,128)(2,1)S(1)}, u32[]{:S(2)}, u32[]{:S(2)}) collective-permute-start(bf16[16,16,256]{2,1,0:T(8,128)(2,1)S(1)} %get-tuple-element.47), channel_id=1, source_target_pairs={{0,12},{4,8},{8,4},{12,0},{1,13},{5,9},{9,5},{13,1},{2,14},{6,10},... | collective-permute-start | bytes 393224 | tf_op jit(solution)/shard_map/ppermute | solution.py:545
  121.4 7.5 %copy-start.10 = (bf16[16,16,256]{2,1,0:T(8,128)(2,1)}, bf16[16,16,256]{2,1,0:T(8,128)(2,1)S(1)}, u32[]{:S(2)}) copy-start(bf16[16,16,256]{2,1,0:T(8,128)(2,1)S(1)} %collective-permute-done.17.refs_1_) | copy-start | bytes 393220
  121.5 7.4 %copy-start.11 = (bf16[16,16,256]{2,1,0:T(8,128)(2,1)}, bf16[16,16,256]{2,1,0:T(8,128)(2,1)S(1)}, u32[]{:S(2)}) copy-start(bf16[16,16,256]{2,1,0:T(8,128)(2,1)S(1)} %collective-permute-done.18.refs_2_) | copy-start | bytes 393220
  128.2 0.7 copy-start.12

commit v4 on v3

--- a/solution.py
+++ b/solution.py
@@ -10,7 +10,6 @@
 
 ITERS = 2
 BLOCK = 32
-AHEAD = 3
 GROUP = 4
 LANES = 128
 MIB = 1024 * 1024
@@ -118,9 +117,8 @@
     pot_out[...] = rows_ref[...].astype(jnp.bfloat16)
 
 
-def route_kernel(dims, info, words_ref, *refs):
+def route_kernel(dims, first, info, words_ref, *refs):
     oct_count, hi_count, lo_count, boxes, slots, disp_rows = dims
-    list_refs, moved_ref = refs[:ITERS], refs[ITERS]
     oct_here, hi_here, lo_here = info[0], info[1], info[2]
     width = LANES // 2
     words = words_ref[...].reshape(-1, LANES)
@@ -149,54 +147,56 @@
     target = device * boxes + lane % boxes
     dest_rows = hi_count * boxes
     source = iota((slots, lanes), 1)
-    list_rows = list_refs[0].shape[0]
+    list_ref = refs[0] if first else refs[1]
+    list_rows = list_ref.shape[0]
     upper = (iota((lanes, lanes), 0) < iota((lanes, lanes), 1)).astype(jnp.float32).astype(jnp.bfloat16)
     ones = jnp.ones((lanes, lanes), jnp.bfloat16)
     ranks = disp_rows * slots
     lower = (iota((ranks, ranks), 1) < iota((ranks, ranks), 0)).astype(jnp.float32).astype(jnp.bfloat16)
-    for it in range(ITERS):
-        found = look((id_col if it == 0 else place_col) == target)
-        if it == 1:
-            moved_ref[...] = found[slots : slots + 8]
-        entry = found[:slots] - 1
-        dest = jnp.where(entry >= 0, entry // 32, -1)
-        disp = jnp.maximum(entry, 0) % 32
-        place = jnp.concatenate(
-            [look(id_col == dest[s : s + 1])[slots : slots + 1] for s in range(slots)], axis=0
+    if first:
+        found = look(id_col == target)
+        refs[1][...] = look(place_col == target)[: slots + 8]
+    else:
+        found = refs[0][...]
+    entry = found[:slots] - 1
+    dest = jnp.where(entry >= 0, entry // 32, -1)
+    disp = jnp.maximum(entry, 0) % 32
+    place = jnp.concatenate(
+        [look(id_col == dest[s : s + 1])[slots : slots + 1] for s in range(slots)], axis=0
+    )
+    owner = place // boxes
+    keep = (entry >= 0) & (owner // (hi_count * lo_count) == oct_here) & (owner % lo_count == lo_here)
+    away = ((owner // lo_count) % hi_count) ^ hi_here
+    shift = jnp.zeros_like(disp)
+    for c in range(1, 3):
+        shift += (disp >= c * disp_rows).astype(jnp.int32)
+    row = disp - shift * disp_rows
+    member_of = [keep & (row == g) for g in range(disp_rows)]
+    marks = jnp.concatenate(member_of, axis=0).astype(jnp.float32).astype(jnp.bfloat16)
+    sums = dot16(marks, ones)
+    starts = dot16(lower, sums.astype(jnp.bfloat16))
+    ordinal = (starts + dot16(marks, upper)).astype(jnp.int32)
+    position = jnp.full((slots, lanes), -1, jnp.int32)
+    for g in range(disp_rows):
+        position = jnp.where(member_of[g], ordinal[g * slots : (g + 1) * slots], position)
+    code = (source * 4 + shift) * dest_rows + away * boxes + place % boxes
+    pieces = [((code // 256**n) % 256).astype(jnp.float32) for n in range(3)]
+    listed = jnp.zeros((3 * list_rows, LANES), jnp.float32)
+    for s in range(slots):
+        spot = position[s : s + 1]
+        in_row = (spot // LANES == iota((list_rows, lanes), 0)) & (spot >= 0)
+        left = jnp.concatenate([jnp.where(in_row, piece[s : s + 1], 0.0) for piece in pieces], axis=0)
+        in_lane = (spot % LANES == iota((LANES, lanes), 0)).astype(jnp.float32).astype(jnp.bfloat16)
+        listed += lax.dot_general(
+            left.astype(jnp.bfloat16), in_lane, (((1,), (1,)), ((), ())), preferred_element_type=jnp.float32
         )
-        owner = place // boxes
-        keep = (entry >= 0) & (owner // (hi_count * lo_count) == oct_here) & (owner % lo_count == lo_here)
-        away = ((owner // lo_count) % hi_count) ^ hi_here
-        shift = jnp.zeros_like(disp)
-        for c in range(1, 3):
-            shift += (disp >= c * disp_rows).astype(jnp.int32)
-        row = disp - shift * disp_rows
-        member_of = [keep & (row == g) for g in range(disp_rows)]
-        marks = jnp.concatenate(member_of, axis=0).astype(jnp.float32).astype(jnp.bfloat16)
-        sums = dot16(marks, ones)
-        starts = dot16(lower, sums.astype(jnp.bfloat16))
-        ordinal = (starts + dot16(marks, upper)).astype(jnp.int32)
-        position = jnp.full((slots, lanes), -1, jnp.int32)
-        for g in range(disp_rows):
-            position = jnp.where(member_of[g], ordinal[g * slots : (g + 1) * slots], position)
-        code = (source * 4 + shift) * dest_rows + away * boxes + place % boxes
-        pieces = [((code // 256**n) % 256).astype(jnp.float32) for n in range(3)]
-        listed = jnp.zeros((3 * list_rows, LANES), jnp.float32)
-        for s in range(slots):
-            spot = position[s : s + 1]
-            in_row = (spot // LANES == iota((list_rows, lanes), 0)) & (spot >= 0)
-            left = jnp.concatenate([jnp.where(in_row, piece[s : s + 1], 0.0) for piece in pieces], axis=0)
-            in_lane = (spot % LANES == iota((LANES, lanes), 0)).astype(jnp.float32).astype(jnp.bfloat16)
-            listed += lax.dot_general(
-                left.astype(jnp.bfloat16), in_lane, (((1,), (1,)), ((), ())), preferred_element_type=jnp.float32
-            )
-        packed = sum(
-            listed[n * list_rows : (n + 1) * list_rows].astype(jnp.int32) * 256**n for n in range(3)
-        )
-        bound = (starts[ranks - 1 : ranks] + sums[ranks - 1 : ranks]).astype(jnp.int32)
-        for g in range(disp_rows):
-            bound = jnp.where(lane == g, starts[g * slots : g * slots + 1].astype(jnp.int32), bound)
-        list_refs[it][...] = jnp.where(iota(packed.shape, 0) == list_rows - 7, bound, packed)
+    packed = sum(
+        listed[n * list_rows : (n + 1) * list_rows].astype(jnp.int32) * 256**n for n in range(3)
+    )
+    bound = (starts[ranks - 1 : ranks] + sums[ranks - 1 : ranks]).astype(jnp.int32)
+    for g in range(disp_rows):
+        bound = jnp.where(lane == g, starts[g * slots : g * slots + 1].astype(jnp.int32), bound)
+    list_ref[...] = jnp.where(iota(packed.shape, 0) == list_rows - 7, bound, packed)
 
 
 def constants_kernel(to_ref, two_ref, mats_ref, lift_ref, drop_ref):
@@ -294,30 +294,23 @@
     source_refs = refs[:source_count]
     xl_ref, w_hbm = refs[source_count : source_count + 2]
     out_refs = refs[source_count + 2 : source_count + 2 + dest_count]
-    wbuf, pbuf, total, held, sems, held_sems = refs[source_count + 2 + dest_count :]
+    wbuf, pbuf, total, held, sems = refs[source_count + 2 + dest_count :]
     plane = order_k * order_k
     list_rows = packed.shape[0] - 7
     half = term_count // 2
     depth = term_count * order_k
     block_boxes = out_refs[0].shape[0]
     dest_rows = dest_count * block_boxes
-    loads = [
-        pltpu.make_async_copy(ref, held.at[pl.ds(n * block_boxes, block_boxes)], held_sems.at[n])
-        for n, ref in enumerate(source_refs)
-    ]
-    for load in loads:
-        load.start()
-
     def load_row(ll):
         for m in range(term_count):
             column = pl.multiple_of((m * disp_count + ll) * plane, plane)
             pltpu.make_async_copy(w_hbm.at[:, pl.ds(column, plane)], wbuf.at[ll, m], sems.at[ll]).start()
 
-    for ll in range(AHEAD):
+    for ll in range(disp_count):
         load_row(ll)
     total[...] = jnp.zeros_like(total)
-    for load in loads:
-        load.wait()
+    for n, ref in enumerate(source_refs):
+        held[pl.ds(n * block_boxes, block_boxes)] = ref[...]
 
     def push_w(ll, j, reg):
         for unit in range(2):
@@ -391,10 +384,6 @@
             place(g)
 
     def per_disp(ll, carry):
-        @pl.when(ll + AHEAD < disp_count)
-        def _():
-            load_row(ll + AHEAD)
-
         pltpu.make_async_copy(wbuf.at[ll], wbuf.at[ll], sems.at[ll]).wait()
         start, stop = packed[list_rows, ll], packed[list_rows, ll + 1]
 
@@ -439,7 +428,7 @@
     return pl.pallas_call(
         functools.partial(conv_kernel, dims),
         out_shape=[tile] * dest_count,
-        in_specs=[SMEM] + [ANY] * len(sources) + [VMEM, ANY],
+        in_specs=[SMEM] + [VMEM] * (len(sources) + 1) + [ANY],
         out_specs=[VMEM] * dest_count,
         scratch_shapes=[
             pltpu.VMEM((disp_count, term_count, plane, plane), jnp.bfloat16),
@@ -447,7 +436,6 @@
             pltpu.VMEM((dest_count * block_boxes + 1, order_k, plane), jnp.float32),
             pltpu.VMEM((len(sources) * block_boxes, order_k, plane), jnp.bfloat16),
             pltpu.SemaphoreType.DMA((disp_count,)),
-            pltpu.SemaphoreType.DMA((len(sources),)),
         ],
         compiler_params=pltpu.CompilerParams(vmem_limit_bytes=40 * MIB),
         name="convolve",
@@ -524,24 +512,26 @@
     fixed = [pltpu.with_memory_space_constraint(fixed[0], pltpu.VMEM)] + list(fixed[1:])
 
     list_rows = -(-(oct_count * lo_count * box_count * slot_count // LANES + 8) // 8) * 8
-    *lists, moved = pl.pallas_call(
-        functools.partial(route_kernel, (oct_count, hi_count, lo_count, box_count, slot_count, disp_rows)),
-        out_shape=[jax.ShapeDtypeStruct((list_rows, LANES), jnp.int32)] * ITERS
-        + [
-            jax.ShapeDtypeStruct((8, LANES), jnp.int32),
-        ],
+    words, fixed = lax.optimization_barrier((words, fixed))
+    sort_dims = (oct_count, hi_count, lo_count, box_count, slot_count, disp_rows)
+    list_shape = jax.ShapeDtypeStruct((list_rows, LANES), jnp.int32)
+    packed, found = pl.pallas_call(
+        functools.partial(route_kernel, sort_dims, True),
+        out_shape=[list_shape, jax.ShapeDtypeStruct((slot_count + 8, LANES), jnp.int32)],
         in_specs=[SMEM, VMEM],
-        out_specs=[VMEM] * (ITERS + 1),
-        compiler_params=pltpu.CompilerParams(vmem_limit_bytes=11 * MIB),
+        out_specs=[VMEM] * 2,
+        compiler_params=pltpu.CompilerParams(vmem_limit_bytes=16 * MIB),
         name="route_slots",
     )(info, words)
-    came_from = moved[1, :box_count] // box_count % sub_count
+    came_from = found[slot_count + 1, :box_count] // box_count % sub_count
     shifted = shifted_factors(x_kernels)
 
     for iteration in range(ITERS):
         last = iteration == ITERS - 1
         sources = gather_sources(source, lo_count)
-        outs = convolve(sources, shifted, yz_kernels, lists[iteration], hi_count, term_count, order_k)
+        outs = convolve(sources, shifted, yz_kernels, packed, hi_count, term_count, order_k)
+        if not last:
+            outs, send_potential = lax.optimization_barrier((outs, send_potential))
         parts = [outs[0]] + [lax.ppermute(outs[r], "hi", flips(hi_count, r)) for r in range(1, hi_count)]
         kernel = functools.partial(tree_kernel, last, hi_count)
         if last:
@@ -556,8 +546,6 @@
                 name="last_tree",
             )(came_from, *parts, *fixed)
         else:
-            near, send_potential = lax.optimization_barrier((parts[1], send_potential))
-            parts[1] = near
             moved_potential = lax.all_to_all(send_potential, ("hi", "lo"), 0, 0, tiled=True)
             source = pl.pallas_call(
                 kernel,
@@ -566,6 +554,15 @@
                 out_specs=VMEM,
                 name="tree_source",
             )(came_from, *parts, *fixed, moved_potential)
+            source, words = lax.optimization_barrier((source, words))
+            packed = pl.pallas_call(
+                functools.partial(route_kernel, sort_dims, False),
+                out_shape=list_shape,
+                in_specs=[SMEM, VMEM, VMEM],
+                out_specs=VMEM,
+                compiler_params=pltpu.CompilerParams(vmem_limit_bytes=16 * MIB),
+                name="route_again",
+            )(info, words, found)
     returned = lax.all_to_all(fields, ("hi", "lo"), 0, 0, tiled=True)
     next_field = pl.pallas_call(
         unpack_kernel,

time: 147 us -> 139 us (0.946); the launches traced: 147 us -> 137 us
  waiting for transfers between devices: 34.5 us -> 26.9 us
  local copies, waits for them, and re-layouts: 7.89 us -> 10.5 us
  Pallas kernels: 57.5 us -> 55.5 us
  starting transfers between devices: 32.1 us -> 30.5 us
    ppermute x6, starting transfers between devices: 12.4 us -> 8.84 us  [shards(): lax.ppermute(outs[r], 'hi', flips(hi_count, r))]
    all_to_all x1, waiting for transfers between devices: 5.4 us -> 1.86 us  [shards(): words = lax.all_to_all(words, ('oct', 'hi', 'lo'), 0, 0, tiled=True)]
    pallas_call x2, Pallas kernels: 39 us -> 36.2 us  [convolve(): pl.pallas_call(functools.partial(conv_kernel, dims), out_shape=[tile] * d...]
    unnamed x33 -> x35, local copies, waits for them, and re-layouts: 6.55 us -> 9.18 us
    ppermute x6, waiting for transfers between devices: 22.8 us -> 20.3 us  [shards(): lax.ppermute(outs[r], 'hi', flips(hi_count, r))]
    all_to_all x1, starting transfers between devices: 4.16 us -> 6.1 us  [shards(): lax.all_to_all(send_potential, ('hi', 'lo'), 0, 0, tiled=True)]
    pallas_call x1 -> x2, Pallas kernels: 4 us -> 4.87 us  [the longest x1 2.52 us: shards(): pl.pallas_call(functools.partial(route_kernel, sort_dims, True), out_shap...]
  transfers between devices with their start and end apart: 22 -> 22, of which waited for: 10 -> 7; matrix products, arithmetic and copies ran while one was open for 1% -> 2% of each run, Pallas kernels for 3% -> 4%
where the time goes in v4:
time: 139 us; the launch traced here: 137 us
  Pallas kernels  55.5 us (40%)
  starting transfers between devices  30.5 us (22%)
  waiting for transfers between devices  26.9 us (19%)
  blocking collectives  12.6 us (9%)
  local copies, waits for them, and re-layouts  10.5 us (8%)
    pallas_call x2, Pallas kernels, convolve(): pl.pallas_call(functools.partial(conv_kernel, dims), out_shape=[tile] * d...  36.2 us
    ppermute x6, waiting for transfers between devices, shards(): lax.ppermute(outs[r], 'hi', flips(hi_count, r))  20.3 us
    all_to_all x1, blocking collectives, shards(): returned = lax.all_to_all(fields, ('hi', 'lo'), 0, 0, tiled=True)  12.6 us
    unnamed x35, local copies, waits for them, and re-layouts  9.18 us
    ppermute x6, starting transfers between devices, shards(): lax.ppermute(outs[r], 'hi', flips(hi_count, r))  8.84 us
    ppermute x6, starting transfers between devices, gather_sources(): lax.ppermute(source, 'lo', flips(lo_count, r))  7.57 us
    all_to_all x1, starting transfers between devices, shards(): words = lax.all_to_all(words, ('oct', 'hi', 'lo'), 0, 0, tiled=True)  6.26 us
    all_to_all x1, starting transfers between devices, shards(): lax.all_to_all(send_potential, ('hi', 'lo'), 0, 0, tiled=True)  6.1 us
  transfers between devices with their start and end apart: 22, of which 7 were waited for; matrix products, arithmetic and copies ran while one was open for 2% of the time, Pallas kernels for 4%

profile of v4, /device:TPU:0, one launch (start us, length us, event | category | flops | bytes accessed | tf_op | source)
XLA Modules:
  0.0 137.5 jit_solution(15878883011712078697)
XLA Ops:
  0.6 1.6 %pack_tables.1 = s32[32,8,128]{2,1,0:T(8,128)} custom-call(s32[16]{0:T(128)} %parent_of.5, s32[16]{0:T(128)} %octant.1, s32[16,16]{1,0:T(8,128)} %disp_ref.1, s32[16,16]{1,0:T(8,128)} %dest_ref.1), custom_call_target="tpu_custom_call" | custom-call | tf_op jit(solution)/shard_map/pack_tables/pallas_call | solution.py:479
  2.2 3.3 %first_source.1 = (bf16[16,16,256]{2,1,0:T(8,128)(2,1)}, bf16[16,16,256]{2,1,0:T(8,128)(2,1)}) custom-call(s32[16]{0:T(128)} %parent_of.5, f32[16,4096]{1,0:T(8,128)} %coef_ref, f32[16,4096]{1,0:T(8,128)} %pot_ref.1, f32[16,16]{1,0:T(8,128)} %to_ref.2), custom_call_target="tpu_custom_call" | custom-call | tf_op jit(solution)/shard_map/first_source/pallas_call | solution.py:489
  5.5 0.4 collective-permute-start.3
  5.9 3.4 %collective-permute-start.2 = (bf16[16,16,256]{2,1,0:T(8,128)(2,1)}, bf16[16,16,256]{2,1,0:T(8,128)(2,1)}, u32[]{:S(2)}, u32[]{:S(2)}) collective-permute-start(bf16[16,16,256]{2,1,0:T(8,128)(2,1)} %get-tuple-element.44.refs_0_), channel_id=1, source_target_pairs={{0,3},{1,2},{2,1},{3,0},{4,7},{5,6},{6,5},{7,4},{8,11},{9,10},{10,... | collective-permute-start | bytes 393224 | tf_op jit(solution)/shard_map/ppermute | solution.py:450
  9.4 0.5 collective-permute-start.1
  10.0 6.3 %all-to-all-start = ((s32[32,8,128]{2,1,0:T(8,128)}), s32[32,8,128]{2,1,0:T(8,128)S(1)}, u32[]{:S(2)}, u32[]{:S(2)}) async-start(s32[32,8,128]{2,1,0:T(8,128)} %pack_tables.1), calls=%async_computation | async-start | bytes 262144 | tf_op jit(solution)/shard_map/all_to_all | solution.py:487
  16.3 1.1 copy.27
  17.8 0.3 collective-permute-start.6
  18.1 0.3 collective-permute-start.5
  18.7 0.7 copy-done.6
  19.4 0.7 copy-done.7
  20.1 0.9 make_constants.1
  21.1 0.6 copy-done.2
  21.6 0.6 copy-done.5
  22.3 1.9 %all-to-all-done.words_ref = s32[32,8,128]{2,1,0:T(8,128)S(1)} async-done(((s32[32,8,128]{2,1,0:T(8,128)}), s32[32,8,128]{2,1,0:T(8,128)S(1)}, u32[]{:S(2)}, u32[]{:S(2)}) %all-to-all-start) | async-done | bytes 131104 | tf_op jit(solution)/shard_map/all_to_all | solution.py:487
  24.2 2.5 %route_slots.1 = (s32[24,128]{1,0:T(8,128)S(1)}, s32[24,128]{1,0:T(8,128)S(1)}) custom-call(s32[3]{0:T(128)S(1)} %pad_add_fusion.info, s32[32,8,128]{2,1,0:T(8,128)S(1)} %all-to-all-done.words_ref), custom_call_target="tpu_custom_call" | custom-call | tf_op jit(solution)/shard_map/route_slots/pallas_call | solution.py:518
  26.8 0.9 copy-done.1
  27.7 17.3 %convolve.2 = (bf16[16,16,256]{2,1,0:T(8,128)(2,1)S(1)}, bf16[16,16,256]{2,1,0:T(8,128)(2,1)S(1)}, bf16[16,16,256]{2,1,0:T(8,128)(2,1)S(1)}, bf16[16,16,256]{2,1,0:T(8,128)(2,1)S(1)}) custom-call(s32[24,128]{1,0:T(8,128)S(1)} %get-tuple-element.43.packed, bf16[16,16,256]{2,1,0:T(8,128)(2,1)S(1)} %copy-done.1, ...), custom_call_target="tpu_custom_call" | custom-call | tf_op jit(solution)/shard_map/convolve/pallas_call | solution.py:428
  45.0 0.6 copy-done.3
  45.7 0.6 copy-done.8
  46.3 0.6 copy-done.9
  47.0 0.6 copy-done.10
  47.6 6.1 %all-to-all-start.1 = ((bf16[16,16,256]{2,1,0:T(8,128)(2,1)}), bf16[16,16,256]{2,1,0:T(8,128)(2,1)}, u32[]{:S(2)}, u32[]{:S(2)}) async-start(bf16[16,16,256]{2,1,0:T(8,128)(2,1)} %get-tuple-element.57), calls=%async_computation.1 | async-start | bytes 262144 | tf_op jit(solution)/shard_map/all_to_all | solution.py:549
  53.7 1.9 %collective-permute-start.7 = (bf16[16,16,256]{2,1,0:T(8,128)(2,1)}, bf16[16,16,256]{2,1,0:T(8,128)(2,1)}, u32[]{:S(2)}, u32[]{:S(2)}) collective-permute-start(bf16[16,16,256]{2,1,0:T(8,128)(2,1)} %copy-done.10), channel_id=1, source_target_pairs={{0,4},{4,0},{8,12},{12,8},{1,5},{5,1},{9,13},{13,9},{2,6},{6,2},{1... | collective-permute-start | bytes 393224 | tf_op jit(solution)/shard_map/ppermute | solution.py:535
  55.6 2.4 %collective-permute-start.8 = (bf16[16,16,256]{2,1,0:T(8,128)(2,1)}, bf16[16,16,256]{2,1,0:T(8,128)(2,1)}, u32[]{:S(2)}, u32[]{:S(2)}) collective-permute-start(bf16[16,16,256]{2,1,0:T(8,128)(2,1)} %copy-done.9), channel_id=1, source_target_pairs={{0,8},{4,12},{8,0},{12,4},{1,9},{5,13},{9,1},{13,5},{2,10},{6,14},... | collective-permute-start | bytes 393224 | tf_op jit(solution)/shard_map/ppermute | solution.py:535
  58.2 0.6 and_select_fusion.came_from
  58.7 4.9 %collective-permute-done.7.refs_1_ = bf16[16,16,256]{2,1,0:T(8,128)(2,1)} collective-permute-done((bf16[16,16,256]{2,1,0:T(8,128)(2,1)}, bf16[16,16,256]{2,1,0:T(8,128)(2,1)}, u32[]{:S(2)}, u32[]{:S(2)}) %collective-permute-start.7) | collective-permute-done | bytes 131104 | tf_op jit(solution)/shard_map/ppermute | solution.py:535
  63.6 5.5 %collective-permute-done.8.refs_2_ = bf16[16,16,256]{2,1,0:T(8,128)(2,1)} collective-permute-done((bf16[16,16,256]{2,1,0:T(8,128)(2,1)}, bf16[16,16,256]{2,1,0:T(8,128)(2,1)}, u32[]{:S(2)}, u32[]{:S(2)}) %collective-permute-start.8) | collective-permute-done | bytes 131104 | tf_op jit(solution)/shard_map/ppermute | solution.py:535
  69.2 4.1 %tree_source.1.refs_0_ = bf16[16,16,256]{2,1,0:T(8,128)(2,1)} custom-call(s32[16]{0:T(128)} %and_select_fusion.came_from, bf16[16,16,256]{2,1,0:T(8,128)(2,1)} %copy-done.3, bf16[16,16,256]{2,1,0:T(8,128)(2,1)} %collective-permute-done.7.refs_1_, bf16[16,16,256]{2,1,0:T(8,128)(2,1)} %collective-permute-done.8.refs_2_, ...), custom_call_target="tpu_custom_call" | custom-call | tf_op jit(solution)/shard_map/tree_source/pallas_call | solution.py:550
  73.3 2.4 %collective-permute-start.12 = (bf16[16,16,256]{2,1,0:T(8,128)(2,1)}, bf16[16,16,256]{2,1,0:T(8,128)(2,1)S(1)}, u32[]{:S(2)}, u32[]{:S(2)}) collective-permute-start(bf16[16,16,256]{2,1,0:T(8,128)(2,1)} %tree_source.1.refs_0_), channel_id=1, source_target_pairs={{0,3},{1,2},{2,1},{3,0},{4,7},{5,6},{6,5},{7,4},{8,11},{9,10},{10,... | collective-permute-start | bytes 393224 | tf_op jit(solution)/shard_map/ppermute | solution.py:450
  75.6 0.6 collective-permute-start.11
  76.2 0.6 collective-permute-start.10
  76.8 4.0 %collective-permute-done.12.refs_3_ = bf16[16,16,256]{2,1,0:T(8,128)(2,1)S(1)} collective-permute-done((bf16[16,16,256]{2,1,0:T(8,128)(2,1)}, bf16[16,16,256]{2,1,0:T(8,128)(2,1)S(1)}, u32[]{:S(2)}, u32[]{:S(2)}) %collective-permute-start.12) | collective-permute-done | bytes 131104 | tf_op jit(solution)/shard_map/ppermute | solution.py:450
  80.7 0.8 collective-permute-done.11.refs_2_
  81.5 0.5 collective-permute-start.14
  82.0 2.3 %route_again.1.packed = s32[24,128]{1,0:T(8,128)S(1)} custom-call(s32[3]{0:T(128)S(1)} %pad_add_fusion.info, s32[32,8,128]{2,1,0:T(8,128)S(1)} %all-to-all-done.words_ref, s32[24,128]{1,0:T(8,128)S(1)} %get-tuple-element.42.refs_0_), custom_call_target="tpu_custom_call" | custom-call | tf_op jit(solution)/shard_map/route_again/pallas_call | solution.py:558
  84.4 0.9 copy-done
  85.3 18.8 %convolve.3 = (bf16[16,16,256]{2,1,0:T(8,128)(2,1)S(1)}, bf16[16,16,256]{2,1,0:T(8,128)(2,1)S(1)}, bf16[16,16,256]{2,1,0:T(8,128)(2,1)S(1)}, bf16[16,16,256]{2,1,0:T(8,128)(2,1)S(1)}) custom-call(s32[24,128]{1,0:T(8,128)S(1)} %route_again.1.packed, bf16[16,16,256]{2,1,0:T(8,128)(2,1)S(1)} %copy-done, ...), custom_call_target="tpu_custom_call" | custom-call | tf_op jit(solution)/shard_map/convolve/pallas_call | solution.py:428
  104.2 0.6 copy-done.4
  104.8 1.5 %collective-permute-start.17 = (bf16[16,16,256]{2,1,0:T(8,128)(2,1)S(1)}, bf16[16,16,256]{2,1,0:T(8,128)(2,1)S(1)}, u32[]{:S(2)}, u32[]{:S(2)}) collective-permute-start(bf16[16,16,256]{2,1,0:T(8,128)(2,1)S(1)} %get-tuple-element.61), channel_id=1, source_target_pairs={{0,4},{4,0},{8,12},{12,8},{1,5},{5,1},{9,13},{13,9},{2,6},{6,2},{1... | collective-permute-start | bytes 393224 | tf_op jit(solution)/shard_map/ppermute | solution.py:535
  106.3 2.9 %collective-permute-start.19 = (bf16[16,16,256]{2,1,0:T(8,128)(2,1)S(1)}, bf16[16,16,256]{2,1,0:T(8,128)(2,1)S(1)}, u32[]{:S(2)}, u32[]{:S(2)}) collective-permute-start(bf16[16,16,256]{2,1,0:T(8,128)(2,1)S(1)} %get-tuple-element.63), channel_id=1, source_target_pairs={{0,12},{4,8},{8,4},{12,0},{1,13},{5,9},{9,5},{13,1},{2,14},{6,10},... | collective-permute-start | bytes 393224 | tf_op jit(solution)/shard_map/ppermute | solution.py:535
  109.2 2.2 %collective-permute-done.17.refs_1_ = bf16[16,16,256]{2,1,0:T(8,128)(2,1)S(1)} collective-permute-done((bf16[16,16,256]{2,1,0:T(8,128)(2,1)S(1)}, bf16[16,16,256]{2,1,0:T(8,128)(2,1)S(1)}, u32[]{:S(2)}, u32[]{:S(2)}) %collective-permute-start.17) | collective-permute-done | bytes 131104 | tf_op jit(solution)/shard_map/ppermute | solution.py:535
  111.4 7.7 %collective-permute-done.18.refs_2_ = bf16[16,16,256]{2,1,0:T(8,128)(2,1)S(1)} collective-permute-done((bf16[16,16,256]{2,1,0:T(8,128)(2,1)S(1)}, bf16[16,16,256]{2,1,0:T(8,128)(2,1)S(1)}, u32[]{:S(2)}, u32[]{:S(2)}) %collective-permute-start.18) | collective-permute-done | bytes 131104 | tf_op jit(solution)/shard_map/ppermute | solution.py:535
  119.1 0.6 copy-done.12
  119.7 0.6 copy-done.13
  120.4 2.8 %last_tree.1 = (bf16[16,16,256]{2,1,0:T(8,128)(2,1)}, f32[2,4096]{1,0:T(2,128)}) custom-call(s32[16]{0:T(128)} %and_select_fusion.came_from, bf16[16,16,256]{2,1,0:T(8,128)(2,1)} %copy-done.4, bf16[16,16,256]{2,1,0:T(8,128)(2,1)} %copy-done.11, bf16[16,16,256]{2,1,0:T(8,128)(2,1)} %copy-done.12, bf16[16,16,256]{2,1,0:T(8,128)(2,1)} %copy-done.13, ...), custom_call_target="tpu_custom_call" | custom-call | tf_op jit(solution)/shard_map/last_tree/pallas_call | solution.py:538
  123.1 12.6 %all_to_all.15.field_ref = bf16[16,16,256]{2,1,0:T(8,128)(2,1)} all-to-all(bf16[16,16,256]{2,1,0:T(8,128)(2,1)} %get-tuple-element.64), channel_id=1, replica_groups=mesh['oct'=2,'hi'=4,'lo'=4] {'hi','lo'}, dimensions={0} | all-to-all | bytes 262144 | tf_op jit(solution)/shard_map/all_to_all | solution.py:566
  135.7 1.8 %unpack_fields.1 = f32[16,4096]{1,0:T(8,128)} custom-call(s32[16]{0:T(128)} %parent_of.5, bf16[16,16,256]{2,1,0:T(8,128)(2,1)} %all_to_all.15.field_ref), custom_call_target="tpu_custom_call" | custom-call | tf_op jit(solution)/shard_map/unpack_fields/pallas_call | solution.py:567
  (47 shorter events, 1.3 us)
Async XLA Ops:
  5.5 21.2 %collective-permute-start.3 = (bf16[16,16,256]{2,1,0:T(8,128)(2,1)}, bf16[16,16,256]{2,1,0:T(8,128)(2,1)}, u32[]{:S(2)}, u32[]{:S(2)}) collective-permute-start(bf16[16,16,256]{2,1,0:T(8,128)(2,1)} %get-tuple-element.44.refs_0_), channel_id=1, source_target_pairs={{0,16},{16,0},{1,17},{17,1},{2,18},{18,2},{3,19},{19,3},{4,20},{20... | collective-permute-start | bytes 393224 | tf_op jit(solution)/shard_map/ppermute | solution.py:451
  5.9 11.9 %collective-permute-start.2 = (bf16[16,16,256]{2,1,0:T(8,128)(2,1)}, bf16[16,16,256]{2,1,0:T(8,128)(2,1)}, u32[]{:S(2)}, u32[]{:S(2)}) collective-permute-start(bf16[16,16,256]{2,1,0:T(8,128)(2,1)} %get-tuple-element.44.refs_0_), channel_id=1, source_target_pairs={{0,3},{1,2},{2,1},{3,0},{4,7},{5,6},{6,5},{7,4},{8,11},{9,10},{10,... | collective-permute-start | bytes 393224 | tf_op jit(solution)/shard_map/ppermute | solution.py:450
  9.4 8.7 %collective-permute-start.1 = (bf16[16,16,256]{2,1,0:T(8,128)(2,1)}, bf16[16,16,256]{2,1,0:T(8,128)(2,1)}, u32[]{:S(2)}, u32[]{:S(2)}) collective-permute-start(bf16[16,16,256]{2,1,0:T(8,128)(2,1)} %get-tuple-element.44.refs_0_), channel_id=1, source_target_pairs={{0,2},{1,3},{2,0},{3,1},{4,6},{5,7},{6,4},{7,5},{8,10},{9,11},{10,... | collective-permute-start | bytes 393224 | tf_op jit(solution)/shard_map/ppermute | solution.py:450
  9.9 8.5 %collective-permute-start = (bf16[16,16,256]{2,1,0:T(8,128)(2,1)}, bf16[16,16,256]{2,1,0:T(8,128)(2,1)}, u32[]{:S(2)}, u32[]{:S(2)}) collective-permute-start(bf16[16,16,256]{2,1,0:T(8,128)(2,1)} %get-tuple-element.44.refs_0_), channel_id=1, source_target_pairs={{0,1},{1,0},{2,3},{3,2},{4,5},{5,4},{6,7},{7,6},{8,9},{9,8},{10,11... | collective-permute-start | bytes 393224 | tf_op jit(solution)/shard_map/ppermute | solution.py:450
  10.0 14.2 %all-to-all-start = ((s32[32,8,128]{2,1,0:T(8,128)}), s32[32,8,128]{2,1,0:T(8,128)S(1)}, u32[]{:S(2)}, u32[]{:S(2)}) async-start(s32[32,8,128]{2,1,0:T(8,128)} %pack_tables.1), calls=%async_computation | async-start | bytes 262144 | tf_op jit(solution)/shard_map/all_to_all | solution.py:487
  17.8 8.9 %collective-permute-start.6 = (bf16[16,16,256]{2,1,0:T(8,128)(2,1)}, bf16[16,16,256]{2,1,0:T(8,128)(2,1)}, u32[]{:S(2)}, u32[]{:S(2)}) collective-permute-start(bf16[16,16,256]{2,1,0:T(8,128)(2,1)} %collective-permute-done.2.refs_3_), channel_id=1, source_target_pairs={{0,16},{16,0},{1,17},{17,1},{2,18},{18,2},{3,19},{19,3},{4,20},{20... | collective-permute-start | bytes 393224 | tf_op jit(solution)/shard_map/ppermute | solution.py:451
  18.1 8.6 %collective-permute-start.5 = (bf16[16,16,256]{2,1,0:T(8,128)(2,1)}, bf16[16,16,256]{2,1,0:T(8,128)(2,1)}, u32[]{:S(2)}, u32[]{:S(2)}) collective-permute-start(bf16[16,16,256]{2,1,0:T(8,128)(2,1)} %collective-permute-done.1.refs_2_), channel_id=1, source_target_pairs={{0,16},{16,0},{1,17},{17,1},{2,18},{18,2},{3,19},{19,3},{4,20},{20... | collective-permute-start | bytes 393224 | tf_op jit(solution)/shard_map/ppermute | solution.py:451
  18.4 8.4 %collective-permute-start.4 = (bf16[16,16,256]{2,1,0:T(8,128)(2,1)}, bf16[16,16,256]{2,1,0:T(8,128)(2,1)}, u32[]{:S(2)}, u32[]{:S(2)}) collective-permute-start(bf16[16,16,256]{2,1,0:T(8,128)(2,1)} %collective-permute-done.refs_1_), channel_id=1, source_target_pairs={{0,16},{16,0},{1,17},{17,1},{2,18},{18,2},{3,19},{19,3},{4,20},{20... | collective-permute-start | bytes 393224 | tf_op jit(solution)/shard_map/ppermute | solution.py:451
  18.7 0.7 copy-start.6
  19.4 0.7 copy-start.7
  21.0 0.6 copy-start.2
  21.6 0.6 copy-start.5
  26.8 0.9 copy-start.1
  45.0 0.7 copy-start.3
  45.7 0.6 copy-start.8
  46.3 0.6 copy-start.9
  47.0 0.6 copy-start.10
  47.6 21.6 %all-to-all-start.1 = ((bf16[16,16,256]{2,1,0:T(8,128)(2,1)}), bf16[16,16,256]{2,1,0:T(8,128)(2,1)}, u32[]{:S(2)}, u32[]{:S(2)}) async-start(bf16[16,16,256]{2,1,0:T(8,128)(2,1)} %get-tuple-element.57), calls=%async_computation.1 | async-start | bytes 262144 | tf_op jit(solution)/shard_map/all_to_all | solution.py:549
  53.7 9.9 %collective-permute-start.7 = (bf16[16,16,256]{2,1,0:T(8,128)(2,1)}, bf16[16,16,256]{2,1,0:T(8,128)(2,1)}, u32[]{:S(2)}, u32[]{:S(2)}) collective-permute-start(bf16[16,16,256]{2,1,0:T(8,128)(2,1)} %copy-done.10), channel_id=1, source_target_pairs={{0,4},{4,0},{8,12},{12,8},{1,5},{5,1},{9,13},{13,9},{2,6},{6,2},{1... | collective-permute-start | bytes 393224 | tf_op jit(solution)/shard_map/ppermute | solution.py:535
  55.6 13.6 %collective-permute-start.8 = (bf16[16,16,256]{2,1,0:T(8,128)(2,1)}, bf16[16,16,256]{2,1,0:T(8,128)(2,1)}, u32[]{:S(2)}, u32[]{:S(2)}) collective-permute-start(bf16[16,16,256]{2,1,0:T(8,128)(2,1)} %copy-done.9), channel_id=1, source_target_pairs={{0,8},{4,12},{8,0},{12,4},{1,9},{5,13},{9,1},{13,5},{2,10},{6,14},... | collective-permute-start | bytes 393224 | tf_op jit(solution)/shard_map/ppermute | solution.py:535
  57.9 11.2 %collective-permute-start.9 = (bf16[16,16,256]{2,1,0:T(8,128)(2,1)}, bf16[16,16,256]{2,1,0:T(8,128)(2,1)}, u32[]{:S(2)}, u32[]{:S(2)}) collective-permute-start(bf16[16,16,256]{2,1,0:T(8,128)(2,1)} %copy-done.8), channel_id=1, source_target_pairs={{0,12},{4,8},{8,4},{12,0},{1,13},{5,9},{9,5},{13,1},{2,14},{6,10},... | collective-permute-start | bytes 393224 | tf_op jit(solution)/shard_map/ppermute | solution.py:535
  73.3 7.5 %collective-permute-start.12 = (bf16[16,16,256]{2,1,0:T(8,128)(2,1)}, bf16[16,16,256]{2,1,0:T(8,128)(2,1)S(1)}, u32[]{:S(2)}, u32[]{:S(2)}) collective-permute-start(bf16[16,16,256]{2,1,0:T(8,128)(2,1)} %tree_source.1.refs_0_), channel_id=1, source_target_pairs={{0,3},{1,2},{2,1},{3,0},{4,7},{5,6},{6,5},{7,4},{8,11},{9,10},{10,... | collective-permute-start | bytes 393224 | tf_op jit(solution)/shard_map/ppermute | solution.py:450
  75.6 5.8 %collective-permute-start.11 = (bf16[16,16,256]{2,1,0:T(8,128)(2,1)}, bf16[16,16,256]{2,1,0:T(8,128)(2,1)S(1)}, u32[]{:S(2)}, u32[]{:S(2)}) collective-permute-start(bf16[16,16,256]{2,1,0:T(8,128)(2,1)} %tree_source.1.refs_0_), channel_id=1, source_target_pairs={{0,2},{1,3},{2,0},{3,1},{4,6},{5,7},{6,4},{7,5},{8,10},{9,11},{10,... | collective-permute-start | bytes 393224 | tf_op jit(solution)/shard_map/ppermute | solution.py:450
  76.2 5.3 %collective-permute-start.10 = (bf16[16,16,256]{2,1,0:T(8,128)(2,1)}, bf16[16,16,256]{2,1,0:T(8,128)(2,1)S(1)}, u32[]{:S(2)}, u32[]{:S(2)}) collective-permute-start(bf16[16,16,256]{2,1,0:T(8,128)(2,1)} %tree_source.1.refs_0_), channel_id=1, source_target_pairs={{0,1},{1,0},{2,3},{3,2},{4,5},{5,4},{6,7},{7,6},{8,9},{9,8},{10,11... | collective-permute-start | bytes 393224 | tf_op jit(solution)/shard_map/ppermute | solution.py:450
  76.8 7.6 %collective-permute-start.13 = (bf16[16,16,256]{2,1,0:T(8,128)(2,1)}, bf16[16,16,256]{2,1,0:T(8,128)(2,1)S(1)}, u32[]{:S(2)}, u32[]{:S(2)}) collective-permute-start(bf16[16,16,256]{2,1,0:T(8,128)(2,1)} %tree_source.1.refs_0_), channel_id=1, source_target_pairs={{0,16},{16,0},{1,17},{17,1},{2,18},{18,2},{3,19},{19,3},{4,20},{20... | collective-permute-start | bytes 393224 | tf_op jit(solution)/shard_map/ppermute | solution.py:451
  80.7 3.6 %collective-permute-start.16 = (bf16[16,16,256]{2,1,0:T(8,128)(2,1)S(1)}, bf16[16,16,256]{2,1,0:T(8,128)(2,1)S(1)}, u32[]{:S(2)}, u32[]{:S(2)}) collective-permute-start(bf16[16,16,256]{2,1,0:T(8,128)(2,1)S(1)} %collective-permute-done.12.refs_3_), channel_id=1, source_target_pairs={{0,16},{16,0},{1,17},{17,1},{2,18},{18,2},{3,19},{19,3},{4,20},{20... | collective-permute-start | bytes 393224 | tf_op jit(solution)/shard_map/ppermute | solution.py:451
  81.5 2.9 %collective-permute-start.15 = (bf16[16,16,256]{2,1,0:T(8,128)(2,1)S(1)}, bf16[16,16,256]{2,1,0:T(8,128)(2,1)S(1)}, u32[]{:S(2)}, u32[]{:S(2)}) collective-permute-start(bf16[16,16,256]{2,1,0:T(8,128)(2,1)S(1)} %collective-permute-done.11.refs_2_), channel_id=1, source_target_pairs={{0,16},{16,0},{1,17},{17,1},{2,18},{18,2},{3,19},{19,3},{4,20},{20... | collective-permute-start | bytes 393224 | tf_op jit(solution)/shard_map/ppermute | solution.py:451
  81.5 2.9 %collective-permute-start.14 = (bf16[16,16,256]{2,1,0:T(8,128)(2,1)S(1)}, bf16[16,16,256]{2,1,0:T(8,128)(2,1)S(1)}, u32[]{:S(2)}, u32[]{:S(2)}) collective-permute-start(bf16[16,16,256]{2,1,0:T(8,128)(2,1)S(1)} %collective-permute-done.10.refs_1_), channel_id=1, source_target_pairs={{0,16},{16,0},{1,17},{17,1},{2,18},{18,2},{3,19},{19,3},{4,20},{20... | collective-permute-start | bytes 393224 | tf_op jit(solution)/shard_map/ppermute | solution.py:451
  84.4 0.9 copy-start
  104.1 0.7 copy-start.4
  104.8 6.6 %collective-permute-start.17 = (bf16[16,16,256]{2,1,0:T(8,128)(2,1)S(1)}, bf16[16,16,256]{2,1,0:T(8,128)(2,1)S(1)}, u32[]{:S(2)}, u32[]{:S(2)}) collective-permute-start(bf16[16,16,256]{2,1,0:T(8,128)(2,1)S(1)} %get-tuple-element.61), channel_id=1, source_target_pairs={{0,4},{4,0},{8,12},{12,8},{1,5},{5,1},{9,13},{13,9},{2,6},{6,2},{1... | collective-permute-start | bytes 393224 | tf_op jit(solution)/shard_map/ppermute | solution.py:535
  106.3 12.7 %collective-permute-start.18 = (bf16[16,16,256]{2,1,0:T(8,128)(2,1)S(1)}, bf16[16,16,256]{2,1,0:T(8,128)(2,1)S(1)}, u32[]{:S(2)}, u32[]{:S(2)}) collective-permute-start(bf16[16,16,256]{2,1,0:T(8,128)(2,1)S(1)} %get-tuple-element.62), channel_id=1, source_target_pairs={{0,8},{4,12},{8,0},{12,4},{1,9},{5,13},{9,1},{13,5},{2,10},{6,14},... | collective-permute-start | bytes 393224 | tf_op jit(solution)/shard_map/ppermute | solution.py:535
  106.3 12.7 %collective-permute-start.19 = (bf16[16,16,256]{2,1,0:T(8,128)(2,1)S(1)}, bf16[16,16,256]{2,1,0:T(8,128)(2,1)S(1)}, u32[]{:S(2)}, u32[]{:S(2)}) collective-permute-start(bf16[16,16,256]{2,1,0:T(8,128)(2,1)S(1)} %get-tuple-element.63), channel_id=1, source_target_pairs={{0,12},{4,8},{8,4},{12,0},{1,13},{5,9},{9,5},{13,1},{2,14},{6,10},... | collective-permute-start | bytes 393224 | tf_op jit(solution)/shard_map/ppermute | solution.py:535
  111.4 9.0 %copy-start.11 = (bf16[16,16,256]{2,1,0:T(8,128)(2,1)}, bf16[16,16,256]{2,1,0:T(8,128)(2,1)S(1)}, u32[]{:S(2)}) copy-start(bf16[16,16,256]{2,1,0:T(8,128)(2,1)S(1)} %collective-permute-done.17.refs_1_) | copy-start | bytes 393220
  119.1 0.7 copy-start.12
  119.7 0.6 copy-start.13

commit v5 on v4

--- a/solution.py
+++ b/solution.py
@@ -10,6 +10,7 @@
 
 ITERS = 2
 BLOCK = 32
+TOTALS = 1
 GROUP = 4
 LANES = 128
 MIB = 1024 * 1024
@@ -51,15 +52,16 @@
     return jnp.broadcast_to(matrix[None, :, :], (order_k, order_k, width)).reshape(order_k * order_k, width)
 
 
-def spread_columns(matrix, flip=False):
+def spread_columns(matrix):
     order_k = matrix.shape[0]
-    shape = (order_k, order_k * order_k)
-    slot, lane = iota(shape, 0), iota(shape, 1)
-    high = (lane // order_k == slot).astype(jnp.float32)
-    low = (lane % order_k == slot).astype(jnp.float32)
-    if flip:
-        matrix = matrix.T
-    return mm(matrix, high), mm(matrix, low)
+    plane = order_k * order_k
+    slot, lane = iota((order_k, 2 * plane), 0), iota((order_k, 2 * plane), 1)
+    chosen = jnp.where(lane < plane, lane // order_k, lane % order_k) == slot
+    rows = jnp.concatenate(halves(matrix) + halves(matrix.T), axis=0)
+    wide = dot16(rows, chosen.astype(jnp.float32).astype(jnp.bfloat16))
+    plain = wide[:order_k] + wide[order_k : 2 * order_k]
+    turned = wide[2 * order_k : 3 * order_k] + wide[3 * order_k :]
+    return plain[:, :plane], plain[:, plane:], turned[:, :plane], turned[:, plane:]
 
 
 def masks(order_k):
@@ -92,8 +94,7 @@
 def first_kernel(parent_of, coef_ref, pot_ref, to_ref, out_ref, pot_out, rows_ref):
     order_k = to_ref.shape[0]
     plane = order_k * order_k
-    to_high, to_low = spread_columns(to_ref[...])
-    back_high, back_low = spread_columns(to_ref[...], True)
+    to_high, to_low, back_high, back_low = spread_columns(to_ref[...])
     row_high, row_low, lane_high, lane_low = masks(order_k)
     value_pair = halves(rows_high(back_high) * rows_low(back_low))
     back_pair = halves(rows_high(to_high) * rows_low(to_low))
@@ -201,10 +202,9 @@
 
 def constants_kernel(to_ref, two_ref, mats_ref, lift_ref, drop_ref):
     order_k = to_ref.shape[0]
-    to_high, to_low = spread_columns(to_ref[...])
-    back_high, back_low = spread_columns(to_ref[...], True)
-    two = [spread_columns(two_ref[c]) for c in range(2)]
-    flip = [spread_columns(two_ref[c], True) for c in range(2)]
+    to_high, to_low, back_high, back_low = spread_columns(to_ref[...])
+    spread = [spread_columns(two_ref[c]) for c in range(2)]
+    two, flip = [four[:2] for four in spread], [four[2:] for four in spread]
     row_high, row_low, lane_high, lane_low = masks(order_k)
     made = []
     for quad in range(4):
@@ -294,7 +294,7 @@
     source_refs = refs[:source_count]
     xl_ref, w_hbm = refs[source_count : source_count + 2]
     out_refs = refs[source_count + 2 : source_count + 2 + dest_count]
-    wbuf, pbuf, total, held, sems = refs[source_count + 2 + dest_count :]
+    wbuf, pbuf, *totals, held, sems = refs[source_count + 2 + dest_count :]
     plane = order_k * order_k
     list_rows = packed.shape[0] - 7
     half = term_count // 2
@@ -308,7 +308,8 @@
 
     for ll in range(disp_count):
         load_row(ll)
-    total[...] = jnp.zeros_like(total)
+    for total in totals:
+        total[...] = jnp.zeros_like(total)
     for n, ref in enumerate(source_refs):
         held[pl.ds(n * block_boxes, block_boxes)] = ref[...]
 
@@ -362,6 +363,7 @@
             for s in range(GROUP):
                 t = g * GROUP + s
                 tile = pltpu.matmul_pop(accs[g % 2][0][t])
+                total = totals[t % TOTALS]
                 dest = jnp.where(t < live, codes[t] % dest_rows, dest_rows)
                 total[dest] = total[dest] + tile
 
@@ -401,7 +403,8 @@
 
     lax.fori_loop(0, disp_count, per_disp, 0)
     for r, out_ref in enumerate(out_refs):
-        out_ref[...] = total[pl.ds(r * block_boxes, block_boxes)].astype(jnp.bfloat16)
+        part = pl.ds(r * block_boxes, block_boxes)
+        out_ref[...] = sum(total[part] for total in totals).astype(jnp.bfloat16)
 
 
 def shifted_factors(x_kernels):
@@ -433,11 +436,11 @@
         scratch_shapes=[
             pltpu.VMEM((disp_count, term_count, plane, plane), jnp.bfloat16),
             pltpu.VMEM((BLOCK * term_count * order_k, plane), jnp.bfloat16),
-            pltpu.VMEM((dest_count * block_boxes + 1, order_k, plane), jnp.float32),
+            *[pltpu.VMEM((dest_count * block_boxes + 1, order_k, plane), jnp.float32)] * TOTALS,
             pltpu.VMEM((len(sources) * block_boxes, order_k, plane), jnp.bfloat16),
             pltpu.SemaphoreType.DMA((disp_count,)),
         ],
-        compiler_params=pltpu.CompilerParams(vmem_limit_bytes=40 * MIB),
+        compiler_params=pltpu.CompilerParams(vmem_limit_bytes=48 * MIB),
         name="convolve",
     )(packed, *sources, shifted, yz_kernels)
 
@@ -531,7 +534,8 @@
         sources = gather_sources(source, lo_count)
         outs = convolve(sources, shifted, yz_kernels, packed, hi_count, term_count, order_k)
         if not last:
-            outs, send_potential = lax.optimization_barrier((outs, send_potential))
+            own_part, send_potential = lax.optimization_barrier((outs[0], send_potential))
+            outs = [own_part] + list(outs[1:])
         parts = [outs[0]] + [lax.ppermute(outs[r], "hi", flips(hi_count, r)) for r in range(1, hi_count)]
         kernel = functools.partial(tree_kernel, last, hi_count)
         if last:

time: 139 us -> 139 us (level); the launches traced: 137 us -> 139 us
  waiting for transfers between devices: 26.9 us -> 22.5 us
  starting transfers between devices: 30.5 us -> 34.5 us
  blocking collectives: 12.6 us -> 15.9 us
    ppermute x8, starting transfers between devices: 1.74 us -> 6.46 us  [gather_sources(): return near + [lax.ppermute(block, 'oct', flips(2, 1)) for block in near]]
    all_to_all x1, blocking collectives: 12.6 us -> 15.9 us  [shards(): returned = lax.all_to_all(fields, ('hi', 'lo'), 0, 0, tiled=True)]
    ppermute x6, waiting for transfers between devices: 4.73 us -> 1.92 us  [gather_sources(): lax.ppermute(source, 'lo', flips(lo_count, r))]
    ppermute x6, waiting for transfers between devices: 20.3 us -> 18.6 us  [shards(): lax.ppermute(outs[r], 'hi', flips(hi_count, r))]
  transfers between devices with their start and end apart: 22 -> 22, of which waited for: 7 -> 9; matrix products, arithmetic and copies ran while one was open for 2% -> 2% of each run, Pallas kernels for 4% -> 4%
where the time goes in v5:
time: 139 us
  Pallas kernels  55.1 us (40%)
  starting transfers between devices  34.5 us (25%)
  waiting for transfers between devices  22.5 us (16%)
  blocking collectives  15.9 us (11%)
  local copies, waits for them, and re-layouts  9.88 us (7%)
    pallas_call x2, Pallas kernels, convolve(): pl.pallas_call(functools.partial(conv_kernel, dims), out_shape=[tile] * d...  35.9 us
    ppermute x6, waiting for transfers between devices, shards(): lax.ppermute(outs[r], 'hi', flips(hi_count, r))  18.6 us
    all_to_all x1, blocking collectives, shards(): returned = lax.all_to_all(fields, ('hi', 'lo'), 0, 0, tiled=True)  15.9 us
    ppermute x6, starting transfers between devices, shards(): lax.ppermute(outs[r], 'hi', flips(hi_count, r))  8.84 us
    unnamed x35, local copies, waits for them, and re-layouts  8.54 us
    ppermute x6, starting transfers between devices, gather_sources(): lax.ppermute(source, 'lo', flips(lo_count, r))  7.57 us
    ppermute x8, starting transfers between devices, gather_sources(): return near + [lax.ppermute(block, 'oct', flips(2, 1)) for block in near]  6.46 us
    all_to_all x1, starting transfers between devices, shards(): words = lax.all_to_all(words, ('oct', 'hi', 'lo'), 0, 0, tiled=True)  6.26 us
  transfers between devices with their start and end apart: 22, of which 9 were waited for; matrix products, arithmetic and copies ran while one was open for 2% of the time, Pallas kernels for 4%

profile of v5, /device:TPU:0, one launch (start us, length us, event | category | flops | bytes accessed | tf_op | source)
XLA Modules:
  0.0 139.3 jit_solution(9257675662498781312)
XLA Ops:
  0.6 1.6 %pack_tables.1 = s32[32,8,128]{2,1,0:T(8,128)} custom-call(s32[16]{0:T(128)} %parent_of.5, s32[16]{0:T(128)} %octant.1, s32[16,16]{1,0:T(8,128)} %disp_ref.1, s32[16,16]{1,0:T(8,128)} %dest_ref.1), custom_call_target="tpu_custom_call" | custom-call | tf_op jit(solution)/shard_map/pack_tables/pallas_call | solution.py:482
  2.2 3.2 %first_source.1 = (bf16[16,16,256]{2,1,0:T(8,128)(2,1)}, bf16[16,16,256]{2,1,0:T(8,128)(2,1)}) custom-call(s32[16]{0:T(128)} %parent_of.5, f32[16,4096]{1,0:T(8,128)} %coef_ref, f32[16,4096]{1,0:T(8,128)} %pot_ref.1, f32[16,16]{1,0:T(8,128)} %to_ref.2), custom_call_target="tpu_custom_call" | custom-call | tf_op jit(solution)/shard_map/first_source/pallas_call | solution.py:492
  5.9 3.4 %collective-permute-start.2 = (bf16[16,16,256]{2,1,0:T(8,128)(2,1)}, bf16[16,16,256]{2,1,0:T(8,128)(2,1)}, u32[]{:S(2)}, u32[]{:S(2)}) collective-permute-start(bf16[16,16,256]{2,1,0:T(8,128)(2,1)} %get-tuple-element.41.refs_0_), channel_id=1, source_target_pairs={{0,3},{1,2},{2,1},{3,0},{4,7},{5,6},{6,5},{7,4},{8,11},{9,10},{10,... | collective-permute-start | bytes 393224 | tf_op jit(solution)/shard_map/ppermute | solution.py:453
  9.3 0.5 collective-permute-start.1
  10.0 6.3 %all-to-all-start = ((s32[32,8,128]{2,1,0:T(8,128)}), s32[32,8,128]{2,1,0:T(8,128)S(1)}, u32[]{:S(2)}, u32[]{:S(2)}) async-start(s32[32,8,128]{2,1,0:T(8,128)} %pack_tables.1), calls=%async_computation | async-start | bytes 262144 | tf_op jit(solution)/shard_map/all_to_all | solution.py:490
  16.2 1.1 copy.27
  18.7 0.7 copy-done.6
  19.4 0.7 copy-done.7
  20.1 0.8 make_constants.1
  20.9 0.6 copy-done.2
  21.5 0.6 copy-done.5
  22.2 2.0 %all-to-all-done.words_ref = s32[32,8,128]{2,1,0:T(8,128)S(1)} async-done(((s32[32,8,128]{2,1,0:T(8,128)}), s32[32,8,128]{2,1,0:T(8,128)S(1)}, u32[]{:S(2)}, u32[]{:S(2)}) %all-to-all-start) | async-done | bytes 131104 | tf_op jit(solution)/shard_map/all_to_all | solution.py:490
  24.1 2.5 %route_slots.1 = (s32[24,128]{1,0:T(8,128)S(1)}, s32[24,128]{1,0:T(8,128)S(1)}) custom-call(s32[3]{0:T(128)S(1)} %pad_add_fusion.info, s32[32,8,128]{2,1,0:T(8,128)S(1)} %all-to-all-done.words_ref), custom_call_target="tpu_custom_call" | custom-call | tf_op jit(solution)/shard_map/route_slots/pallas_call | solution.py:521
  26.7 0.9 copy-done.1
  27.6 16.8 %convolve.2 = (bf16[16,16,256]{2,1,0:T(8,128)(2,1)S(1)}, bf16[16,16,256]{2,1,0:T(8,128)(2,1)S(1)}, bf16[16,16,256]{2,1,0:T(8,128)(2,1)S(1)}, bf16[16,16,256]{2,1,0:T(8,128)(2,1)S(1)}) custom-call(s32[24,128]{1,0:T(8,128)S(1)} %get-tuple-element.40.packed, bf16[16,16,256]{2,1,0:T(8,128)(2,1)S(1)} %copy-done.1, ...), custom_call_target="tpu_custom_call" | custom-call | tf_op jit(solution)/shard_map/convolve/pallas_call | solution.py:431
  44.4 0.6 copy-done.3
  45.1 0.6 copy-done.8
  45.7 0.6 copy-done.9
  46.3 0.6 copy-done.10
  47.0 5.4 %all-to-all-start.1 = ((bf16[16,16,256]{2,1,0:T(8,128)(2,1)}), bf16[16,16,256]{2,1,0:T(8,128)(2,1)}, u32[]{:S(2)}, u32[]{:S(2)}) async-start(bf16[16,16,256]{2,1,0:T(8,128)(2,1)} %get-tuple-element.51), calls=%async_computation.1 | async-start | bytes 262144 | tf_op jit(solution)/shard_map/all_to_all | solution.py:553
  52.4 1.9 %collective-permute-start.7 = (bf16[16,16,256]{2,1,0:T(8,128)(2,1)}, bf16[16,16,256]{2,1,0:T(8,128)(2,1)}, u32[]{:S(2)}, u32[]{:S(2)}) collective-permute-start(bf16[16,16,256]{2,1,0:T(8,128)(2,1)} %copy-done.10), channel_id=1, source_target_pairs={{0,4},{4,0},{8,12},{12,8},{1,5},{5,1},{9,13},{13,9},{2,6},{6,2},{1... | collective-permute-start | bytes 393224 | tf_op jit(solution)/shard_map/ppermute | solution.py:539
  54.3 2.4 %collective-permute-start.8 = (bf16[16,16,256]{2,1,0:T(8,128)(2,1)}, bf16[16,16,256]{2,1,0:T(8,128)(2,1)}, u32[]{:S(2)}, u32[]{:S(2)}) collective-permute-start(bf16[16,16,256]{2,1,0:T(8,128)(2,1)} %copy-done.9), channel_id=1, source_target_pairs={{0,8},{4,12},{8,0},{12,4},{1,9},{5,13},{9,1},{13,5},{2,10},{6,14},... | collective-permute-start | bytes 393224 | tf_op jit(solution)/shard_map/ppermute | solution.py:539
  56.8 0.6 and_select_fusion.came_from
  57.4 1.4 %collective-permute-done.7.refs_1_ = bf16[16,16,256]{2,1,0:T(8,128)(2,1)} collective-permute-done((bf16[16,16,256]{2,1,0:T(8,128)(2,1)}, bf16[16,16,256]{2,1,0:T(8,128)(2,1)}, u32[]{:S(2)}, u32[]{:S(2)}) %collective-permute-start.7) | collective-permute-done | bytes 131104 | tf_op jit(solution)/shard_map/ppermute | solution.py:539
  58.8 5.5 %collective-permute-done.8.refs_2_ = bf16[16,16,256]{2,1,0:T(8,128)(2,1)} collective-permute-done((bf16[16,16,256]{2,1,0:T(8,128)(2,1)}, bf16[16,16,256]{2,1,0:T(8,128)(2,1)}, u32[]{:S(2)}, u32[]{:S(2)}) %collective-permute-start.8) | collective-permute-done | bytes 131104 | tf_op jit(solution)/shard_map/ppermute | solution.py:539
  64.3 2.1 %collective-permute-done.9.refs_3_ = bf16[16,16,256]{2,1,0:T(8,128)(2,1)} collective-permute-done((bf16[16,16,256]{2,1,0:T(8,128)(2,1)}, bf16[16,16,256]{2,1,0:T(8,128)(2,1)}, u32[]{:S(2)}, u32[]{:S(2)}) %collective-permute-start.9) | collective-permute-done | bytes 131104 | tf_op jit(solution)/shard_map/ppermute | solution.py:539
  66.4 4.1 %tree_source.1.refs_0_ = bf16[16,16,256]{2,1,0:T(8,128)(2,1)} custom-call(s32[16]{0:T(128)} %and_select_fusion.came_from, bf16[16,16,256]{2,1,0:T(8,128)(2,1)} %copy-done.3, bf16[16,16,256]{2,1,0:T(8,128)(2,1)} %collective-permute-done.7.refs_1_, bf16[16,16,256]{2,1,0:T(8,128)(2,1)} %collective-permute-done.8.refs_2_, ...), custom_call_target="tpu_custom_call" | custom-call | tf_op jit(solution)/shard_map/tree_source/pallas_call | solution.py:554
  70.5 2.4 %collective-permute-start.12 = (bf16[16,16,256]{2,1,0:T(8,128)(2,1)}, bf16[16,16,256]{2,1,0:T(8,128)(2,1)S(1)}, u32[]{:S(2)}, u32[]{:S(2)}) collective-permute-start(bf16[16,16,256]{2,1,0:T(8,128)(2,1)} %tree_source.1.refs_0_), channel_id=1, source_target_pairs={{0,3},{1,2},{2,1},{3,0},{4,7},{5,6},{6,5},{7,4},{8,11},{9,10},{10,... | collective-permute-start | bytes 393224 | tf_op jit(solution)/shard_map/ppermute | solution.py:453
  72.9 0.6 collective-permute-start.11
  73.5 0.6 collective-permute-start.10
  74.0 2.1 %collective-permute-start.13 = (bf16[16,16,256]{2,1,0:T(8,128)(2,1)}, bf16[16,16,256]{2,1,0:T(8,128)(2,1)S(1)}, u32[]{:S(2)}, u32[]{:S(2)}) collective-permute-start(bf16[16,16,256]{2,1,0:T(8,128)(2,1)} %tree_source.1.refs_0_), channel_id=1, source_target_pairs={{0,16},{16,0},{1,17},{17,1},{2,18},{18,2},{3,19},{19,3},{4,20},{20... | collective-permute-start | bytes 393224 | tf_op jit(solution)/shard_map/ppermute | solution.py:454
  76.1 0.5 collective-permute-done.12.refs_3_
  76.6 2.2 %collective-permute-start.16 = (bf16[16,16,256]{2,1,0:T(8,128)(2,1)S(1)}, bf16[16,16,256]{2,1,0:T(8,128)(2,1)S(1)}, u32[]{:S(2)}, u32[]{:S(2)}) collective-permute-start(bf16[16,16,256]{2,1,0:T(8,128)(2,1)S(1)} %collective-permute-done.12.refs_3_), channel_id=1, source_target_pairs={{0,16},{16,0},{1,17},{17,1},{2,18},{18,2},{3,19},{19,3},{4,20},{20... | collective-permute-start | bytes 393224 | tf_op jit(solution)/shard_map/ppermute | solution.py:454
  78.8 1.4 collective-permute-done.11.refs_2_
  81.2 2.3 %route_again.1.packed = s32[24,128]{1,0:T(8,128)S(1)} custom-call(s32[3]{0:T(128)S(1)} %pad_add_fusion.info, s32[32,8,128]{2,1,0:T(8,128)S(1)} %all-to-all-done.words_ref, s32[24,128]{1,0:T(8,128)S(1)} %get-tuple-element.39.refs_0_), custom_call_target="tpu_custom_call" | custom-call | tf_op jit(solution)/shard_map/route_again/pallas_call | solution.py:562
  83.6 0.9 copy-done
  84.5 19.1 %convolve.3 = (bf16[16,16,256]{2,1,0:T(8,128)(2,1)S(1)}, bf16[16,16,256]{2,1,0:T(8,128)(2,1)S(1)}, bf16[16,16,256]{2,1,0:T(8,128)(2,1)S(1)}, bf16[16,16,256]{2,1,0:T(8,128)(2,1)S(1)}) custom-call(s32[24,128]{1,0:T(8,128)S(1)} %route_again.1.packed, bf16[16,16,256]{2,1,0:T(8,128)(2,1)S(1)} %copy-done, ...), custom_call_target="tpu_custom_call" | custom-call | tf_op jit(solution)/shard_map/convolve/pallas_call | solution.py:431
  103.6 0.6 copy-done.4
  104.3 1.9 %collective-permute-start.17 = (bf16[16,16,256]{2,1,0:T(8,128)(2,1)S(1)}, bf16[16,16,256]{2,1,0:T(8,128)(2,1)S(1)}, u32[]{:S(2)}, u32[]{:S(2)}) collective-permute-start(bf16[16,16,256]{2,1,0:T(8,128)(2,1)S(1)} %get-tuple-element.55), channel_id=1, source_target_pairs={{0,4},{4,0},{8,12},{12,8},{1,5},{5,1},{9,13},{13,9},{2,6},{6,2},{1... | collective-permute-start | bytes 393224 | tf_op jit(solution)/shard_map/ppermute | solution.py:539
  106.2 0.6 collective-permute-start.18
  106.8 1.9 %collective-permute-start.19 = (bf16[16,16,256]{2,1,0:T(8,128)(2,1)S(1)}, bf16[16,16,256]{2,1,0:T(8,128)(2,1)S(1)}, u32[]{:S(2)}, u32[]{:S(2)}) collective-permute-start(bf16[16,16,256]{2,1,0:T(8,128)(2,1)S(1)} %get-tuple-element.57), channel_id=1, source_target_pairs={{0,12},{4,8},{8,4},{12,0},{1,13},{5,9},{9,5},{13,1},{2,14},{6,10},... | collective-permute-start | bytes 393224 | tf_op jit(solution)/shard_map/ppermute | solution.py:539
  108.6 0.6 collective-permute-done.17.refs_1_
  109.2 3.0 %collective-permute-done.18.refs_2_ = bf16[16,16,256]{2,1,0:T(8,128)(2,1)S(1)} collective-permute-done((bf16[16,16,256]{2,1,0:T(8,128)(2,1)S(1)}, bf16[16,16,256]{2,1,0:T(8,128)(2,1)S(1)}, u32[]{:S(2)}, u32[]{:S(2)}) %collective-permute-start.18) | collective-permute-done | bytes 131104 | tf_op jit(solution)/shard_map/ppermute | solution.py:539
  112.2 6.1 %collective-permute-done.19.refs_3_ = bf16[16,16,256]{2,1,0:T(8,128)(2,1)S(1)} collective-permute-done((bf16[16,16,256]{2,1,0:T(8,128)(2,1)S(1)}, bf16[16,16,256]{2,1,0:T(8,128)(2,1)S(1)}, u32[]{:S(2)}, u32[]{:S(2)}) %collective-permute-start.19) | collective-permute-done | bytes 131104 | tf_op jit(solution)/shard_map/ppermute | solution.py:539
  118.3 0.6 copy-done.13
  118.9 2.8 %last_tree.1 = (bf16[16,16,256]{2,1,0:T(8,128)(2,1)}, f32[2,4096]{1,0:T(2,128)}) custom-call(s32[16]{0:T(128)} %and_select_fusion.came_from, bf16[16,16,256]{2,1,0:T(8,128)(2,1)} %copy-done.4, bf16[16,16,256]{2,1,0:T(8,128)(2,1)} %copy-done.11, bf16[16,16,256]{2,1,0:T(8,128)(2,1)} %copy-done.12, bf16[16,16,256]{2,1,0:T(8,128)(2,1)} %copy-done.13, ...), custom_call_target="tpu_custom_call" | custom-call | tf_op jit(solution)/shard_map/last_tree/pallas_call | solution.py:542
  121.7 15.9 %all_to_all.15.field_ref = bf16[16,16,256]{2,1,0:T(8,128)(2,1)} all-to-all(bf16[16,16,256]{2,1,0:T(8,128)(2,1)} %get-tuple-element.58), channel_id=1, replica_groups=mesh['oct'=2,'hi'=4,'lo'=4] {'hi','lo'}, dimensions={0} | all-to-all | bytes 262144 | tf_op jit(solution)/shard_map/all_to_all | solution.py:570
  137.5 1.8 %unpack_fields.1 = f32[16,4096]{1,0:T(8,128)} custom-call(s32[16]{0:T(128)} %parent_of.5, bf16[16,16,256]{2,1,0:T(8,128)(2,1)} %all_to_all.15.field_ref), custom_call_target="tpu_custom_call" | custom-call | tf_op jit(solution)/shard_map/unpack_fields/pallas_call | solution.py:571
  (47 shorter events, 3.2 us)
Async XLA Ops:
  5.4 21.2 %collective-permute-start.3 = (bf16[16,16,256]{2,1,0:T(8,128)(2,1)}, bf16[16,16,256]{2,1,0:T(8,128)(2,1)}, u32[]{:S(2)}, u32[]{:S(2)}) collective-permute-start(bf16[16,16,256]{2,1,0:T(8,128)(2,1)} %get-tuple-element.41.refs_0_), channel_id=1, source_target_pairs={{0,16},{16,0},{1,17},{17,1},{2,18},{18,2},{3,19},{19,3},{4,20},{20... | collective-permute-start | bytes 393224 | tf_op jit(solution)/shard_map/ppermute | solution.py:454
  5.9 11.9 %collective-permute-start.2 = (bf16[16,16,256]{2,1,0:T(8,128)(2,1)}, bf16[16,16,256]{2,1,0:T(8,128)(2,1)}, u32[]{:S(2)}, u32[]{:S(2)}) collective-permute-start(bf16[16,16,256]{2,1,0:T(8,128)(2,1)} %get-tuple-element.41.refs_0_), channel_id=1, source_target_pairs={{0,3},{1,2},{2,1},{3,0},{4,7},{5,6},{6,5},{7,4},{8,11},{9,10},{10,... | collective-permute-start | bytes 393224 | tf_op jit(solution)/shard_map/ppermute | solution.py:453
  9.3 8.7 %collective-permute-start.1 = (bf16[16,16,256]{2,1,0:T(8,128)(2,1)}, bf16[16,16,256]{2,1,0:T(8,128)(2,1)}, u32[]{:S(2)}, u32[]{:S(2)}) collective-permute-start(bf16[16,16,256]{2,1,0:T(8,128)(2,1)} %get-tuple-element.41.refs_0_), channel_id=1, source_target_pairs={{0,2},{1,3},{2,0},{3,1},{4,6},{5,7},{6,4},{7,5},{8,10},{9,11},{10,... | collective-permute-start | bytes 393224 | tf_op jit(solution)/shard_map/ppermute | solution.py:453
  9.8 8.5 %collective-permute-start = (bf16[16,16,256]{2,1,0:T(8,128)(2,1)}, bf16[16,16,256]{2,1,0:T(8,128)(2,1)}, u32[]{:S(2)}, u32[]{:S(2)}) collective-permute-start(bf16[16,16,256]{2,1,0:T(8,128)(2,1)} %get-tuple-element.41.refs_0_), channel_id=1, source_target_pairs={{0,1},{1,0},{2,3},{3,2},{4,5},{5,4},{6,7},{7,6},{8,9},{9,8},{10,11... | collective-permute-start | bytes 393224 | tf_op jit(solution)/shard_map/ppermute | solution.py:453
  10.0 14.2 %all-to-all-start = ((s32[32,8,128]{2,1,0:T(8,128)}), s32[32,8,128]{2,1,0:T(8,128)S(1)}, u32[]{:S(2)}, u32[]{:S(2)}) async-start(s32[32,8,128]{2,1,0:T(8,128)} %pack_tables.1), calls=%async_computation | async-start | bytes 262144 | tf_op jit(solution)/shard_map/all_to_all | solution.py:490
  17.8 8.9 %collective-permute-start.6 = (bf16[16,16,256]{2,1,0:T(8,128)(2,1)}, bf16[16,16,256]{2,1,0:T(8,128)(2,1)}, u32[]{:S(2)}, u32[]{:S(2)}) collective-permute-start(bf16[16,16,256]{2,1,0:T(8,128)(2,1)} %collective-permute-done.2.refs_3_), channel_id=1, source_target_pairs={{0,16},{16,0},{1,17},{17,1},{2,18},{18,2},{3,19},{19,3},{4,20},{20... | collective-permute-start | bytes 393224 | tf_op jit(solution)/shard_map/ppermute | solution.py:454
  18.1 8.6 %collective-permute-start.5 = (bf16[16,16,256]{2,1,0:T(8,128)(2,1)}, bf16[16,16,256]{2,1,0:T(8,128)(2,1)}, u32[]{:S(2)}, u32[]{:S(2)}) collective-permute-start(bf16[16,16,256]{2,1,0:T(8,128)(2,1)} %collective-permute-done.1.refs_2_), channel_id=1, source_target_pairs={{0,16},{16,0},{1,17},{17,1},{2,18},{18,2},{3,19},{19,3},{4,20},{20... | collective-permute-start | bytes 393224 | tf_op jit(solution)/shard_map/ppermute | solution.py:454
  18.3 8.4 %collective-permute-start.4 = (bf16[16,16,256]{2,1,0:T(8,128)(2,1)}, bf16[16,16,256]{2,1,0:T(8,128)(2,1)}, u32[]{:S(2)}, u32[]{:S(2)}) collective-permute-start(bf16[16,16,256]{2,1,0:T(8,128)(2,1)} %collective-permute-done.refs_1_), channel_id=1, source_target_pairs={{0,16},{16,0},{1,17},{17,1},{2,18},{18,2},{3,19},{19,3},{4,20},{20... | collective-permute-start | bytes 393224 | tf_op jit(solution)/shard_map/ppermute | solution.py:454
  18.7 0.7 copy-start.6
  19.4 0.7 copy-start.7
  20.9 0.6 copy-start.2
  21.5 0.6 copy-start.5
  26.7 0.9 copy-start.1
  44.4 0.7 copy-start.3
  45.1 0.6 copy-start.8
  45.7 0.6 copy-start.9
  46.3 0.6 copy-start.10
  47.0 19.4 %all-to-all-start.1 = ((bf16[16,16,256]{2,1,0:T(8,128)(2,1)}), bf16[16,16,256]{2,1,0:T(8,128)(2,1)}, u32[]{:S(2)}, u32[]{:S(2)}) async-start(bf16[16,16,256]{2,1,0:T(8,128)(2,1)} %get-tuple-element.51), calls=%async_computation.1 | async-start | bytes 262144 | tf_op jit(solution)/shard_map/all_to_all | solution.py:553
  52.4 6.4 %collective-permute-start.7 = (bf16[16,16,256]{2,1,0:T(8,128)(2,1)}, bf16[16,16,256]{2,1,0:T(8,128)(2,1)}, u32[]{:S(2)}, u32[]{:S(2)}) collective-permute-start(bf16[16,16,256]{2,1,0:T(8,128)(2,1)} %copy-done.10), channel_id=1, source_target_pairs={{0,4},{4,0},{8,12},{12,8},{1,5},{5,1},{9,13},{13,9},{2,6},{6,2},{1... | collective-permute-start | bytes 393224 | tf_op jit(solution)/shard_map/ppermute | solution.py:539
  54.3 10.1 %collective-permute-start.8 = (bf16[16,16,256]{2,1,0:T(8,128)(2,1)}, bf16[16,16,256]{2,1,0:T(8,128)(2,1)}, u32[]{:S(2)}, u32[]{:S(2)}) collective-permute-start(bf16[16,16,256]{2,1,0:T(8,128)(2,1)} %copy-done.9), channel_id=1, source_target_pairs={{0,8},{4,12},{8,0},{12,4},{1,9},{5,13},{9,1},{13,5},{2,10},{6,14},... | collective-permute-start | bytes 393224 | tf_op jit(solution)/shard_map/ppermute | solution.py:539
  56.6 9.8 %collective-permute-start.9 = (bf16[16,16,256]{2,1,0:T(8,128)(2,1)}, bf16[16,16,256]{2,1,0:T(8,128)(2,1)}, u32[]{:S(2)}, u32[]{:S(2)}) collective-permute-start(bf16[16,16,256]{2,1,0:T(8,128)(2,1)} %copy-done.8), channel_id=1, source_target_pairs={{0,12},{4,8},{8,4},{12,0},{1,13},{5,9},{9,5},{13,1},{2,14},{6,10},... | collective-permute-start | bytes 393224 | tf_op jit(solution)/shard_map/ppermute | solution.py:539
  70.5 6.1 %collective-permute-start.12 = (bf16[16,16,256]{2,1,0:T(8,128)(2,1)}, bf16[16,16,256]{2,1,0:T(8,128)(2,1)S(1)}, u32[]{:S(2)}, u32[]{:S(2)}) collective-permute-start(bf16[16,16,256]{2,1,0:T(8,128)(2,1)} %tree_source.1.refs_0_), channel_id=1, source_target_pairs={{0,3},{1,2},{2,1},{3,0},{4,7},{5,6},{6,5},{7,4},{8,11},{9,10},{10,... | collective-permute-start | bytes 393224 | tf_op jit(solution)/shard_map/ppermute | solution.py:453
  72.9 7.3 %collective-permute-start.11 = (bf16[16,16,256]{2,1,0:T(8,128)(2,1)}, bf16[16,16,256]{2,1,0:T(8,128)(2,1)S(1)}, u32[]{:S(2)}, u32[]{:S(2)}) collective-permute-start(bf16[16,16,256]{2,1,0:T(8,128)(2,1)} %tree_source.1.refs_0_), channel_id=1, source_target_pairs={{0,2},{1,3},{2,0},{3,1},{4,6},{5,7},{6,4},{7,5},{8,10},{9,11},{10,... | collective-permute-start | bytes 393224 | tf_op jit(solution)/shard_map/ppermute | solution.py:453
  73.5 7.3 %collective-permute-start.10 = (bf16[16,16,256]{2,1,0:T(8,128)(2,1)}, bf16[16,16,256]{2,1,0:T(8,128)(2,1)S(1)}, u32[]{:S(2)}, u32[]{:S(2)}) collective-permute-start(bf16[16,16,256]{2,1,0:T(8,128)(2,1)} %tree_source.1.refs_0_), channel_id=1, source_target_pairs={{0,1},{1,0},{2,3},{3,2},{4,5},{5,4},{6,7},{7,6},{8,9},{9,8},{10,11... | collective-permute-start | bytes 393224 | tf_op jit(solution)/shard_map/ppermute | solution.py:453
  74.0 9.5 %collective-permute-start.13 = (bf16[16,16,256]{2,1,0:T(8,128)(2,1)}, bf16[16,16,256]{2,1,0:T(8,128)(2,1)S(1)}, u32[]{:S(2)}, u32[]{:S(2)}) collective-permute-start(bf16[16,16,256]{2,1,0:T(8,128)(2,1)} %tree_source.1.refs_0_), channel_id=1, source_target_pairs={{0,16},{16,0},{1,17},{17,1},{2,18},{18,2},{3,19},{19,3},{4,20},{20... | collective-permute-start | bytes 393224 | tf_op jit(solution)/shard_map/ppermute | solution.py:454
  76.6 6.9 %collective-permute-start.16 = (bf16[16,16,256]{2,1,0:T(8,128)(2,1)S(1)}, bf16[16,16,256]{2,1,0:T(8,128)(2,1)S(1)}, u32[]{:S(2)}, u32[]{:S(2)}) collective-permute-start(bf16[16,16,256]{2,1,0:T(8,128)(2,1)S(1)} %collective-permute-done.12.refs_3_), channel_id=1, source_target_pairs={{0,16},{16,0},{1,17},{17,1},{2,18},{18,2},{3,19},{19,3},{4,20},{20... | collective-permute-start | bytes 393224 | tf_op jit(solution)/shard_map/ppermute | solution.py:454
  80.2 3.3 %collective-permute-start.15 = (bf16[16,16,256]{2,1,0:T(8,128)(2,1)S(1)}, bf16[16,16,256]{2,1,0:T(8,128)(2,1)S(1)}, u32[]{:S(2)}, u32[]{:S(2)}) collective-permute-start(bf16[16,16,256]{2,1,0:T(8,128)(2,1)S(1)} %collective-permute-done.11.refs_2_), channel_id=1, source_target_pairs={{0,16},{16,0},{1,17},{17,1},{2,18},{18,2},{3,19},{19,3},{4,20},{20... | collective-permute-start | bytes 393224 | tf_op jit(solution)/shard_map/ppermute | solution.py:454
  80.7 2.8 %collective-permute-start.14 = (bf16[16,16,256]{2,1,0:T(8,128)(2,1)S(1)}, bf16[16,16,256]{2,1,0:T(8,128)(2,1)S(1)}, u32[]{:S(2)}, u32[]{:S(2)}) collective-permute-start(bf16[16,16,256]{2,1,0:T(8,128)(2,1)S(1)} %collective-permute-done.10.refs_1_), channel_id=1, source_target_pairs={{0,16},{16,0},{1,17},{17,1},{2,18},{18,2},{3,19},{19,3},{4,20},{20... | collective-permute-start | bytes 393224 | tf_op jit(solution)/shard_map/ppermute | solution.py:454
  83.6 0.9 copy-start
  103.6 0.7 copy-start.4
  104.3 5.0 %collective-permute-start.17 = (bf16[16,16,256]{2,1,0:T(8,128)(2,1)S(1)}, bf16[16,16,256]{2,1,0:T(8,128)(2,1)S(1)}, u32[]{:S(2)}, u32[]{:S(2)}) collective-permute-start(bf16[16,16,256]{2,1,0:T(8,128)(2,1)S(1)} %get-tuple-element.55), channel_id=1, source_target_pairs={{0,4},{4,0},{8,12},{12,8},{1,5},{5,1},{9,13},{13,9},{2,6},{6,2},{1... | collective-permute-start | bytes 393224 | tf_op jit(solution)/shard_map/ppermute | solution.py:539
  106.2 6.0 %collective-permute-start.18 = (bf16[16,16,256]{2,1,0:T(8,128)(2,1)S(1)}, bf16[16,16,256]{2,1,0:T(8,128)(2,1)S(1)}, u32[]{:S(2)}, u32[]{:S(2)}) collective-permute-start(bf16[16,16,256]{2,1,0:T(8,128)(2,1)S(1)} %get-tuple-element.56), channel_id=1, source_target_pairs={{0,8},{4,12},{8,0},{12,4},{1,9},{5,13},{9,1},{13,5},{2,10},{6,14},... | collective-permute-start | bytes 393224 | tf_op jit(solution)/shard_map/ppermute | solution.py:539
  106.8 11.5 %collective-permute-start.19 = (bf16[16,16,256]{2,1,0:T(8,128)(2,1)S(1)}, bf16[16,16,256]{2,1,0:T(8,128)(2,1)S(1)}, u32[]{:S(2)}, u32[]{:S(2)}) collective-permute-start(bf16[16,16,256]{2,1,0:T(8,128)(2,1)S(1)} %get-tuple-element.57), channel_id=1, source_target_pairs={{0,12},{4,8},{8,4},{12,0},{1,13},{5,9},{9,5},{13,1},{2,14},{6,10},... | collective-permute-start | bytes 393224 | tf_op jit(solution)/shard_map/ppermute | solution.py:539
  109.2 9.7 %copy-start.11 = (bf16[16,16,256]{2,1,0:T(8,128)(2,1)}, bf16[16,16,256]{2,1,0:T(8,128)(2,1)S(1)}, u32[]{:S(2)}) copy-start(bf16[16,16,256]{2,1,0:T(8,128)(2,1)S(1)} %collective-permute-done.17.refs_1_) | copy-start | bytes 393220
  112.2 6.1 %copy-start.12 = (bf16[16,16,256]{2,1,0:T(8,128)(2,1)}, bf16[16,16,256]{2,1,0:T(8,128)(2,1)S(1)}, u32[]{:S(2)}) copy-start(bf16[16,16,256]{2,1,0:T(8,128)(2,1)S(1)} %collective-permute-done.18.refs_2_) | copy-start | bytes 393220
  118.3 0.6 copy-start.13

commit v6 on v5

--- a/solution.py
+++ b/solution.py
@@ -91,7 +91,8 @@
         out_ref[d] = words
 
 
-def first_kernel(parent_of, coef_ref, pot_ref, to_ref, out_ref, pot_out, rows_ref):
+def first_kernel(parent_of, info, coef_ref, pot_ref, to_ref, *refs):
+    *out_refs, rows_ref = refs
     order_k = to_ref.shape[0]
     plane = order_k * order_k
     to_high, to_low, back_high, back_low = spread_columns(to_ref[...])
@@ -107,15 +108,19 @@
     values = mm_halves(value_x, halves(mm_halves(halves(by_x(coef_ref)), value_pair)))
     product = values * (by_x(pot_ref) + 0.25 * values * values)
     source = mm_halves(source_x, halves(mm_halves(halves(product), back_pair)))
-    out_ref[...] = source.astype(jnp.bfloat16).reshape(out_ref.shape)
-    peers = rows_ref.shape[0]
-    if peers > pot_ref.shape[0]:
+    boxes = pot_ref.shape[0]
+    source = source.astype(jnp.bfloat16).reshape(boxes, order_k, plane)
+    peers, lo_count = rows_ref.shape[0], len(out_refs)
+    if peers > boxes:
         rows_ref[...] = jnp.zeros_like(rows_ref)
-    for b in range(pot_ref.shape[0]):
-        peer = parent_of[b] * 8 // pot_ref.shape[0] % peers
+    for b in range(boxes):
+        peer = parent_of[b] * 8 // boxes % peers
         for x in range(order_k):
             rows_ref[peer, x : x + 1, :] = pot_ref[b : b + 1, x * plane : (x + 1) * plane]
-    pot_out[...] = rows_ref[...].astype(jnp.bfloat16)
+    for r, out_ref in enumerate(out_refs):
+        out_ref[:boxes] = source
+        for h in range(peers // lo_count):
+            out_ref[boxes + h] = rows_ref[h * lo_count + (info[2] ^ r)].astype(jnp.bfloat16)
 
 
 def route_kernel(dims, first, info, words_ref, *refs):
@@ -234,14 +239,14 @@
     )
 
 
-def tree_kernel(last, part_count, came_from, *refs):
+def tree_kernel(last, part_count, boxes, came_from, info, *refs):
     parts = refs[:part_count]
     mats_ref, lift_ref, drop_ref = refs[part_count : part_count + 3]
     rest = refs[part_count + 3 :]
-    gathered = parts[0][...].astype(jnp.float32)
+    gathered = parts[0][:boxes].astype(jnp.float32)
     for part in parts[1:]:
-        gathered = gathered + part[...].astype(jnp.float32)
-    boxes, order_k, plane = gathered.shape
+        gathered = gathered + part[:boxes].astype(jnp.float32)
+    order_k, plane = gathered.shape[1:]
     parent_count = boxes // 8
 
     def matrix(n):
@@ -271,8 +276,15 @@
             for i in range(order_k):
                 parent_ref[p : p + 1, i * plane : (i + 1) * plane] = own[p * order_k + i : p * order_k + i + 1]
     else:
-        pot_ref, out_ref = rest
-        potential = jnp.concatenate([pot_ref[came_from[b]] for b in range(boxes)], axis=0).astype(jnp.float32)
+        out_ref, pot_ref = rest
+        lo_count = parts[0].shape[0] - boxes
+        for r, part in enumerate(parts):
+            pot_ref[r * lo_count : (r + 1) * lo_count] = part[boxes:]
+        spots = [
+            (came_from[b] // lo_count ^ info[1]) * lo_count + (came_from[b] % lo_count ^ info[2])
+            for b in range(boxes)
+        ]
+        potential = jnp.concatenate([pot_ref[spot] for spot in spots], axis=0).astype(jnp.float32)
         current = halves(jnp.concatenate(fields, axis=0))
         values = mm_halves(matrix(10), halves(mm_halves(current, matrix(8))))
         product = values * (potential + 0.25 * values * values)
@@ -289,8 +301,8 @@
             out_ref[b : b + 1, x * plane : (x + 1) * plane] = box[x : x + 1]
 
 
-def conv_kernel(dims, packed, *refs):
-    term_count, order_k, disp_count, source_count, dest_count = dims
+def conv_kernel(dims, packed, info, *refs):
+    term_count, order_k, disp_count, source_count, dest_count, block_boxes = dims
     source_refs = refs[:source_count]
     xl_ref, w_hbm = refs[source_count : source_count + 2]
     out_refs = refs[source_count + 2 : source_count + 2 + dest_count]
@@ -299,7 +311,7 @@
     list_rows = packed.shape[0] - 7
     half = term_count // 2
     depth = term_count * order_k
-    block_boxes = out_refs[0].shape[0]
+    extra = out_refs[0].shape[0] - block_boxes
     dest_rows = dest_count * block_boxes
     def load_row(ll):
         for m in range(term_count):
@@ -311,7 +323,7 @@
     for total in totals:
         total[...] = jnp.zeros_like(total)
     for n, ref in enumerate(source_refs):
-        held[pl.ds(n * block_boxes, block_boxes)] = ref[...]
+        held[pl.ds(n * block_boxes, block_boxes)] = ref[:block_boxes]
 
     def push_w(ll, j, reg):
         for unit in range(2):
@@ -404,7 +416,9 @@
     lax.fori_loop(0, disp_count, per_disp, 0)
     for r, out_ref in enumerate(out_refs):
         part = pl.ds(r * block_boxes, block_boxes)
-        out_ref[...] = sum(total[part] for total in totals).astype(jnp.bfloat16)
+        out_ref[:block_boxes] = sum(total[part] for total in totals).astype(jnp.bfloat16)
+        for l in range(extra):
+            out_ref[block_boxes + l] = source_refs[l][block_boxes + (info[1] ^ r)]
 
 
 def shifted_factors(x_kernels):
@@ -422,16 +436,15 @@
     return jnp.stack([parts[p] for p in range(len(parts))], axis=1)
 
 
-def convolve(sources, shifted, yz_kernels, packed, dest_count, term_count, order_k):
+def convolve(sources, shifted, yz_kernels, packed, info, dest_count, term_count, order_k, block_boxes, extra):
     plane = order_k * order_k
-    block_boxes = sources[0].shape[0]
     disp_count = yz_kernels.shape[1] // (term_count * plane)
-    dims = (term_count, order_k, disp_count, len(sources), dest_count)
-    tile = jax.ShapeDtypeStruct((block_boxes, order_k, plane), jnp.bfloat16)
+    dims = (term_count, order_k, disp_count, len(sources), dest_count, block_boxes)
+    tile = jax.ShapeDtypeStruct((block_boxes + extra, order_k, plane), jnp.bfloat16)
     return pl.pallas_call(
         functools.partial(conv_kernel, dims),
         out_shape=[tile] * dest_count,
-        in_specs=[SMEM] + [VMEM] * (len(sources) + 1) + [ANY],
+        in_specs=[SMEM] * 2 + [VMEM] * (len(sources) + 1) + [ANY],
         out_specs=[VMEM] * dest_count,
         scratch_shapes=[
             pltpu.VMEM((disp_count, term_count, plane, plane), jnp.bfloat16),
@@ -442,15 +455,15 @@
         ],
         compiler_params=pltpu.CompilerParams(vmem_limit_bytes=48 * MIB),
         name="convolve",
-    )(packed, *sources, shifted, yz_kernels)
+    )(packed, info, *sources, shifted, yz_kernels)
 
 
 def flips(count, step):
     return [(i, i ^ step) for i in range(count)]
 
 
-def gather_sources(source, lo_count):
-    near = [source] + [lax.ppermute(source, "lo", flips(lo_count, r)) for r in range(1, lo_count)]
+def gather_sources(blocks):
+    near = [blocks[0]] + [lax.ppermute(block, "lo", flips(len(blocks), r)) for r, block in enumerate(blocks) if r]
     return near + [lax.ppermute(block, "oct", flips(2, 1)) for block in near]
 
 
@@ -489,17 +502,18 @@
     words, coefficients = lax.optimization_barrier((words, coefficients))
     words = lax.all_to_all(words, ("oct", "hi", "lo"), 0, 0, tiled=True)
 
-    source, send_potential = pl.pallas_call(
+    blocks = pl.pallas_call(
         first_kernel,
-        out_shape=[jax.ShapeDtypeStruct(tile, jnp.bfloat16), peer_tiles],
-        in_specs=[SMEM] + [VMEM] * 3,
-        out_specs=[VMEM] * 2,
+        out_shape=[jax.ShapeDtypeStruct((box_count + hi_count, order_k, plane), jnp.bfloat16)] * lo_count,
+        in_specs=[SMEM] * 2 + [VMEM] * 3,
+        out_specs=[VMEM] * lo_count,
         scratch_shapes=[pltpu.VMEM(peer_tiles.shape, jnp.float32)],
         name="first_source",
-    )(parent_of, coefficients, potential, to_values)
+    )(parent_of, info, coefficients, potential, to_values)
 
     parents = box_count // 8 * order_k
-    source, late_values = lax.optimization_barrier((source, to_values))
+    first, late_values = lax.optimization_barrier((blocks[0], to_values))
+    blocks = [first] + list(blocks[1:])
     fixed = pl.pallas_call(
         constants_kernel,
         out_shape=[
@@ -531,13 +545,20 @@
 
     for iteration in range(ITERS):
         last = iteration == ITERS - 1
-        sources = gather_sources(source, lo_count)
-        outs = convolve(sources, shifted, yz_kernels, packed, hi_count, term_count, order_k)
-        if not last:
-            own_part, send_potential = lax.optimization_barrier((outs[0], send_potential))
-            outs = [own_part] + list(outs[1:])
+        outs = convolve(
+            gather_sources(blocks),
+            shifted,
+            yz_kernels,
+            packed,
+            info,
+            hi_count,
+            term_count,
+            order_k,
+            box_count,
+            0 if last else lo_count,
+        )
         parts = [outs[0]] + [lax.ppermute(outs[r], "hi", flips(hi_count, r)) for r in range(1, hi_count)]
-        kernel = functools.partial(tree_kernel, last, hi_count)
+        kernel = functools.partial(tree_kernel, last, hi_count, box_count)
         if last:
             fields, parents = pl.pallas_call(
                 kernel,
@@ -545,20 +566,21 @@
                     peer_tiles,
                     jax.ShapeDtypeStruct((box_count // 8, order_k * plane), jnp.float32),
                 ],
-                in_specs=[SMEM] + [VMEM] * (hi_count + 3),
+                in_specs=[SMEM] * 2 + [VMEM] * (hi_count + 3),
                 out_specs=[VMEM] * 2,
                 name="last_tree",
-            )(came_from, *parts, *fixed)
+            )(came_from, info, *parts, *fixed)
         else:
-            moved_potential = lax.all_to_all(send_potential, ("hi", "lo"), 0, 0, tiled=True)
             source = pl.pallas_call(
                 kernel,
                 out_shape=jax.ShapeDtypeStruct(tile, jnp.bfloat16),
-                in_specs=[SMEM] + [VMEM] * (hi_count + 4),
+                in_specs=[SMEM] * 2 + [VMEM] * (hi_count + 3),
                 out_specs=VMEM,
+                scratch_shapes=[pltpu.VMEM(peer_tiles.shape, jnp.bfloat16)],
                 name="tree_source",
-            )(came_from, *parts, *fixed, moved_potential)
+            )(came_from, info, *parts, *fixed)
             source, words = lax.optimization_barrier((source, words))
+            blocks = [source] * lo_count
             packed = pl.pallas_call(
                 functools.partial(route_kernel, sort_dims, False),
                 out_shape=list_shape,

time: 139 us -> 136 us (0.978)
  starting transfers between devices: 34.5 us -> 27.5 us
  waiting for transfers between devices: 22.5 us -> 27.9 us
  blocking collectives: 15.9 us -> 12 us
    all_to_all x1 -> x0, starting transfers between devices: 5.39 us -> none  [shards(): lax.all_to_all(send_potential, ('hi', 'lo'), 0, 0, tiled=True)]
    ppermute x6, waiting for transfers between devices: 1.92 us -> 7.27 us  [gather_sources(): lax.ppermute(block, 'lo', flips(len(blocks), r))]
    ppermute x8, starting transfers between devices: 6.46 us -> 1.17 us  [gather_sources(): return near + [lax.ppermute(block, 'oct', flips(2, 1)) for block in near]]
    all_to_all x1, blocking collectives: 15.9 us -> 12 us  [shards(): returned = lax.all_to_all(fields, ('hi', 'lo'), 0, 0, tiled=True)]
    ppermute x6, starting transfers between devices: 8.84 us -> 12.1 us  [shards(): lax.ppermute(outs[r], 'hi', flips(hi_count, r))]
    ppermute x6, waiting for transfers between devices: 18.6 us -> 20.6 us  [shards(): lax.ppermute(outs[r], 'hi', flips(hi_count, r))]
    all_to_all x1, waiting for transfers between devices: 1.97 us -> 0.01 us  [shards(): words = lax.all_to_all(words, ('oct', 'hi', 'lo'), 0, 0, tiled=True)]
    unnamed x35 -> x41, local copies, waits for them, and re-layouts: 8.54 us -> 9.39 us
  transfers between devices with their start and end apart: 22 -> 21, of which waited for: 9 -> 8; matrix products, arithmetic and copies ran while one was open for 2% -> 2% of each run, Pallas kernels for 4% -> 7%
where the time goes in v6:
time: 136 us; the launch traced here: 135 us
  Pallas kernels  55 us (40%)
  waiting for transfers between devices  27.9 us (21%)
  starting transfers between devices  27.5 us (20%)
  blocking collectives  12 us (9%)
  local copies, waits for them, and re-layouts  10.7 us (8%)
    pallas_call x2, Pallas kernels, convolve(): pl.pallas_call(functools.partial(conv_kernel, dims), out_shape=[tile] * d...  35.7 us
    ppermute x6, waiting for transfers between devices, shards(): lax.ppermute(outs[r], 'hi', flips(hi_count, r))  20.6 us
    ppermute x6, starting transfers between devices, shards(): lax.ppermute(outs[r], 'hi', flips(hi_count, r))  12.1 us
    all_to_all x1, blocking collectives, shards(): returned = lax.all_to_all(fields, ('hi', 'lo'), 0, 0, tiled=True)  12 us
    unnamed x41, local copies, waits for them, and re-layouts  9.39 us
    all_to_all x1, starting transfers between devices, shards(): words = lax.all_to_all(words, ('oct', 'hi', 'lo'), 0, 0, tiled=True)  7.3 us
    ppermute x6, waiting for transfers between devices, gather_sources(): lax.ppermute(block, 'lo', flips(len(blocks), r))  7.27 us
    ppermute x6, starting transfers between devices, gather_sources(): lax.ppermute(block, 'lo', flips(len(blocks), r))  6.98 us
  transfers between devices with their start and end apart: 21, of which 8 were waited for; matrix products, arithmetic and copies ran while one was open for 2% of the time, Pallas kernels for 7%

profile of v6, /device:TPU:0, one launch (start us, length us, event | category | flops | bytes accessed | tf_op | source)
XLA Modules:
  0.0 135.3 jit_solution(16832146709039593928)
XLA Ops:
  0.6 1.6 %pack_tables.1 = s32[32,8,128]{2,1,0:T(8,128)} custom-call(s32[16]{0:T(128)} %parent_of.5, s32[16]{0:T(128)} %octant.1, s32[16,16]{1,0:T(8,128)} %disp_ref.1, s32[16,16]{1,0:T(8,128)} %dest_ref.1), custom_call_target="tpu_custom_call" | custom-call | tf_op jit(solution)/shard_map/pack_tables/pallas_call | solution.py:495
  2.2 7.3 %all-to-all-start = ((s32[32,8,128]{2,1,0:T(8,128)}), s32[32,8,128]{2,1,0:T(8,128)S(1)}, u32[]{:S(2)}, u32[]{:S(2)}) async-start(s32[32,8,128]{2,1,0:T(8,128)} %pack_tables.1), calls=%async_computation | async-start | bytes 262144 | tf_op jit(solution)/shard_map/all_to_all | solution.py:503
  9.5 0.7 pad_add_fusion.info
  10.2 3.4 %first_source.1 = (bf16[20,16,256]{2,1,0:T(8,128)(2,1)}, bf16[20,16,256]{2,1,0:T(8,128)(2,1)}, bf16[20,16,256]{2,1,0:T(8,128)(2,1)}, bf16[20,16,256]{2,1,0:T(8,128)(2,1)}) custom-call(s32[16]{0:T(128)} %parent_of.5, s32[3]{0:T(128)} %pad_add_fusion.info, f32[16,4096]{1,0:T(8,128)} %coef_ref, f32[16,4096]{1,0:T(8,128)} %pot_ref.1, f32[16,16]{1,0:T(8,128)} %to_ref.2), custom_call_target="tpu_custom_call" | custom-call | tf_op jit(solution)/shard_map/first_source/pallas_call | solution.py:505
  13.6 0.2 collective-permute-start.3
  13.9 1.7 %collective-permute-start = (bf16[20,16,256]{2,1,0:T(8,128)(2,1)}, bf16[20,16,256]{2,1,0:T(8,128)(2,1)}, u32[]{:S(2)}, u32[]{:S(2)}) collective-permute-start(bf16[20,16,256]{2,1,0:T(8,128)(2,1)} %get-tuple-element.42), channel_id=1, source_target_pairs={{0,1},{1,0},{2,3},{3,2},{4,5},{5,4},{6,7},{7,6},{8,9},{9,8},{10,11... | collective-permute-start | bytes 491528 | tf_op jit(solution)/shard_map/ppermute | solution.py:466
  15.5 1.5 %collective-permute-start.1 = (bf16[20,16,256]{2,1,0:T(8,128)(2,1)}, bf16[20,16,256]{2,1,0:T(8,128)(2,1)}, u32[]{:S(2)}, u32[]{:S(2)}) collective-permute-start(bf16[20,16,256]{2,1,0:T(8,128)(2,1)} %get-tuple-element.43), channel_id=1, source_target_pairs={{0,2},{1,3},{2,0},{3,1},{4,6},{5,7},{6,4},{7,5},{8,10},{9,11},{10,... | collective-permute-start | bytes 491528 | tf_op jit(solution)/shard_map/ppermute | solution.py:466
  17.0 0.3 collective-permute-start.2
  17.4 1.1 copy.27
  18.9 0.7 copy-done.6
  19.6 0.7 copy-done.10
  20.3 0.8 make_constants.1
  21.2 0.6 copy-done.3
  21.8 0.6 copy-done.5
  22.4 3.2 %collective-permute-done.1.refs_2_ = bf16[20,16,256]{2,1,0:T(8,128)(2,1)} collective-permute-done((bf16[20,16,256]{2,1,0:T(8,128)(2,1)}, bf16[20,16,256]{2,1,0:T(8,128)(2,1)}, u32[]{:S(2)}, u32[]{:S(2)}) %collective-permute-start.1) | collective-permute-done | bytes 163872 | tf_op jit(solution)/shard_map/ppermute | solution.py:466
  25.5 0.5 collective-permute-start.6
  26.1 0.7 copy-done.7
  26.8 2.5 %route_slots.1 = (s32[24,128]{1,0:T(8,128)S(1)}, s32[24,128]{1,0:T(8,128)S(1)}) custom-call(s32[3]{0:T(128)S(1)} %copy-done.7, s32[32,8,128]{2,1,0:T(8,128)S(1)} %all-to-all-done.words_ref), custom_call_target="tpu_custom_call" | custom-call | tf_op jit(solution)/shard_map/route_slots/pallas_call | solution.py:535
  29.4 0.9 copy-done.1
  30.3 0.7 copy-done.8
  31.0 18.3 %convolve.2 = (bf16[20,16,256]{2,1,0:T(8,128)(2,1)S(1)}, bf16[20,16,256]{2,1,0:T(8,128)(2,1)S(1)}, bf16[20,16,256]{2,1,0:T(8,128)(2,1)S(1)}, bf16[20,16,256]{2,1,0:T(8,128)(2,1)S(1)}) custom-call(s32[24,128]{1,0:T(8,128)S(1)} %get-tuple-element.40.packed, s32[3]{0:T(128)S(1)} %copy-done.8, bf16[20,16,256]{2,1,0:T(8,128)(2,1)S(1)} %copy-done.1, ...), custom_call_target="tpu_custom_call" | custom-call | tf_op jit(solution)/shard_map/convolve/pallas_call | solution.py:444
  49.3 0.7 copy-done.2
  50.0 0.3 collective-permute-start.7
  50.3 4.7 %collective-permute-start.8 = (bf16[20,16,256]{2,1,0:T(8,128)(2,1)S(1)}, bf16[20,16,256]{2,1,0:T(8,128)(2,1)S(1)}, u32[]{:S(2)}, u32[]{:S(2)}) collective-permute-start(bf16[20,16,256]{2,1,0:T(8,128)(2,1)S(1)} %get-tuple-element.47), channel_id=1, source_target_pairs={{0,8},{4,12},{8,0},{12,4},{1,9},{5,13},{9,1},{13,5},{2,10},{6,14},... | collective-permute-start | bytes 491528 | tf_op jit(solution)/shard_map/ppermute | solution.py:560
  55.0 0.5 and_select_fusion.came_from
  55.5 1.8 %collective-permute-done.7.refs_1_ = bf16[20,16,256]{2,1,0:T(8,128)(2,1)S(1)} collective-permute-done((bf16[20,16,256]{2,1,0:T(8,128)(2,1)S(1)}, bf16[20,16,256]{2,1,0:T(8,128)(2,1)S(1)}, u32[]{:S(2)}, u32[]{:S(2)}) %collective-permute-start.7) | collective-permute-done | bytes 163872 | tf_op jit(solution)/shard_map/ppermute | solution.py:560
  57.4 9.2 %collective-permute-done.8.refs_2_ = bf16[20,16,256]{2,1,0:T(8,128)(2,1)S(1)} collective-permute-done((bf16[20,16,256]{2,1,0:T(8,128)(2,1)S(1)}, bf16[20,16,256]{2,1,0:T(8,128)(2,1)S(1)}, u32[]{:S(2)}, u32[]{:S(2)}) %collective-permute-start.8) | collective-permute-done | bytes 163872 | tf_op jit(solution)/shard_map/ppermute | solution.py:560
  66.6 0.7 copy-done.12
  67.3 0.7 copy-done.13
  67.9 4.1 %tree_source.1.refs_0_ = bf16[16,16,256]{2,1,0:T(8,128)(2,1)} custom-call(s32[16]{0:T(128)} %and_select_fusion.came_from, s32[3]{0:T(128)} %pad_add_fusion.info, bf16[20,16,256]{2,1,0:T(8,128)(2,1)} %copy-done.2, bf16[20,16,256]{2,1,0:T(8,128)(2,1)} %copy-done.11, bf16[20,16,256]{2,1,0:T(8,128)(2,1)} %copy-done.12, bf16[20,16,256]{2,1,0:T(8,128)(2,1)} %copy-done.13, ...), custom_call_target="tpu_custom_call" | custom-call | tf_op jit(solution)/shard_map/tree_source/pallas_call | solution.py:574
  72.1 1.7 %collective-permute-start.12 = (bf16[16,16,256]{2,1,0:T(8,128)(2,1)}, bf16[16,16,256]{2,1,0:T(8,128)(2,1)S(1)}, u32[]{:S(2)}, u32[]{:S(2)}) collective-permute-start(bf16[16,16,256]{2,1,0:T(8,128)(2,1)} %tree_source.1.refs_0_), channel_id=1, source_target_pairs={{0,3},{1,2},{2,1},{3,0},{4,7},{5,6},{6,5},{7,4},{8,11},{9,10},{10,... | collective-permute-start | bytes 393224 | tf_op jit(solution)/shard_map/ppermute | solution.py:466
  73.8 0.5 collective-permute-start.11
  74.3 1.3 collective-permute-start.10
  75.5 2.6 %collective-permute-done.12.refs_3_ = bf16[16,16,256]{2,1,0:T(8,128)(2,1)S(1)} collective-permute-done((bf16[16,16,256]{2,1,0:T(8,128)(2,1)}, bf16[16,16,256]{2,1,0:T(8,128)(2,1)S(1)}, u32[]{:S(2)}, u32[]{:S(2)}) %collective-permute-start.12) | collective-permute-done | bytes 131104 | tf_op jit(solution)/shard_map/ppermute | solution.py:466
  78.2 1.3 collective-permute-done.11.refs_2_
  79.7 0.4 collective-permute-start.14
  80.1 2.3 %route_again.1.packed = s32[24,128]{1,0:T(8,128)S(1)} custom-call(s32[3]{0:T(128)S(1)} %copy-done.9, s32[32,8,128]{2,1,0:T(8,128)S(1)} %all-to-all-done.words_ref, s32[24,128]{1,0:T(8,128)S(1)} %get-tuple-element.39.refs_0_), custom_call_target="tpu_custom_call" | custom-call | tf_op jit(solution)/shard_map/route_again/pallas_call | solution.py:584
  82.5 0.9 copy-done
  83.4 17.4 %convolve.3 = (bf16[16,16,256]{2,1,0:T(8,128)(2,1)S(1)}, bf16[16,16,256]{2,1,0:T(8,128)(2,1)S(1)}, bf16[16,16,256]{2,1,0:T(8,128)(2,1)S(1)}, bf16[16,16,256]{2,1,0:T(8,128)(2,1)S(1)}) custom-call(s32[24,128]{1,0:T(8,128)S(1)} %route_again.1.packed, s32[3]{0:T(128)S(1)} %copy-done.9, bf16[16,16,256]{2,1,0:T(8,128)(2,1)S(1)} %copy-done, ...), custom_call_target="tpu_custom_call" | custom-call | tf_op jit(solution)/shard_map/convolve/pallas_call | solution.py:444
  100.8 0.6 copy-done.4
  101.4 4.7 %collective-permute-start.17 = (bf16[16,16,256]{2,1,0:T(8,128)(2,1)S(1)}, bf16[16,16,256]{2,1,0:T(8,128)(2,1)S(1)}, u32[]{:S(2)}, u32[]{:S(2)}) collective-permute-start(bf16[16,16,256]{2,1,0:T(8,128)(2,1)S(1)} %get-tuple-element.55), channel_id=1, source_target_pairs={{0,4},{4,0},{8,12},{12,8},{1,5},{5,1},{9,13},{13,9},{2,6},{6,2},{1... | collective-permute-start | bytes 393224 | tf_op jit(solution)/shard_map/ppermute | solution.py:560
  106.1 2.4 %collective-permute-start.19 = (bf16[16,16,256]{2,1,0:T(8,128)(2,1)S(1)}, bf16[16,16,256]{2,1,0:T(8,128)(2,1)S(1)}, u32[]{:S(2)}, u32[]{:S(2)}) collective-permute-start(bf16[16,16,256]{2,1,0:T(8,128)(2,1)S(1)} %get-tuple-element.57), channel_id=1, source_target_pairs={{0,12},{4,8},{8,4},{12,0},{1,13},{5,9},{9,5},{13,1},{2,14},{6,10},... | collective-permute-start | bytes 393224 | tf_op jit(solution)/shard_map/ppermute | solution.py:560
  108.5 2.0 %collective-permute-done.17.refs_1_ = bf16[16,16,256]{2,1,0:T(8,128)(2,1)S(1)} collective-permute-done((bf16[16,16,256]{2,1,0:T(8,128)(2,1)S(1)}, bf16[16,16,256]{2,1,0:T(8,128)(2,1)S(1)}, u32[]{:S(2)}, u32[]{:S(2)}) %collective-permute-start.17) | collective-permute-done | bytes 131104 | tf_op jit(solution)/shard_map/ppermute | solution.py:560
  110.4 7.6 %collective-permute-done.18.refs_2_ = bf16[16,16,256]{2,1,0:T(8,128)(2,1)S(1)} collective-permute-done((bf16[16,16,256]{2,1,0:T(8,128)(2,1)S(1)}, bf16[16,16,256]{2,1,0:T(8,128)(2,1)S(1)}, u32[]{:S(2)}, u32[]{:S(2)}) %collective-permute-start.18) | collective-permute-done | bytes 131104 | tf_op jit(solution)/shard_map/ppermute | solution.py:560
  118.0 0.7 copy-done.16
  118.7 2.8 %last_tree.1 = (bf16[16,16,256]{2,1,0:T(8,128)(2,1)}, f32[2,4096]{1,0:T(2,128)}) custom-call(s32[16]{0:T(128)} %and_select_fusion.came_from, s32[3]{0:T(128)} %pad_add_fusion.info, bf16[16,16,256]{2,1,0:T(8,128)(2,1)} %copy-done.4, bf16[16,16,256]{2,1,0:T(8,128)(2,1)} %copy-done.14, bf16[16,16,256]{2,1,0:T(8,128)(2,1)} %copy-done.15, ...), custom_call_target="tpu_custom_call" | custom-call | tf_op jit(solution)/shard_map/last_tree/pallas_call | solution.py:563
  121.5 12.0 %all_to_all.10.field_ref = bf16[16,16,256]{2,1,0:T(8,128)(2,1)} all-to-all(bf16[16,16,256]{2,1,0:T(8,128)(2,1)} %get-tuple-element.58), channel_id=1, replica_groups=mesh['oct'=2,'hi'=4,'lo'=4] {'hi','lo'}, dimensions={0} | all-to-all | bytes 262144 | tf_op jit(solution)/shard_map/all_to_all | solution.py:592
  133.5 1.8 %unpack_fields.1 = f32[16,4096]{1,0:T(8,128)} custom-call(s32[16]{0:T(128)} %parent_of.5, bf16[16,16,256]{2,1,0:T(8,128)(2,1)} %all_to_all.10.field_ref), custom_call_target="tpu_custom_call" | custom-call | tf_op jit(solution)/shard_map/unpack_fields/pallas_call | solution.py:593
  (51 shorter events, 0.7 us)
Async XLA Ops:
  2.2 24.0 %all-to-all-start = ((s32[32,8,128]{2,1,0:T(8,128)}), s32[32,8,128]{2,1,0:T(8,128)S(1)}, u32[]{:S(2)}, u32[]{:S(2)}) async-start(s32[32,8,128]{2,1,0:T(8,128)} %pack_tables.1), calls=%async_computation | async-start | bytes 262144 | tf_op jit(solution)/shard_map/all_to_all | solution.py:503
  10.2 69.9 %copy-start.9 = (s32[3]{0:T(128)S(1)}, s32[3]{0:T(128)}, u32[]{:S(2)}) copy-start(s32[3]{0:T(128)} %pad_add_fusion.info) | copy-start | bytes 40
  13.6 15.7 %collective-permute-start.3 = (bf16[20,16,256]{2,1,0:T(8,128)(2,1)}, bf16[20,16,256]{2,1,0:T(8,128)(2,1)}, u32[]{:S(2)}, u32[]{:S(2)}) collective-permute-start(bf16[20,16,256]{2,1,0:T(8,128)(2,1)} %get-tuple-element.41.refs_0_), channel_id=1, source_target_pairs={{0,16},{16,0},{1,17},{17,1},{2,18},{18,2},{3,19},{19,3},{4,20},{20... | collective-permute-start | bytes 491528 | tf_op jit(solution)/shard_map/ppermute | solution.py:467
  13.9 8.5 %collective-permute-start = (bf16[20,16,256]{2,1,0:T(8,128)(2,1)}, bf16[20,16,256]{2,1,0:T(8,128)(2,1)}, u32[]{:S(2)}, u32[]{:S(2)}) collective-permute-start(bf16[20,16,256]{2,1,0:T(8,128)(2,1)} %get-tuple-element.42), channel_id=1, source_target_pairs={{0,1},{1,0},{2,3},{3,2},{4,5},{5,4},{6,7},{7,6},{8,9},{9,8},{10,11... | collective-permute-start | bytes 491528 | tf_op jit(solution)/shard_map/ppermute | solution.py:466
  15.5 10.0 %collective-permute-start.1 = (bf16[20,16,256]{2,1,0:T(8,128)(2,1)}, bf16[20,16,256]{2,1,0:T(8,128)(2,1)}, u32[]{:S(2)}, u32[]{:S(2)}) collective-permute-start(bf16[20,16,256]{2,1,0:T(8,128)(2,1)} %get-tuple-element.43), channel_id=1, source_target_pairs={{0,2},{1,3},{2,0},{3,1},{4,6},{5,7},{6,4},{7,5},{8,10},{9,11},{10,... | collective-permute-start | bytes 491528 | tf_op jit(solution)/shard_map/ppermute | solution.py:466
  17.0 8.5 %collective-permute-start.2 = (bf16[20,16,256]{2,1,0:T(8,128)(2,1)}, bf16[20,16,256]{2,1,0:T(8,128)(2,1)}, u32[]{:S(2)}, u32[]{:S(2)}) collective-permute-start(bf16[20,16,256]{2,1,0:T(8,128)(2,1)} %get-tuple-element.44), channel_id=1, source_target_pairs={{0,3},{1,2},{2,1},{3,0},{4,7},{5,6},{6,5},{7,4},{8,11},{9,10},{10,... | collective-permute-start | bytes 491528 | tf_op jit(solution)/shard_map/ppermute | solution.py:466
  18.9 0.7 copy-start.6
  19.6 0.7 copy-start.10
  21.2 0.6 copy-start.3
  21.8 0.6 copy-start.5
  22.4 7.0 %collective-permute-start.4 = (bf16[20,16,256]{2,1,0:T(8,128)(2,1)}, bf16[20,16,256]{2,1,0:T(8,128)(2,1)}, u32[]{:S(2)}, u32[]{:S(2)}) collective-permute-start(bf16[20,16,256]{2,1,0:T(8,128)(2,1)} %collective-permute-done.refs_1_), channel_id=1, source_target_pairs={{0,16},{16,0},{1,17},{17,1},{2,18},{18,2},{3,19},{19,3},{4,20},{20... | collective-permute-start | bytes 491528 | tf_op jit(solution)/shard_map/ppermute | solution.py:467
  25.5 3.8 %collective-permute-start.5 = (bf16[20,16,256]{2,1,0:T(8,128)(2,1)}, bf16[20,16,256]{2,1,0:T(8,128)(2,1)}, u32[]{:S(2)}, u32[]{:S(2)}) collective-permute-start(bf16[20,16,256]{2,1,0:T(8,128)(2,1)} %collective-permute-done.1.refs_2_), channel_id=1, source_target_pairs={{0,16},{16,0},{1,17},{17,1},{2,18},{18,2},{3,19},{19,3},{4,20},{20... | collective-permute-start | bytes 491528 | tf_op jit(solution)/shard_map/ppermute | solution.py:467
  25.5 3.8 %collective-permute-start.6 = (bf16[20,16,256]{2,1,0:T(8,128)(2,1)}, bf16[20,16,256]{2,1,0:T(8,128)(2,1)}, u32[]{:S(2)}, u32[]{:S(2)}) collective-permute-start(bf16[20,16,256]{2,1,0:T(8,128)(2,1)} %collective-permute-done.2.refs_3_), channel_id=1, source_target_pairs={{0,16},{16,0},{1,17},{17,1},{2,18},{18,2},{3,19},{19,3},{4,20},{20... | collective-permute-start | bytes 491528 | tf_op jit(solution)/shard_map/ppermute | solution.py:467
  26.1 0.7 copy-start.7
  29.4 0.9 copy-start.1
  30.3 0.7 copy-start.8
  49.3 0.7 copy-start.2
  50.0 7.4 %collective-permute-start.7 = (bf16[20,16,256]{2,1,0:T(8,128)(2,1)S(1)}, bf16[20,16,256]{2,1,0:T(8,128)(2,1)S(1)}, u32[]{:S(2)}, u32[]{:S(2)}) collective-permute-start(bf16[20,16,256]{2,1,0:T(8,128)(2,1)S(1)} %get-tuple-element.46), channel_id=1, source_target_pairs={{0,4},{4,0},{8,12},{12,8},{1,5},{5,1},{9,13},{13,9},{2,6},{6,2},{1... | collective-permute-start | bytes 491528 | tf_op jit(solution)/shard_map/ppermute | solution.py:560
  50.3 16.4 %collective-permute-start.8 = (bf16[20,16,256]{2,1,0:T(8,128)(2,1)S(1)}, bf16[20,16,256]{2,1,0:T(8,128)(2,1)S(1)}, u32[]{:S(2)}, u32[]{:S(2)}) collective-permute-start(bf16[20,16,256]{2,1,0:T(8,128)(2,1)S(1)} %get-tuple-element.47), channel_id=1, source_target_pairs={{0,8},{4,12},{8,0},{12,4},{1,9},{5,13},{9,1},{13,5},{2,10},{6,14},... | collective-permute-start | bytes 491528 | tf_op jit(solution)/shard_map/ppermute | solution.py:560
  55.0 11.6 %collective-permute-start.9 = (bf16[20,16,256]{2,1,0:T(8,128)(2,1)S(1)}, bf16[20,16,256]{2,1,0:T(8,128)(2,1)S(1)}, u32[]{:S(2)}, u32[]{:S(2)}) collective-permute-start(bf16[20,16,256]{2,1,0:T(8,128)(2,1)S(1)} %get-tuple-element.48), channel_id=1, source_target_pairs={{0,12},{4,8},{8,4},{12,0},{1,13},{5,9},{9,5},{13,1},{2,14},{6,10},... | collective-permute-start | bytes 491528 | tf_op jit(solution)/shard_map/ppermute | solution.py:560
  57.4 9.3 %copy-start.11 = (bf16[20,16,256]{2,1,0:T(8,128)(2,1)}, bf16[20,16,256]{2,1,0:T(8,128)(2,1)S(1)}, u32[]{:S(2)}) copy-start(bf16[20,16,256]{2,1,0:T(8,128)(2,1)S(1)} %collective-permute-done.7.refs_1_) | copy-start | bytes 491524
  66.6 0.7 copy-start.12
  67.3 0.7 copy-start.13
  72.1 6.1 %collective-permute-start.12 = (bf16[16,16,256]{2,1,0:T(8,128)(2,1)}, bf16[16,16,256]{2,1,0:T(8,128)(2,1)S(1)}, u32[]{:S(2)}, u32[]{:S(2)}) collective-permute-start(bf16[16,16,256]{2,1,0:T(8,128)(2,1)} %tree_source.1.refs_0_), channel_id=1, source_target_pairs={{0,3},{1,2},{2,1},{3,0},{4,7},{5,6},{6,5},{7,4},{8,11},{9,10},{10,... | collective-permute-start | bytes 393224 | tf_op jit(solution)/shard_map/ppermute | solution.py:466
  73.8 5.8 %collective-permute-start.11 = (bf16[16,16,256]{2,1,0:T(8,128)(2,1)}, bf16[16,16,256]{2,1,0:T(8,128)(2,1)S(1)}, u32[]{:S(2)}, u32[]{:S(2)}) collective-permute-start(bf16[16,16,256]{2,1,0:T(8,128)(2,1)} %tree_source.1.refs_0_), channel_id=1, source_target_pairs={{0,2},{1,3},{2,0},{3,1},{4,6},{5,7},{6,4},{7,5},{8,10},{9,11},{10,... | collective-permute-start | bytes 393224 | tf_op jit(solution)/shard_map/ppermute | solution.py:466
  74.3 5.4 %collective-permute-start.10 = (bf16[16,16,256]{2,1,0:T(8,128)(2,1)}, bf16[16,16,256]{2,1,0:T(8,128)(2,1)S(1)}, u32[]{:S(2)}, u32[]{:S(2)}) collective-permute-start(bf16[16,16,256]{2,1,0:T(8,128)(2,1)} %tree_source.1.refs_0_), channel_id=1, source_target_pairs={{0,1},{1,0},{2,3},{3,2},{4,5},{5,4},{6,7},{7,6},{8,9},{9,8},{10,11... | collective-permute-start | bytes 393224 | tf_op jit(solution)/shard_map/ppermute | solution.py:466
  75.5 6.9 %collective-permute-start.13 = (bf16[16,16,256]{2,1,0:T(8,128)(2,1)}, bf16[16,16,256]{2,1,0:T(8,128)(2,1)S(1)}, u32[]{:S(2)}, u32[]{:S(2)}) collective-permute-start(bf16[16,16,256]{2,1,0:T(8,128)(2,1)} %tree_source.1.refs_0_), channel_id=1, source_target_pairs={{0,16},{16,0},{1,17},{17,1},{2,18},{18,2},{3,19},{19,3},{4,20},{20... | collective-permute-start | bytes 393224 | tf_op jit(solution)/shard_map/ppermute | solution.py:467
  78.2 4.2 %collective-permute-start.16 = (bf16[16,16,256]{2,1,0:T(8,128)(2,1)S(1)}, bf16[16,16,256]{2,1,0:T(8,128)(2,1)S(1)}, u32[]{:S(2)}, u32[]{:S(2)}) collective-permute-start(bf16[16,16,256]{2,1,0:T(8,128)(2,1)S(1)} %collective-permute-done.12.refs_3_), channel_id=1, source_target_pairs={{0,16},{16,0},{1,17},{17,1},{2,18},{18,2},{3,19},{19,3},{4,20},{20... | collective-permute-start | bytes 393224 | tf_op jit(solution)/shard_map/ppermute | solution.py:467
  79.5 2.9 %collective-permute-start.15 = (bf16[16,16,256]{2,1,0:T(8,128)(2,1)S(1)}, bf16[16,16,256]{2,1,0:T(8,128)(2,1)S(1)}, u32[]{:S(2)}, u32[]{:S(2)}) collective-permute-start(bf16[16,16,256]{2,1,0:T(8,128)(2,1)S(1)} %collective-permute-done.11.refs_2_), channel_id=1, source_target_pairs={{0,16},{16,0},{1,17},{17,1},{2,18},{18,2},{3,19},{19,3},{4,20},{20... | collective-permute-start | bytes 393224 | tf_op jit(solution)/shard_map/ppermute | solution.py:467
  79.7 2.8 %collective-permute-start.14 = (bf16[16,16,256]{2,1,0:T(8,128)(2,1)S(1)}, bf16[16,16,256]{2,1,0:T(8,128)(2,1)S(1)}, u32[]{:S(2)}, u32[]{:S(2)}) collective-permute-start(bf16[16,16,256]{2,1,0:T(8,128)(2,1)S(1)} %collective-permute-done.10.refs_1_), channel_id=1, source_target_pairs={{0,16},{16,0},{1,17},{17,1},{2,18},{18,2},{3,19},{19,3},{4,20},{20... | collective-permute-start | bytes 393224 | tf_op jit(solution)/shard_map/ppermute | solution.py:467
  82.4 0.9 copy-start
  100.7 0.7 copy-start.4
  101.4 9.0 %collective-permute-start.17 = (bf16[16,16,256]{2,1,0:T(8,128)(2,1)S(1)}, bf16[16,16,256]{2,1,0:T(8,128)(2,1)S(1)}, u32[]{:S(2)}, u32[]{:S(2)}) collective-permute-start(bf16[16,16,256]{2,1,0:T(8,128)(2,1)S(1)} %get-tuple-element.55), channel_id=1, source_target_pairs={{0,4},{4,0},{8,12},{12,8},{1,5},{5,1},{9,13},{13,9},{2,6},{6,2},{1... | collective-permute-start | bytes 393224 | tf_op jit(solution)/shard_map/ppermute | solution.py:560
  106.1 11.9 %collective-permute-start.18 = (bf16[16,16,256]{2,1,0:T(8,128)(2,1)S(1)}, bf16[16,16,256]{2,1,0:T(8,128)(2,1)S(1)}, u32[]{:S(2)}, u32[]{:S(2)}) collective-permute-start(bf16[16,16,256]{2,1,0:T(8,128)(2,1)S(1)} %get-tuple-element.56), channel_id=1, source_target_pairs={{0,8},{4,12},{8,0},{12,4},{1,9},{5,13},{9,1},{13,5},{2,10},{6,14},... | collective-permute-start | bytes 393224 | tf_op jit(solution)/shard_map/ppermute | solution.py:560
  106.1 11.9 %collective-permute-start.19 = (bf16[16,16,256]{2,1,0:T(8,128)(2,1)S(1)}, bf16[16,16,256]{2,1,0:T(8,128)(2,1)S(1)}, u32[]{:S(2)}, u32[]{:S(2)}) collective-permute-start(bf16[16,16,256]{2,1,0:T(8,128)(2,1)S(1)} %get-tuple-element.57), channel_id=1, source_target_pairs={{0,12},{4,8},{8,4},{12,0},{1,13},{5,9},{9,5},{13,1},{2,14},{6,10},... | collective-permute-start | bytes 393224 | tf_op jit(solution)/shard_map/ppermute | solution.py:560
  110.4 8.3 %copy-start.14 = (bf16[16,16,256]{2,1,0:T(8,128)(2,1)}, bf16[16,16,256]{2,1,0:T(8,128)(2,1)S(1)}, u32[]{:S(2)}) copy-start(bf16[16,16,256]{2,1,0:T(8,128)(2,1)S(1)} %collective-permute-done.17.refs_1_) | copy-start | bytes 393220
  118.0 0.7 copy-start.15
  118.0 0.7 copy-start.16
